TPU v7x, 32 devices: a whole 2x2x4 slice. The times are simulated.
32 devices in a mesh: dp: 4 (over y, core), seq: 8 (over z, x).
Axes of the slice: x: 2, y: 2, z: 4, core: 2. Of those that a mesh axis runs over, the one named last changes fastest.
Arguments:
- tokens: bfloat16 [4096, 1024], P(('dp', 'seq')), may hold values from -6 to 6
- gate_values: float32 [4096, 2], P(('dp', 'seq')), may hold values from 0.2 to 1
- expert_ids: int32 [4096, 2], P(('dp', 'seq')), may hold values from 0 to 31, all different within a row; in each aligned block of 128 rows (0 to 127, 128 to 255, ...) at most 9 rows name the same one
- cotangent: bfloat16 [4096, 1024], P(('dp', 'seq')), may hold values from -6 to 6
- weight_in: bfloat16 [32768, 1024], P('seq'), may hold values from -0.1875 to 0.1875
- weight_out: bfloat16 [32768, 1024], P('seq'), may hold values from -0.1875 to 0.1875
Outputs:
- layer_out: bfloat16 [4096, 1024], P(('dp', 'seq'))
- gate_grad: float32 [4096, 2], P(('dp', 'seq'))
- input_grad: bfloat16 [4096, 1024], P(('dp', 'seq'))
- weight_in_grad: float32 [1024, 32768], P('dp', 'seq')
- weight_out_grad: float32 [1024, 32768], P('dp', 'seq')
Inputs may be any that keep to these rules, and one draw needn't show every extreme that they name: `expert_ids`: each row names two different experts; within the rows of one device no expert is named more than 9 times, a bound that some block reaches.
All inputs are finite; a program needn't handle non-finite values.
Results may differ from a plain program's by a relative error of at most 0.017.
Values may be sent and summed in bfloat16 or wider, within the bound.
No kernel may reach another device: no remote copies, remote signals or barrier semaphores. Data moves between devices by JAX's collectives and lax.ppermute only.
A program may use at most 128 MiB of HBM per device.

v0:
```python
import jax
import jax.numpy as jnp
import numpy as np
from jax import lax
from jax.sharding import PartitionSpec as P

E = 32
FF = 1024
CAP = 9


gelu_scale = 0.7978845608028654
gelu_cubic = 0.044715


def gelu_value(values):
    inner_arg = gelu_scale * (values + gelu_cubic * values * values * values)
    return 0.5 * values * (1.0 + jnp.tanh(inner_arg))


def gelu_slope(values):
    inner_arg = gelu_scale * (values + gelu_cubic * values * values * values)
    tanh_val = jnp.tanh(inner_arg)
    return 0.5 * (1.0 + tanh_val) + 0.5 * values * (1.0 - tanh_val * tanh_val) * gelu_scale * (
        1.0 + 3.0 * gelu_cubic * values * values
    )


def slot_numbers(ids_block):
    flat_ids = ids_block.reshape(-1)
    onehot = (flat_ids[:, None] == jnp.arange(E, dtype=jnp.int32)[None, :]).astype(jnp.int32)
    before = jnp.cumsum(onehot, axis=0) - onehot
    return jnp.sum(before * onehot, axis=1).reshape(ids_block.shape)


def local(tokens, gate_values, expert_ids, cotangent, weight_in, weight_out):
    seq_count = lax.axis_size("seq")
    group_count = lax.axis_size("dp")
    own_units = weight_in.shape[0]
    block_units = min(FF, own_units)
    held_experts = own_units // block_units
    block_count = FF // block_units
    tok_count = tokens.shape[0]
    model_width = tokens.shape[1]
    factor = (E / (2.0 * tok_count * seq_count * group_count)) ** 0.5
    row_total = seq_count * CAP
    slot_of = slot_numbers(expert_ids)
    flat_target = (expert_ids * CAP + slot_of).reshape(-1)
    token_of = jnp.repeat(jnp.arange(tok_count, dtype=jnp.int32), 2)
    slot_token = jnp.zeros((E * CAP,), jnp.int32).at[flat_target].set(token_of)
    slot_used = jnp.zeros((E * CAP,), jnp.float32).at[flat_target].set(1.0)
    slot_gate = jnp.zeros((E * CAP,), jnp.float32).at[flat_target].set(gate_values.reshape(-1))
    column = np.arange(seq_count * held_experts * CAP)
    owner_of = column // (held_experts * CAP)
    local_of = column // CAP % held_experts
    expert_of = (owner_of * own_units + local_of * block_units) // FF
    code_table = jnp.asarray(expert_of * CAP + column % CAP, dtype=jnp.int32)
    col_token = slot_token[code_table]
    col_used = slot_used[code_table]
    col_gate = slot_gate[code_table]
    send_shape = (seq_count, held_experts * CAP, model_width)
    send_x = (
        (tokens[col_token].astype(jnp.float32) * col_used[:, None])
        .astype(jnp.bfloat16)
        .reshape(send_shape)
    )
    send_d = (
        (cotangent[col_token].astype(jnp.float32) * col_gate[:, None])
        .astype(jnp.bfloat16)
        .reshape(send_shape)
    )
    win_local = weight_in.reshape(held_experts, block_units, model_width)
    wout_local = weight_out.reshape(held_experts, block_units, model_width)

    def to_rows(arrived):
        grouped = arrived.reshape(seq_count, held_experts, CAP, model_width)
        return jnp.transpose(grouped, (1, 0, 2, 3)).reshape(held_experts, row_total, model_width)

    def from_rows(results):
        grouped = results.reshape(held_experts, seq_count, CAP, model_width)
        return jnp.transpose(grouped, (1, 0, 2, 3)).reshape(send_shape)

    rows_x = to_rows(lax.all_to_all(send_x, "seq", split_axis=0, concat_axis=0, tiled=True))
    hidden = jnp.einsum("krd,kfd->krf", rows_x, win_local, preferred_element_type=jnp.float32)
    owner_act = gelu_value(hidden).astype(jnp.bfloat16)
    part_out = jnp.einsum(
        "krf,kfd->krd", owner_act, wout_local, preferred_element_type=jnp.float32
    ).astype(jnp.bfloat16)
    hidden, act, part_out = (hidden, owner_act, part_out)
    back_out = lax.all_to_all(from_rows(part_out), "seq", split_axis=0, concat_axis=0, tiled=True)
    rows_d = to_rows(lax.all_to_all(send_d, "seq", split_axis=0, concat_axis=0, tiled=True))
    back_hidden = jnp.einsum("krd,kfd->krf", rows_d, wout_local, preferred_element_type=jnp.float32)
    owner_dhid = (back_hidden * gelu_slope(hidden)).astype(jnp.bfloat16)
    part_in = jnp.einsum(
        "krf,kfd->krd", owner_dhid, win_local, preferred_element_type=jnp.float32
    ).astype(jnp.bfloat16)
    dhid, part_in = (owner_dhid, part_in)
    back_in = lax.all_to_all(from_rows(part_in), "seq", split_axis=0, concat_axis=0, tiled=True)

    def collect(returned):
        flat_rows = returned.reshape(-1, model_width)
        summed = jnp.zeros((tok_count, 2, model_width), jnp.float32)
        for block_index in range(block_count):
            unit_start = expert_ids * FF + block_index * block_units
            row_at = (
                unit_start // own_units * (held_experts * CAP)
                + unit_start % own_units // block_units * CAP
                + slot_of
            )
            summed = summed + flat_rows[row_at].astype(jnp.float32)
        return summed

    expert_out = collect(back_out)
    layer_out = jnp.sum(gate_values[:, :, None] * expert_out, axis=1).astype(jnp.bfloat16)
    gate_grad = jnp.sum(cotangent.astype(jnp.float32)[:, None, :] * expert_out, axis=2)
    input_grad = jnp.sum(collect(back_in), axis=1).astype(jnp.bfloat16)
    x_columns = jnp.transpose(rows_x, (2, 0, 1))
    d_columns = jnp.transpose(rows_d, (2, 0, 1))
    grad_in_part = (
        jnp.einsum("dkr,krf->dkf", x_columns, dhid, preferred_element_type=jnp.float32).reshape(
            lax.axis_size("dp") * (model_width // group_count), own_units
        )
        * factor
    )
    grad_out_part = (
        jnp.einsum("dkr,krf->dkf", d_columns, act, preferred_element_type=jnp.float32).reshape(
            lax.axis_size("dp") * (model_width // group_count), own_units
        )
        * factor
    )
    summed_grads = lax.psum_scatter(
        jnp.concatenate([grad_in_part, grad_out_part], axis=1).astype(jnp.bfloat16),
        "dp",
        scatter_dimension=0,
        tiled=True,
    ).astype(jnp.float32)
    weight_in_grad = summed_grads[:, :own_units]
    weight_out_grad = summed_grads[:, own_units:]
    return (layer_out, gate_grad, input_grad, weight_in_grad, weight_out_grad)


def solution(mesh):
    in_specs = (
        P(("dp", "seq"), None),
        P(("dp", "seq"), None),
        P(("dp", "seq"), None),
        P(("dp", "seq"), None),
        P("seq", None),
        P("seq", None),
    )
    out_specs = (
        P(("dp", "seq"), None),
        P(("dp", "seq"), None),
        P(("dp", "seq"), None),
        P("dp", "seq"),
        P("dp", "seq"),
    )
    return jax.shard_map(local, mesh=mesh, in_specs=in_specs, out_specs=out_specs, check_vma=False)
```

profile of v0, /device:TPU:0, one launch (start us, length us, event | category | flops | bytes accessed | tf_op | source)
XLA Modules:
  0.0 264.5 jit_solution(12241100516920325931)
XLA Ops:
  7.2 0.7 broadcast_multiply_fusion
  7.9 0.8 copy.41
  9.1 0.6 reduce-window.6
  10.5 1.4 scatter_custom_fusion.1
  11.9 2.4 gather_fusion.2
  14.6 1.4 scatter_custom_fusion
  16.0 2.4 gather_fusion
  18.5 2.1 gather_fusion.1
  20.7 1.0 multiply_convert_fusion.3
  21.7 7.3 %all-to-all-start = ((bf16[8,36,1024]{2,1,0:T(8,128)(2,1)}), bf16[8,36,1024]{2,1,0:T(8,128)(2,1)S(1)}, u32[]{:S(2)}, u32[]{:S(2)}) async-start(bf16[8,36,1024]{2,1,0:T(8,128)(2,1)} %multiply_convert_fusion.3), calls=%async_computation | async-start | bytes 1310720 | tf_op jit(solution)/shard_map/all_to_all | solution.py:83
  29.2 1.4 scatter_custom_fusion.2
  30.6 2.4 gather_fusion.5
  33.1 2.1 gather_fusion.4
  35.3 1.0 multiply_convert_fusion.2
  36.3 9.9 %all-to-all-done = bf16[8,36,1024]{2,1,0:T(8,128)(2,1)S(1)} async-done(((bf16[8,36,1024]{2,1,0:T(8,128)(2,1)}), bf16[8,36,1024]{2,1,0:T(8,128)(2,1)S(1)}, u32[]{:S(2)}, u32[]{:S(2)}) %all-to-all-start) | async-done | bytes 589856 | tf_op jit(solution)/shard_map/all_to_all | solution.py:83
  46.2 3.6 %all-to-all-start.2 = ((bf16[8,36,1024]{2,1,0:T(8,128)(2,1)}), bf16[8,36,1024]{2,1,0:T(8,128)(2,1)S(1)}, u32[]{:S(2)}, u32[]{:S(2)}) async-start(bf16[8,36,1024]{2,1,0:T(8,128)(2,1)} %multiply_convert_fusion.2), calls=%async_computation.2 | async-start | bytes 1310720 | tf_op jit(solution)/shard_map/all_to_all | solution.py:91
  49.8 0.2 reduce-scatter.2.cloned.1.call-start
  50.1 0.3 copy.45
  50.4 0.5 copy.46
  50.9 16.5 %all-to-all-done.2 = bf16[8,36,1024]{2,1,0:T(8,128)(2,1)S(1)} async-done(((bf16[8,36,1024]{2,1,0:T(8,128)(2,1)}), bf16[8,36,1024]{2,1,0:T(8,128)(2,1)S(1)}, u32[]{:S(2)}, u32[]{:S(2)}) %all-to-all-start.2) | async-done | bytes 589856 | tf_op jit(solution)/shard_map/all_to_all | solution.py:91
  67.3 0.3 copy.53
  67.7 0.5 copy.54
  68.1 6.2 %fusion.11 = f32[4,72,1024]{2,1,0:T(8,128)S(1)} fusion(bf16[4,1024,1024]{2,1,0:T(8,128)(2,1)} %bitcast.59, bf16[4,72,1024]{2,0,1:T(4,128)(2,1)S(1)} %bitcast.67), kind=kOutput, calls=%fused_computation.34 | convolution fusion | flops 603979776 | bytes 10158080 | tf_op jit(solution)/shard_map/krd,kfd->krf/dot_general | solution.py:84
  74.4 5.6 %multiply_convert_fusion = bf16[4,1024,1024]{2,1,0:T(8,128)(2,1)} fusion(bf16[4,72,1024]{2,0,1:T(4,128)(2,1)S(1)} %bitcast.75, f32[4,72,1024]{2,1,0:T(8,128)S(1)} %fusion.11), kind=kOutput, calls=%fused_computation.11 | convolution fusion | flops 615022592 | bytes 10158080 | tf_op jit(solution)/shard_map/dkr,krf->dkf/dot_general | solution.py:126
  80.0 2.7 %fusion = bf16[4,72,1024]{2,1,0:T(8,128)(2,1)S(1)} fusion(bf16[4,1024,1024]{2,1,0:T(8,128)(2,1)S(1)} %bitcast.65, f32[4,72,1024]{2,1,0:T(8,128)S(1)} %fusion.11, bf16[4,72,1024]{2,0,1:T(4,128)(2,1)S(1)} %bitcast.76), kind=kOutput, calls=%fused_computation.16 | convolution fusion | flops 609583104 | bytes 10747904 | tf_op jit(solution)/shard_map/krd,kfd->krf/dot_general | solution.py:92
  82.7 11.5 %copy.62 = bf16[1024,4096]{1,0:T(8,128)(2,1)} copy(bf16[1024,4096]{0,1:T(8,128)(2,1)} %bitcast.66) | data formatting | bytes 16777216 | tf_op jit(solution)/shard_map/mul | solution.py:126
  94.2 5.6 %multiply_convert_fusion.1 = bf16[4,1024,1024]{2,1,0:T(8,128)(2,1)} fusion(bf16[4,72,1024]{2,1,0:T(8,128)(2,1)S(1)} %fusion, bf16[4,72,1024]{2,0,1:T(4,128)(2,1)S(1)} %bitcast.68), kind=kOutput, calls=%fused_computation.12 | convolution fusion | flops 612368384 | bytes 9568256 | tf_op jit(solution)/shard_map/dkr,krf->dkf/dot_general | solution.py:120
  99.8 12.0 %copy.61 = bf16[1024,4096]{1,0:T(8,128)(2,1)} copy(bf16[1024,4096]{0,1:T(8,128)(2,1)} %bitcast.61) | data formatting | bytes 16777216 | tf_op jit(solution)/shard_map/mul | solution.py:120
  111.8 13.7 %pad_maximum_fusion = bf16[1024,8192]{1,0:T(8,128)(2,1)} fusion(bf16[1024,4096]{1,0:T(8,128)(2,1)} %copy.62, bf16[1024,4096]{1,0:T(8,128)(2,1)} %copy.61), kind=kLoop, calls=%fused_computation.10 | loop fusion | flops 33554432 | bytes 33554432 | tf_op jit(solution)/shard_map/concatenate | solution.py:132
  125.6 5.0 %convolution_convert_fusion = bf16[4,72,1024]{2,1,0:T(8,128)(2,1)S(1)} fusion(bf16[4,72,1024]{2,1,0:T(8,128)(2,1)S(1)} %fusion, bf16[4,1024,1024]{2,1,0:T(8,128)(2,1)} %bitcast.60), kind=kOutput, calls=%fused_computation.17 | convolution fusion | flops 604274688 | bytes 9568256 | tf_op jit(solution)/shard_map/krf,kfd->krd/dot_general | solution.py:94
  130.6 0.5 copy.56
  131.2 1.2 copy.58
  132.4 3.6 %all-to-all-start.3 = ((bf16[8,36,1024]{2,1,0:T(8,128)(2,1)}), bf16[8,36,1024]{2,1,0:T(8,128)(2,1)S(1)}, u32[]{:S(2)}, u32[]{:S(2)}) async-start(bf16[8,36,1024]{2,1,0:T(8,128)(2,1)} %copy.58), calls=%async_computation.3 | async-start | bytes 1310720 | tf_op jit(solution)/shard_map/all_to_all | solution.py:98
  136.0 6.9 %convolution_convert_fusion.1 = bf16[4,72,1024]{2,1,0:T(8,128)(2,1)S(1)} fusion(bf16[4,1024,1024]{2,1,0:T(8,128)(2,1)} %bitcast.62, f32[4,72,1024]{2,1,0:T(8,128)S(1)} %fusion.11), kind=kOutput, calls=%fused_computation.18 | convolution fusion | flops 606928896 | bytes 10158080 | tf_op jit(solution)/shard_map/krf,kfd->krd/dot_general | solution.py:86
  142.9 0.5 copy.48
  143.6 1.2 copy.50
  144.7 8.7 %all-to-all-done.3 = bf16[8,36,1024]{2,1,0:T(8,128)(2,1)S(1)} async-done(((bf16[8,36,1024]{2,1,0:T(8,128)(2,1)}), bf16[8,36,1024]{2,1,0:T(8,128)(2,1)S(1)}, u32[]{:S(2)}, u32[]{:S(2)}) %all-to-all-start.3) | async-done | bytes 589856 | tf_op jit(solution)/shard_map/all_to_all | solution.py:98
  153.5 3.8 %all-to-all-start.1 = ((bf16[8,36,1024]{2,1,0:T(8,128)(2,1)}), bf16[8,36,1024]{2,1,0:T(8,128)(2,1)S(1)}, u32[]{:S(2)}, u32[]{:S(2)}) async-start(bf16[8,36,1024]{2,1,0:T(8,128)(2,1)} %copy.50), calls=%async_computation.1 | async-start | bytes 1310720 | tf_op jit(solution)/shard_map/all_to_all | solution.py:90
  157.6 1.2 gather_fusion.6
  158.8 0.2 reshape.218
  159.0 15.6 %all-to-all-done.1 = bf16[8,36,1024]{2,1,0:T(8,128)(2,1)S(1)} async-done(((bf16[8,36,1024]{2,1,0:T(8,128)(2,1)}), bf16[8,36,1024]{2,1,0:T(8,128)(2,1)S(1)}, u32[]{:S(2)}, u32[]{:S(2)}) %all-to-all-start.1) | async-done | bytes 589856 | tf_op jit(solution)/shard_map/all_to_all | solution.py:90
  174.7 1.2 gather_fusion.3
  175.9 0.7 reshape.249
  176.6 2.6 multiply_reduce_fusion
  179.1 0.6 copy.63
  179.8 2.1 reduce_sum.42
  181.8 69.1 %reduce-scatter.2.cloned.1.call-done = bf16[256,8192]{1,0:T(8,128)(2,1)} async-done(((bf16[1024,8192]{1,0:T(8,128)(2,1)}), bf16[256,8192]{1,0:T(8,128)(2,1)}) %reduce-scatter.2.cloned.1.call-update) | async-done | bytes 4194320 | tf_op jit(solution)/shard_map/reduce_scatter | solution.py:131
  250.9 6.7 %fusion.32 = (f32[256,4096]{1,0:T(8,128)}, f32[256,4096]{1,0:T(8,128)}) fusion(bf16[256,8192]{1,0:T(8,128)(2,1)} %reduce-scatter.2.cloned.1.call-done), kind=kLoop, calls=%fused_computation.78 | loop fusion | bytes 16777216 | tf_op jit(solution)/shard_map/slice | solution.py:138
  (46 shorter events, 2.7 us)
Async XLA Ops:
  7.2 11.3 %copy-start = (bf16[128,1024]{1,0:T(8,128)(2,1)S(1)}, bf16[128,1024]{1,0:T(8,128)(2,1)}, u32[]{:S(2)}) copy-start(bf16[128,1024]{1,0:T(8,128)(2,1)} %param.7) | copy-start | bytes 786436
  20.7 8.2 %copy-start.3 = (f32[128,2]{0,1:T(2,128)S(1)}, f32[128,2]{0,1:T(2,128)}, u32[]{:S(2)}) copy-start(f32[128,2]{0,1:T(2,128)} %param.8) | copy-start | bytes 3076
  21.7 24.5 %all-to-all-start = ((bf16[8,36,1024]{2,1,0:T(8,128)(2,1)}), bf16[8,36,1024]{2,1,0:T(8,128)(2,1)S(1)}, u32[]{:S(2)}, u32[]{:S(2)}) async-start(bf16[8,36,1024]{2,1,0:T(8,128)(2,1)} %multiply_convert_fusion.3), calls=%async_computation | async-start | bytes 1310720 | tf_op jit(solution)/shard_map/all_to_all | solution.py:83
  28.9 4.2 %copy-start.2 = (bf16[128,1024]{1,0:T(8,128)(2,1)S(1)}, bf16[128,1024]{1,0:T(8,128)(2,1)}, u32[]{:S(2)}) copy-start(bf16[128,1024]{1,0:T(8,128)(2,1)} %param.10) | copy-start | bytes 786436
  46.2 21.1 %all-to-all-start.2 = ((bf16[8,36,1024]{2,1,0:T(8,128)(2,1)}), bf16[8,36,1024]{2,1,0:T(8,128)(2,1)S(1)}, u32[]{:S(2)}, u32[]{:S(2)}) async-start(bf16[8,36,1024]{2,1,0:T(8,128)(2,1)} %multiply_convert_fusion.2), calls=%async_computation.2 | async-start | bytes 1310720 | tf_op jit(solution)/shard_map/all_to_all | solution.py:91
  49.8 201.1 %reduce-scatter.2.cloned.1.call-start = ((), (), s32[]{:S(2)}) async-start(), calls=%async_computation.5 | async-start | bytes 20971520 | tf_op jit(solution)/shard_map/reduce_scatter | solution.py:131
  68.1 11.9 %slice-start = ((s8[8388608]{0:T(1024)(128)(4,1)}), s8[4194304]{0:T(1024)(128)(4,1)S(1)}, s32[]{:S(2)}) async-start(s8[8388608]{0:T(1024)(128)(4,1)} %bitcast.63), calls=%async_computation.6 | async-start | bytes 8388608
  74.3 5.7 %slice-start.1 = ((s8[8388608]{0:T(1024)(128)(4,1)}), s8[4194304]{0:T(1024)(128)(4,1)S(1)}, s32[]{:S(2)}) async-start(s8[8388608]{0:T(1024)(128)(4,1)} %bitcast.63), calls=%async_computation.7 | async-start | bytes 8388608
  132.4 21.1 %all-to-all-start.3 = ((bf16[8,36,1024]{2,1,0:T(8,128)(2,1)}), bf16[8,36,1024]{2,1,0:T(8,128)(2,1)S(1)}, u32[]{:S(2)}, u32[]{:S(2)}) async-start(bf16[8,36,1024]{2,1,0:T(8,128)(2,1)} %copy.58), calls=%async_computation.3 | async-start | bytes 1310720 | tf_op jit(solution)/shard_map/all_to_all | solution.py:98
  153.5 21.1 %all-to-all-start.1 = ((bf16[8,36,1024]{2,1,0:T(8,128)(2,1)}), bf16[8,36,1024]{2,1,0:T(8,128)(2,1)S(1)}, u32[]{:S(2)}, u32[]{:S(2)}) async-start(bf16[8,36,1024]{2,1,0:T(8,128)(2,1)} %copy.50), calls=%async_computation.1 | async-start | bytes 1310720 | tf_op jit(solution)/shard_map/all_to_all | solution.py:90
  250.9 6.7 %copy-start.1 = (bf16[128,1024]{1,0:T(8,128)(2,1)S(1)}, bf16[128,1024]{1,0:T(8,128)(2,1)}, u32[]{:S(2)}) copy-start(bf16[128,1024]{1,0:T(8,128)(2,1)} %param.7) | copy-start | bytes 786436
Sparse Core Ops, SparseCore 0:
  125.7 125.1 reduce-scatter.1
where the time goes:
time: 266 us; the launch traced here: 265 us
  waiting for transfers between devices  120 us (45%)
  local copies, waits for them, and re-layouts  57.7 us (22%)
  matrix products  32.1 us (12%)
  other arithmetic  22 us (8%)
  starting transfers between devices  18.5 us (7%)
  between operations  14.4 us (5%)
    reduce_scatter x1, waiting for transfers between devices, local(): lax.psum_scatter(jnp.concatenate([grad_in_part, grad_out_part], axis=1).a...  69.1 us
    all_to_all x1, waiting for transfers between devices, local(): lax.all_to_all(send_d, 'seq', split_axis=0, concat_axis=0, tiled=True)  16.5 us
    all_to_all x1, waiting for transfers between devices, local(): lax.all_to_all(from_rows(part_out), 'seq', split_axis=0, concat_axis=0, t...  15.6 us
    concatenate x1, other arithmetic, local(): jnp.concatenate([grad_in_part, grad_out_part], axis=1).astype(jnp.bfloat16)  13.7 us
    mul x1, local copies, waits for them, and re-layouts, local(): jnp.einsum('dkr,krf->dkf', x_columns, dhid, preferred_element_type=jnp.fl...  12 us
    mul x1, local copies, waits for them, and re-layouts, local(): jnp.einsum('dkr,krf->dkf', d_columns, act, preferred_element_type=jnp.flo...  11.5 us
    all_to_all x1, waiting for transfers between devices, local(): lax.all_to_all(send_x, 'seq', split_axis=0, concat_axis=0, tiled=True)  9.92 us
    all_to_all x1, waiting for transfers between devices, local(): lax.all_to_all(from_rows(part_in), 'seq', split_axis=0, concat_axis=0, ti...  8.75 us
  transfers between devices with their start and end apart: 5, of which 5 were waited for; matrix products, arithmetic and copies ran while one was open for 12% of the time, Pallas kernels for 0%

commit v1 on v0

--- a/solution.py
+++ b/solution.py
@@ -1,13 +1,20 @@
+import functools
+
 import jax
 import jax.numpy as jnp
 import numpy as np
 from jax import lax
+from jax.experimental import pallas as pl
+from jax.experimental.pallas import tpu as pltpu
 from jax.sharding import PartitionSpec as P
 
 E = 32
 FF = 1024
 CAP = 9
 
+BF16 = jnp.bfloat16
+F32 = jnp.float32
+VMEM_BYTES = 50 * 1024 * 1024
 
 gelu_scale = 0.7978845608028654
 gelu_cubic = 0.044715
@@ -26,6 +33,375 @@
     )
 
 
+def gelu_both(values):
+    square = values * values
+    tanh_val = jnp.tanh(gelu_scale * (values + gelu_cubic * square * values))
+    half_up = 0.5 * (1.0 + tanh_val)
+    slope = half_up + 0.5 * values * (1.0 - tanh_val * tanh_val) * gelu_scale * (
+        1.0 + 3.0 * gelu_cubic * square
+    )
+    return values * half_up, slope
+
+
+def iota(shape, dim):
+    return lax.broadcasted_iota(jnp.int32, shape, dim)
+
+
+def quotient(numbers, divisor):
+    return jnp.floor((numbers.astype(F32) + 0.5) * (1.0 / divisor)).astype(jnp.int32)
+
+
+def dot(a, b, dims):
+    return lax.dot_general(a, b, ((dims[0], dims[1]), ((), ())), preferred_element_type=F32)
+
+
+def ones_where(mask):
+    return jnp.where(mask, 1.0, 0.0).astype(BF16)
+
+
+def slab_slot(numbers, slots):
+    slab = quotient(numbers, 2 * slots)
+    rest = numbers - slab * (2 * slots)
+    right = (rest >= slots).astype(jnp.int32)
+    return slab * slots + rest - right * slots, right
+
+
+def dispatch_kernel(slots, ids_ref, gate_ref, tok_ref, cot_ref, x_ref, d_ref, target_ref):
+    count = tok_ref.shape[0]
+    half = tok_ref.shape[1] // 2
+    rows = x_ref.shape[0]
+    ids = ids_ref[...]
+    first, second = ids[0:1, :], ids[1:2, :]
+    expert = iota((E, count), 0)
+    hot_first, hot_second = expert == first, expert == second
+    earlier = ones_where(iota((count, count), 0) < iota((count, count), 1))
+    before = dot(ones_where(hot_first | hot_second), earlier, ((1,), (0,)))
+    slot_first = jnp.sum(jnp.where(hot_first, before, 0.0), axis=0, keepdims=True)
+    slot_second = jnp.sum(jnp.where(hot_second, before, 0.0), axis=0, keepdims=True)
+    target_first = first * CAP + slot_first.astype(jnp.int32)
+    target_second = second * CAP + slot_second.astype(jnp.int32)
+    target_ref[0:1, :] = target_first
+    target_ref[1:2, :] = target_second
+    slot, right = slab_slot(iota((rows, 1), 0), slots)
+    is_first, is_second = slot == target_first, slot == target_second
+    pick = ones_where(is_first | is_second)
+    is_right = right == 1
+    rows_x = dot(pick, tok_ref[...], ((1,), (0,)))
+    x_ref[...] = jnp.where(is_right, rows_x[:, half:], rows_x[:, :half]).astype(BF16)
+    gates = gate_ref[...]
+    gate = jnp.sum(
+        jnp.where(is_first, gates[0:1, :], 0.0) + jnp.where(is_second, gates[1:2, :], 0.0),
+        axis=1,
+        keepdims=True,
+    )
+    rows_d = dot(pick, cot_ref[...], ((1,), (0,)))
+    d_ref[...] = (jnp.where(is_right, rows_d[:, half:], rows_d[:, :half]) * gate).astype(BF16)
+
+
+def group_rows(slab_ref, slots, held, sources):
+    per_expert = sources * CAP
+    number = iota((held * per_expert, 1), 0)
+    expert = quotient(number, per_expert)
+    rest = number - expert * per_expert
+    source = quotient(rest, CAP)
+    row = source * (2 * slots) + expert * CAP + rest - source * CAP
+    at = iota((held * per_expert, 2 * slots * sources), 1)
+    slabs = slab_ref[...]
+    return [dot(ones_where(at == row + side * slots), slabs, ((1,), (0,))) for side in (0, 1)]
+
+
+def slab_rows(rows, slots, held, sources):
+    per_expert = sources * CAP
+    half = rows.shape[1] // 2
+    number = iota((2 * slots * sources, 1), 0)
+    source = quotient(number, 2 * slots)
+    rest = number - source * (2 * slots)
+    is_right = rest >= slots
+    rest = jnp.where(is_right, rest - slots, rest)
+    expert = quotient(rest, CAP)
+    row = expert * per_expert + source * CAP + rest - expert * CAP
+    at = iota((2 * slots * sources, held * per_expert), 1)
+    out = dot(ones_where(at == row), rows, ((1,), (0,)))
+    return jnp.where(is_right, out[:, half:], out[:, :half])
+
+
+def expert_kernel(
+    slots, held, sources, forward, *refs
+):
+    if forward:
+        slab_ref, up_ref, down_ref, out_ref, slope_ref, rows_ref, part_ref = refs
+    else:
+        slab_ref, slope_ref, up_ref, down_ref, out_ref, rows_ref, part_ref = refs
+    step = pl.program_id(0)
+    per_expert = sources * CAP
+    half = slab_ref.shape[1]
+
+    @pl.when(step == 0)
+    def _():
+        left, right = group_rows(slab_ref, slots, held, sources)
+        for k in range(held):
+            span = slice(k * per_expert, (k + 1) * per_expert)
+            rows_ref[k, :, :half] = left[span].astype(BF16)
+            rows_ref[k, :, half:] = right[span].astype(BF16)
+
+    hidden = dot(rows_ref[step], up_ref[...], ((1,), (1,)))
+    if forward:
+        act, slope = gelu_both(hidden)
+        slope_ref[0] = slope
+    else:
+        act = hidden * slope_ref[0]
+    part = dot(act.astype(BF16), down_ref[...], ((1,), (0,)))
+    part_ref[pl.ds(pl.multiple_of(step * per_expert, 8), per_expert), :] = part
+
+    @pl.when(step == held - 1)
+    def _():
+        out_ref[...] = slab_rows(part_ref[...].astype(BF16), slots, held, sources).astype(BF16)
+
+
+def hidden_kernel(slots, held, sources, groups, *refs):
+    slab_refs, (column_ref, up_ref, act_ref, slope_ref, own_ref, rows_ref) = refs[:groups], refs[groups:]
+    step = pl.program_id(0)
+    half = slab_refs[0].shape[1]
+    fill_rows(slab_refs, rows_ref, step, slots, held, sources)
+    hidden = dot(rows_ref[step], up_ref[...], ((1,), (1,)))
+    act, slope = gelu_both(hidden)
+    act_ref[0] = act.astype(BF16)
+    slope_ref[0] = slope.astype(BF16)
+    wide = own_ref.shape[2]
+    own_ref[0] = rows_ref[step, :, pl.ds(pl.multiple_of(column_ref[0], 128), wide)]
+
+
+def fill_rows(slab_refs, rows_ref, step, slots, held, sources):
+    per_expert = sources * CAP
+    half = slab_refs[0].shape[1]
+
+    @pl.when(step == 0)
+    def _():
+        grouped = [group_rows(ref, slots, held, sources) for ref in slab_refs]
+        for side in (0, 1):
+            for k in range(held):
+                span = slice(k * per_expert, (k + 1) * per_expert)
+                joined = jnp.concatenate([parts[side][span] for parts in grouped], axis=0)
+                rows_ref[k, :, side * half : (side + 1) * half] = joined.astype(BF16)
+
+
+def gradient_kernel(slots, held, sources, groups, factor, *refs):
+    slab_refs = refs[:groups]
+    column_ref, up_ref, act_ref, slope_ref, own_ref, grad_in_ref, grad_out_ref, rows_ref = refs[groups:]
+    step = pl.program_id(0)
+    fill_rows(slab_refs, rows_ref, step, slots, held, sources)
+    back = dot(rows_ref[step], up_ref[...], ((1,), (1,)))
+    dhid = (back * slope_ref[0].astype(F32)).astype(BF16)
+    wide = own_ref.shape[2]
+    own_d = rows_ref[step, :, pl.ds(pl.multiple_of(column_ref[0], 128), wide)]
+    grad_in_ref[...] = dot(own_ref[0], dhid, ((0,), (0,))) * factor
+    grad_out_ref[...] = dot(own_d, act_ref[0], ((0,), (0,))) * factor
+
+
+def as_column(row):
+    count = row.shape[1]
+    same = iota((count, count), 0) == iota((count, count), 1)
+    return jnp.sum(jnp.where(same, row, 0.0), axis=1, keepdims=True)
+
+
+def as_row(column):
+    count = column.shape[0]
+    same = iota((count, count), 0) == iota((count, count), 1)
+    return jnp.sum(jnp.where(same, column, 0.0), axis=0, keepdims=True)
+
+
+def picked(target_ref, slots, rows):
+    slot, right = slab_slot(iota((1, rows), 1), slots)
+    columns = [as_column(target_ref[k : k + 1, :].astype(F32)).astype(jnp.int32) for k in (0, 1)]
+    return [[(slot == column) & (right == side) for side in (0, 1)] for column in columns]
+
+
+def output_kernel(slots, target_ref, gate_ref, cot_ref, back_ref, out_ref, gate_grad_ref):
+    half = back_ref.shape[1]
+    masks = picked(target_ref, slots, back_ref.shape[0])
+    back = back_ref[...]
+    gates = gate_ref[...]
+    cot = cot_ref[...].astype(F32)
+    layer, dots = [0.0, 0.0], []
+    for k in (0, 1):
+        gate = as_column(gates[k : k + 1, :])
+        grad = 0.0
+        for side in (0, 1):
+            rows = dot(ones_where(masks[k][side]), back, ((1,), (0,)))
+            layer[side] = layer[side] + gate * rows
+            part = cot[:, side * half : (side + 1) * half] * rows
+            grad = grad + jnp.sum(part, axis=1, keepdims=True)
+        dots.append(as_row(grad))
+    for side in (0, 1):
+        out_ref[:, side * half : (side + 1) * half] = layer[side].astype(BF16)
+    gate_grad_ref[...] = jnp.concatenate(dots, axis=0)
+
+
+def input_kernel(slots, target_ref, back_ref, out_ref):
+    half = back_ref.shape[1]
+    masks = picked(target_ref, slots, back_ref.shape[0])
+    back = back_ref[...]
+    for side in (0, 1):
+        pick = ones_where(masks[0][side] | masks[1][side])
+        out_ref[:, side * half : (side + 1) * half] = dot(pick, back, ((1,), (0,))).astype(BF16)
+
+
+def params():
+    return pltpu.CompilerParams(vmem_limit_bytes=VMEM_BYTES)
+
+
+def cost(flops, bytes_accessed):
+    return pl.CostEstimate(flops=int(flops), bytes_accessed=int(bytes_accessed), transcendentals=0)
+
+
+def local_rows(tokens, gate_values, expert_ids, cotangent, weight_in, weight_out):
+    sources = lax.axis_size("seq")
+    groups = lax.axis_size("dp")
+    count, width = tokens.shape
+    half = width // 2
+    held = weight_in.shape[0] // FF
+    slots = held * CAP
+    per_expert = sources * CAP
+    stacked = sources * 2 * slots
+    factor = (E / (2.0 * count * sources * groups)) ** 0.5
+    slab = jax.ShapeDtypeStruct((stacked, half), BF16)
+    vmem = pl.BlockSpec(memory_space=pltpu.VMEM)
+
+    def whole(shape):
+        return pl.BlockSpec(shape, lambda k: (0,) * len(shape))
+
+    def by_expert(shape):
+        return pl.BlockSpec((1, *shape), lambda k: (k, 0, 0))
+
+    weights = pl.BlockSpec((FF, width), lambda k: (k, 0))
+    ids_rows, gate_rows = expert_ids.T, gate_values.T
+    send_x, send_d, target = pl.pallas_call(
+        functools.partial(dispatch_kernel, slots),
+        out_shape=(slab, slab, jax.ShapeDtypeStruct((2, count), jnp.int32)),
+        in_specs=[vmem] * 4,
+        out_specs=(vmem,) * 3,
+        compiler_params=params(),
+        name="dispatch",
+    )(ids_rows, gate_rows, tokens, cotangent)
+
+    def exchange(stack):
+        cut = stack.reshape(sources, 2 * slots, half)
+        return lax.all_to_all(cut, "seq", split_axis=0, concat_axis=0, tiled=True).reshape(stacked, half)
+
+    def from_peers(stack):
+        got = [stack]
+        bit = groups // 2
+        while bit:
+            pairs = [(i, i ^ bit) for i in range(groups)]
+            got = got + [lax.ppermute(one, "dp", pairs) for one in got]
+            bit = bit // 2
+        return got
+
+    product = 2 * held * per_expert * FF * width
+    weight_bytes = 2 * weight_in.size
+
+    got_x = exchange(send_x)
+    got_d = exchange(send_d)
+    all_x = from_peers(got_x)
+
+    send_out, slope = pl.pallas_call(
+        functools.partial(expert_kernel, slots, held, sources, True),
+        grid=(held,),
+        out_shape=(slab, jax.ShapeDtypeStruct((held, per_expert, FF), F32)),
+        in_specs=[whole((stacked, half)), weights, weights],
+        out_specs=(whole((stacked, half)), by_expert((per_expert, FF))),
+        scratch_shapes=[
+            pltpu.VMEM((held, per_expert, width), BF16),
+            pltpu.VMEM((held * per_expert, width), F32),
+        ],
+        compiler_params=params(),
+        cost_estimate=cost(2 * product, 2 * weight_bytes),
+        name="expert_forward",
+    )(got_x, weight_in, weight_out)
+    got_out = exchange(send_out)
+    all_d = from_peers(got_d)
+    send_in = pl.pallas_call(
+        functools.partial(expert_kernel, slots, held, sources, False),
+        grid=(held,),
+        out_shape=slab,
+        in_specs=[whole((stacked, half)), by_expert((per_expert, FF)), weights, weights],
+        out_specs=whole((stacked, half)),
+        scratch_shapes=[
+            pltpu.VMEM((held, per_expert, width), BF16),
+            pltpu.VMEM((held * per_expert, width), F32),
+        ],
+        compiler_params=params(),
+        cost_estimate=cost(2 * product, 2 * weight_bytes),
+        name="expert_backward",
+    )(got_d, slope, weight_out, weight_in)
+    got_in = exchange(send_in)
+
+    share = width // groups
+    column = (lax.axis_index("dp") * share).astype(jnp.int32).reshape(1)
+    scalar = pl.BlockSpec(memory_space=pltpu.SMEM)
+    group_rows_count = groups * per_expert
+    act, slope_all, own_x = pl.pallas_call(
+        functools.partial(hidden_kernel, slots, held, sources, groups),
+        grid=(held,),
+        out_shape=(
+            jax.ShapeDtypeStruct((held, group_rows_count, FF), BF16),
+            jax.ShapeDtypeStruct((held, group_rows_count, FF), BF16),
+            jax.ShapeDtypeStruct((held, group_rows_count, share), BF16),
+        ),
+        in_specs=[whole((stacked, half))] * groups + [scalar, weights],
+        out_specs=(
+            by_expert((group_rows_count, FF)),
+            by_expert((group_rows_count, FF)),
+            by_expert((group_rows_count, share)),
+        ),
+        scratch_shapes=[pltpu.VMEM((held, group_rows_count, width), BF16)],
+        compiler_params=params(),
+        cost_estimate=cost(groups * product, 2 * weight_bytes),
+        name="hidden_all",
+    )(*all_x, column, weight_in)
+    gradient = jax.ShapeDtypeStruct((share, held * FF), F32)
+    gradient_spec = pl.BlockSpec((share, FF), lambda k: (0, k))
+    weight_in_grad, weight_out_grad = pl.pallas_call(
+        functools.partial(gradient_kernel, slots, held, sources, groups, factor),
+        grid=(held,),
+        out_shape=(gradient, gradient),
+        in_specs=[whole((stacked, half))] * groups
+        + [
+            scalar,
+            weights,
+            by_expert((group_rows_count, FF)),
+            by_expert((group_rows_count, FF)),
+            by_expert((group_rows_count, share)),
+        ],
+        out_specs=(gradient_spec, gradient_spec),
+        scratch_shapes=[pltpu.VMEM((held, group_rows_count, width), BF16)],
+        compiler_params=params(),
+        cost_estimate=cost((groups + 2) * product, 4 * weight_bytes),
+        name="gradients",
+    )(*all_d, column, weight_out, act, slope_all, own_x)
+
+    layer_out, gate_grad = pl.pallas_call(
+        functools.partial(output_kernel, slots),
+        out_shape=(
+            jax.ShapeDtypeStruct((count, width), BF16),
+            jax.ShapeDtypeStruct((2, count), F32),
+        ),
+        in_specs=[vmem] * 4,
+        out_specs=(vmem, vmem),
+        compiler_params=params(),
+        name="combine_output",
+    )(target, gate_rows, cotangent, got_out)
+    input_grad = pl.pallas_call(
+        functools.partial(input_kernel, slots),
+        out_shape=jax.ShapeDtypeStruct((count, width), BF16),
+        in_specs=[vmem] * 2,
+        out_specs=vmem,
+        compiler_params=params(),
+        name="combine_input",
+    )(target, got_in)
+    return layer_out, gate_grad.T, input_grad, weight_in_grad, weight_out_grad
+
+
 def slot_numbers(ids_block):
     flat_ids = ids_block.reshape(-1)
     onehot = (flat_ids[:, None] == jnp.arange(E, dtype=jnp.int32)[None, :]).astype(jnp.int32)
@@ -33,7 +409,7 @@
     return jnp.sum(before * onehot, axis=1).reshape(ids_block.shape)
 
 
-def local(tokens, gate_values, expert_ids, cotangent, weight_in, weight_out):
+def local_sums(tokens, gate_values, expert_ids, cotangent, weight_in, weight_out):
     seq_count = lax.axis_size("seq")
     group_count = lax.axis_size("dp")
     own_units = weight_in.shape[0]
@@ -82,19 +458,17 @@
 
     rows_x = to_rows(lax.all_to_all(send_x, "seq", split_axis=0, concat_axis=0, tiled=True))
     hidden = jnp.einsum("krd,kfd->krf", rows_x, win_local, preferred_element_type=jnp.float32)
-    owner_act = gelu_value(hidden).astype(jnp.bfloat16)
+    act = gelu_value(hidden).astype(jnp.bfloat16)
     part_out = jnp.einsum(
-        "krf,kfd->krd", owner_act, wout_local, preferred_element_type=jnp.float32
+        "krf,kfd->krd", act, wout_local, preferred_element_type=jnp.float32
     ).astype(jnp.bfloat16)
-    hidden, act, part_out = (hidden, owner_act, part_out)
     back_out = lax.all_to_all(from_rows(part_out), "seq", split_axis=0, concat_axis=0, tiled=True)
     rows_d = to_rows(lax.all_to_all(send_d, "seq", split_axis=0, concat_axis=0, tiled=True))
     back_hidden = jnp.einsum("krd,kfd->krf", rows_d, wout_local, preferred_element_type=jnp.float32)
-    owner_dhid = (back_hidden * gelu_slope(hidden)).astype(jnp.bfloat16)
+    dhid = (back_hidden * gelu_slope(hidden)).astype(jnp.bfloat16)
     part_in = jnp.einsum(
-        "krf,kfd->krd", owner_dhid, win_local, preferred_element_type=jnp.float32
+        "krf,kfd->krd", dhid, win_local, preferred_element_type=jnp.float32
     ).astype(jnp.bfloat16)
-    dhid, part_in = (owner_dhid, part_in)
     back_in = lax.all_to_all(from_rows(part_in), "seq", split_axis=0, concat_axis=0, tiled=True)
 
     def collect(returned):
@@ -118,13 +492,13 @@
     d_columns = jnp.transpose(rows_d, (2, 0, 1))
     grad_in_part = (
         jnp.einsum("dkr,krf->dkf", x_columns, dhid, preferred_element_type=jnp.float32).reshape(
-            lax.axis_size("dp") * (model_width // group_count), own_units
+            model_width, own_units
         )
         * factor
     )
     grad_out_part = (
         jnp.einsum("dkr,krf->dkf", d_columns, act, preferred_element_type=jnp.float32).reshape(
-            lax.axis_size("dp") * (model_width // group_count), own_units
+            model_width, own_units
         )
         * factor
     )
@@ -139,6 +513,16 @@
     return (layer_out, gate_grad, input_grad, weight_in_grad, weight_out_grad)
 
 
+def local(tokens, gate_values, expert_ids, cotangent, weight_in, weight_out):
+    units = weight_in.shape[0]
+    row_values = lax.axis_size("seq") * max(units // FF, 1) * CAP * lax.axis_size("dp")
+    if units % FF == 0 and row_values < units:
+        plan = local_rows
+    else:
+        plan = local_sums
+    return plan(tokens, gate_values, expert_ids, cotangent, weight_in, weight_out)
+
+
 def solution(mesh):
     in_specs = (
         P(("dp", "seq"), None),

time: 266 us -> 114 us (0.43)
  waiting for transfers between devices: 120 us -> 20.6 us
  local copies, waits for them, and re-layouts: 57.7 us -> 3.26 us
  Pallas kernels: 0 us -> 50.4 us
  matrix products: 32.1 us -> 0 us
  blocking collectives: 0 us -> 23.6 us
  other arithmetic: 22 us -> 0 us
  between operations: 14.4 us -> 0.68 us
  starting transfers between devices: 18.5 us -> 14.5 us
    reduce_scatter x1 -> x0, waiting for transfers between devices: 69.1 us -> none  [local(): lax.psum_scatter(jnp.concatenate([grad_in_part, grad_out_part], axis=1).a...]
    pallas_call x0 -> x7, Pallas kernels: none -> 50.4 us  [the longest x1 12.7 us: local_rows(): pl.pallas_call(functools.partial(gradient_kernel, slots, held, sources, g...]
    all_to_all x4 -> x3, waiting for transfers between devices: 50.7 us -> 7.81 us  [exchange(): lax.all_to_all(cut, 'seq', split_axis=0, concat_axis=0, tiled=True)]
    dot_general x6 -> x0, matrix products: 32.1 us -> none  [the longest x1 6.9 us: local(): jnp.einsum('krf,kfd->krd', owner_act, wout_local, preferred_element_type=...]
    mul x5 -> x0, local copies, waits for them, and re-layouts: 23.7 us -> none  [the longest x1 12 us: local(): jnp.einsum('dkr,krf->dkf', x_columns, dhid, preferred_element_type=jnp.fl...]
    all_to_all x0 -> x1, blocking collectives: none -> 23.6 us  [exchange(): lax.all_to_all(cut, 'seq', split_axis=0, concat_axis=0, tiled=True)]
    gather x8 -> x0, local copies, waits for them, and re-layouts: 14 us -> none  [the longest x3 2.54 us: collect(): summed = summed + flat_rows[row_at].astype(jnp.float32)]
    concatenate x1 -> x0, other arithmetic: 13.7 us -> none  [local(): jnp.concatenate([grad_in_part, grad_out_part], axis=1).astype(jnp.bfloat16)]
  transfers between devices with their start and end apart: 5 -> 9, of which waited for: 5 -> 3; matrix products, arithmetic and copies ran while one was open for 12% -> 0% of each run, Pallas kernels for 0% -> 32%
where the time goes in v1:
time: 114 us; the launch traced here: 113 us
  Pallas kernels  50.4 us (44%)
  blocking collectives  23.6 us (21%)
  waiting for transfers between devices  20.6 us (18%)
  starting transfers between devices  14.5 us (13%)
  local copies, waits for them, and re-layouts  3.26 us (3%)
    all_to_all x1, blocking collectives, exchange(): lax.all_to_all(cut, 'seq', split_axis=0, concat_axis=0, tiled=True)  23.6 us
    ppermute x6, waiting for transfers between devices, from_peers(): got = got + [lax.ppermute(one, 'dp', pairs) for one in got]  12.8 us
    pallas_call x1, Pallas kernels, local_rows(): pl.pallas_call(functools.partial(gradient_kernel, slots, held, sources, g...  12.7 us
    pallas_call x1, Pallas kernels, local_rows(): pl.pallas_call(functools.partial(hidden_kernel, slots, held, sources, gro...  11.7 us
    all_to_all x3, starting transfers between devices, exchange(): lax.all_to_all(cut, 'seq', split_axis=0, concat_axis=0, tiled=True)  10.9 us
    pallas_call x1, Pallas kernels, local_rows(): pl.pallas_call(functools.partial(expert_kernel, slots, held, sources, Tru...  10.8 us
    pallas_call x1, Pallas kernels, local_rows(): pl.pallas_call(functools.partial(expert_kernel, slots, held, sources, Fal...  10.6 us
    all_to_all x3, waiting for transfers between devices, exchange(): lax.all_to_all(cut, 'seq', split_axis=0, concat_axis=0, tiled=True)  7.81 us
  transfers between devices with their start and end apart: 9, of which 3 were waited for; matrix products, arithmetic and copies ran while one was open for 0% of the time, Pallas kernels for 32%

profile of v1, /device:TPU:0, one launch (start us, length us, event | category | flops | bytes accessed | tf_op | source)
XLA Modules:
  0.0 113.0 jit_solution(6576527492847354390)
XLA Ops:
  0.6 0.0 copy-start
  0.6 0.9 copy-done
  1.6 0.0 copy-start.2
  1.6 0.9 copy-done.2
  2.5 0.0 copy-start.3
  2.5 0.7 copy-done.3
  3.2 0.0 copy-start.5
  3.2 0.7 copy-done.5
  3.9 1.7 %dispatch.1 = (bf16[576,512]{1,0:T(8,128)(2,1)S(1)}, bf16[576,512]{1,0:T(8,128)(2,1)}, s32[2,128]{1,0:T(2,128)S(1)}) custom-call(s32[2,128]{1,0:T(2,128)S(1)} %bitcast.25, f32[2,128]{1,0:T(2,128)S(1)} %bitcast.23, bf16[128,1024]{1,0:T(8,128)(2,1)S(1)} %copy-done.2, bf16[128,1024]{1,0:T(8,128)(2,1)S(1)} %copy-done), custom_call_target="tpu_custom_call" | custom-call | tf_op jit(solution)/shard_map/dispatch/pallas_call | solution.py:278
  5.6 23.6 %all_to_all.20 = bf16[8,72,512]{2,1,0:T(8,128)(2,1)S(1)} all-to-all(bf16[8,72,512]{2,1,0:T(8,128)(2,1)S(1)} %bitcast.22), channel_id=1, replica_groups=mesh['dp'=4,'seq'=8] {'seq'}, dimensions={0} | all-to-all | bytes 1179648 | tf_op jit(solution)/shard_map/all_to_all | solution.py:289
  29.2 3.5 %all-to-all-start.2 = ((bf16[8,72,512]{2,1,0:T(8,128)(2,1)}), bf16[8,72,512]{2,1,0:T(8,128)(2,1)S(1)}, u32[]{:S(2)}, u32[]{:S(2)}) async-start(bf16[8,72,512]{2,1,0:T(8,128)(2,1)} %bitcast.7), calls=%async_computation.2 | async-start | bytes 1179648 | tf_op jit(solution)/shard_map/all_to_all | solution.py:289
  32.8 10.8 %expert_forward.1 = (bf16[576,512]{1,0:T(8,128)(2,1)}, f32[4,72,1024]{2,1,0:T(8,128)S(1)}) custom-call(bf16[576,512]{1,0:T(8,128)(2,1)S(1)} %bitcast.16, bf16[4096,1024]{1,0:T(8,128)(2,1)} %refs_5_.2, bf16[4096,1024]{1,0:T(8,128)(2,1)} %refs_5_.3), custom_call_target="tpu_custom_call" | custom-call | flops 1207959552 | bytes 16777216 | tf_op jit(solution)/shard_map/expert_forward/pallas_call | solution.py:307
  43.6 4.3 %all-to-all-done.2 = bf16[8,72,512]{2,1,0:T(8,128)(2,1)S(1)} async-done(((bf16[8,72,512]{2,1,0:T(8,128)(2,1)}), bf16[8,72,512]{2,1,0:T(8,128)(2,1)S(1)}, u32[]{:S(2)}, u32[]{:S(2)}) %all-to-all-start.2) | async-done | bytes 589856 | tf_op jit(solution)/shard_map/all_to_all | solution.py:289
  48.0 3.6 %all-to-all-start.1 = ((bf16[8,72,512]{2,1,0:T(8,128)(2,1)}), bf16[8,72,512]{2,1,0:T(8,128)(2,1)S(1)}, u32[]{:S(2)}, u32[]{:S(2)}) async-start(bf16[8,72,512]{2,1,0:T(8,128)(2,1)} %bitcast.4), calls=%async_computation.1 | async-start | bytes 1179648 | tf_op jit(solution)/shard_map/all_to_all | solution.py:289
  51.6 1.5 %collective-permute-start.3 = (bf16[576,512]{1,0:T(8,128)(2,1)S(1)}, bf16[576,512]{1,0:T(8,128)(2,1)}, u32[]{:S(2)}, u32[]{:S(2)}) collective-permute-start(bf16[576,512]{1,0:T(8,128)(2,1)S(1)} %bitcast.17), channel_id=1, source_target_pairs={{0,16},{8,24},{16,0},{24,8},{1,17},{9,25},{17,1},{25,9},{2,18},{10... | collective-permute-start | bytes 1769480 | tf_op jit(solution)/shard_map/ppermute | solution.py:296
  53.1 0.0 copy-start.1
  53.1 0.0 copy-start.4
  53.1 10.6 %expert_backward.1 = bf16[576,512]{1,0:T(8,128)(2,1)} custom-call(bf16[576,512]{1,0:T(8,128)(2,1)S(1)} %bitcast.12, f32[4,72,1024]{2,1,0:T(8,128)S(1)} %get-tuple-element.23.refs_1_, bf16[4096,1024]{1,0:T(8,128)(2,1)} %refs_5_.3, bf16[4096,1024]{1,0:T(8,128)(2,1)} %refs_5_.2), custom_call_target="tpu_custom_call" | custom-call | flops 1207959552 | bytes 16777216 | tf_op jit(solution)/shard_map/expert_backward/pallas_call | solution.py:323
  63.8 3.5 %all-to-all-done.1 = bf16[8,72,512]{2,1,0:T(8,128)(2,1)S(1)} async-done(((bf16[8,72,512]{2,1,0:T(8,128)(2,1)}), bf16[8,72,512]{2,1,0:T(8,128)(2,1)S(1)}, u32[]{:S(2)}, u32[]{:S(2)}) %all-to-all-start.1) | async-done | bytes 589856 | tf_op jit(solution)/shard_map/all_to_all | solution.py:289
  67.3 3.7 %all-to-all-start.3 = ((bf16[8,72,512]{2,1,0:T(8,128)(2,1)}), bf16[8,72,512]{2,1,0:T(8,128)(2,1)S(1)}, u32[]{:S(2)}, u32[]{:S(2)}) async-start(bf16[8,72,512]{2,1,0:T(8,128)(2,1)} %bitcast.9), calls=%async_computation.3 | async-start | bytes 1179648 | tf_op jit(solution)/shard_map/all_to_all | solution.py:289
  71.0 1.6 %collective-permute-start = (bf16[576,512]{1,0:T(8,128)(2,1)S(1)}, bf16[576,512]{1,0:T(8,128)(2,1)S(1)}, u32[]{:S(2)}, u32[]{:S(2)}) collective-permute-start(bf16[576,512]{1,0:T(8,128)(2,1)S(1)} %bitcast.13), channel_id=1, source_target_pairs={{0,16},{8,24},{16,0},{24,8},{1,17},{9,25},{17,1},{25,9},{2,18},{10... | collective-permute-start | bytes 1769480 | tf_op jit(solution)/shard_map/ppermute | solution.py:296
  72.6 0.0 collective-permute-start.4
  72.6 0.0 collective-permute-done.3.refs_1_
  72.6 0.5 collective-permute-start.5
  73.1 0.0 collective-permute-start.1
  73.1 12.8 %collective-permute-done.refs_1_ = bf16[576,512]{1,0:T(8,128)(2,1)S(1)} collective-permute-done((bf16[576,512]{1,0:T(8,128)(2,1)S(1)}, bf16[576,512]{1,0:T(8,128)(2,1)S(1)}, u32[]{:S(2)}, u32[]{:S(2)}) %collective-permute-start) | collective-permute-done | bytes 589856 | tf_op jit(solution)/shard_map/ppermute | solution.py:296
  85.8 0.0 collective-permute-start.2
  85.8 0.0 copy-done.1
  85.9 0.0 copy-done.4
  85.9 1.5 %combine_output.1 = (bf16[128,1024]{1,0:T(8,128)(2,1)}, f32[2,128]{1,0:T(2,128)}) custom-call(s32[2,128]{1,0:T(2,128)S(1)} %get-tuple-element.17.target_ref, f32[2,128]{1,0:T(2,128)S(1)} %bitcast.24, bf16[128,1024]{1,0:T(8,128)(2,1)S(1)} %copy-done.1, bf16[576,512]{1,0:T(8,128)(2,1)S(1)} %bitcast.20), custom_call_target="tpu_custom_call" | custom-call | tf_op jit(solution)/shard_map/combine_output/pallas_call | solution.py:383
  87.3 0.0 all-to-all-done.3
  87.3 1.3 %combine_input.1 = bf16[128,1024]{1,0:T(8,128)(2,1)} custom-call(s32[2,128]{1,0:T(2,128)S(1)} %get-tuple-element.17.target_ref, bf16[576,512]{1,0:T(8,128)(2,1)S(1)} %bitcast.21), custom_call_target="tpu_custom_call" | custom-call | tf_op jit(solution)/shard_map/combine_input/pallas_call | solution.py:394
  88.6 0.0 collective-permute-done.4.refs_2_
  88.6 0.0 collective-permute-done.5.refs_3_
  88.6 11.7 %hidden_all.1 = (bf16[4,288,1024]{2,1,0:T(8,128)(2,1)}, bf16[4,288,1024]{2,1,0:T(8,128)(2,1)}, bf16[4,288,256]{2,1,0:T(8,128)(2,1)S(1)}) custom-call(bf16[576,512]{1,0:T(8,128)(2,1)S(1)} %bitcast.19, bf16[576,512]{1,0:T(8,128)(2,1)} %collective-permute-done.3.refs_1_, bf16[576,512]{1,0:T(8,128)(2,1)} %collective-permute-done.4.refs_2_, ...), custom_call_target="tpu_custom_call" | custom-call | flops 2415919104 | bytes 16777216 | tf_op jit(solution)/shard_map/hidden_all/pallas_call | solution.py:343
  100.3 0.0 collective-permute-done.1.refs_2_
  100.3 0.0 collective-permute-done.2.refs_3_
  100.3 12.7 %gradients.1 = (f32[256,4096]{1,0:T(8,128)}, f32[256,4096]{1,0:T(8,128)}) custom-call(bf16[576,512]{1,0:T(8,128)(2,1)S(1)} %bitcast.15, bf16[576,512]{1,0:T(8,128)(2,1)S(1)} %collective-permute-done.refs_1_, bf16[576,512]{1,0:T(8,128)(2,1)} %collective-permute-done.1.refs_2_, bf16[576,512]{1,0:T(8,128)(2,1)} %collective-permute-done.2.refs_3_, ...), custom_call_target="tpu_custom_call" | custom-call | flops 3623878656 | bytes 33554432 | tf_op jit(solution)/shard_map/gradients/pallas_call | solution.py:364
Async XLA Ops:
  0.6 1.0 copy-start
  1.6 0.9 copy-start.2
  2.5 0.7 copy-start.3
  3.2 0.7 copy-start.5
  29.2 18.7 %all-to-all-start.2 = ((bf16[8,72,512]{2,1,0:T(8,128)(2,1)}), bf16[8,72,512]{2,1,0:T(8,128)(2,1)S(1)}, u32[]{:S(2)}, u32[]{:S(2)}) async-start(bf16[8,72,512]{2,1,0:T(8,128)(2,1)} %bitcast.7), calls=%async_computation.2 | async-start | bytes 1179648 | tf_op jit(solution)/shard_map/all_to_all | solution.py:289
  48.0 19.3 %all-to-all-start.1 = ((bf16[8,72,512]{2,1,0:T(8,128)(2,1)}), bf16[8,72,512]{2,1,0:T(8,128)(2,1)S(1)}, u32[]{:S(2)}, u32[]{:S(2)}) async-start(bf16[8,72,512]{2,1,0:T(8,128)(2,1)} %bitcast.4), calls=%async_computation.1 | async-start | bytes 1179648 | tf_op jit(solution)/shard_map/all_to_all | solution.py:289
  51.6 21.0 %collective-permute-start.3 = (bf16[576,512]{1,0:T(8,128)(2,1)S(1)}, bf16[576,512]{1,0:T(8,128)(2,1)}, u32[]{:S(2)}, u32[]{:S(2)}) collective-permute-start(bf16[576,512]{1,0:T(8,128)(2,1)S(1)} %bitcast.17), channel_id=1, source_target_pairs={{0,16},{8,24},{16,0},{24,8},{1,17},{9,25},{17,1},{25,9},{2,18},{10... | collective-permute-start | bytes 1769480 | tf_op jit(solution)/shard_map/ppermute | solution.py:296
  53.1 32.7 %copy-start.1 = (bf16[128,1024]{1,0:T(8,128)(2,1)S(1)}, bf16[128,1024]{1,0:T(8,128)(2,1)}, u32[]{:S(2)}) copy-start(bf16[128,1024]{1,0:T(8,128)(2,1)} %cot_ref.3) | copy-start | bytes 786436
  53.1 32.7 %copy-start.4 = (f32[128,2]{0,1:T(2,128)S(1)}, f32[128,2]{0,1:T(2,128)}, u32[]{:S(2)}) copy-start(f32[128,2]{0,1:T(2,128)} %param.7) | copy-start | bytes 3076
  67.3 20.1 %all-to-all-start.3 = ((bf16[8,72,512]{2,1,0:T(8,128)(2,1)}), bf16[8,72,512]{2,1,0:T(8,128)(2,1)S(1)}, u32[]{:S(2)}, u32[]{:S(2)}) async-start(bf16[8,72,512]{2,1,0:T(8,128)(2,1)} %bitcast.9), calls=%async_computation.3 | async-start | bytes 1179648 | tf_op jit(solution)/shard_map/all_to_all | solution.py:289
  71.0 14.9 %collective-permute-start = (bf16[576,512]{1,0:T(8,128)(2,1)S(1)}, bf16[576,512]{1,0:T(8,128)(2,1)S(1)}, u32[]{:S(2)}, u32[]{:S(2)}) collective-permute-start(bf16[576,512]{1,0:T(8,128)(2,1)S(1)} %bitcast.13), channel_id=1, source_target_pairs={{0,16},{8,24},{16,0},{24,8},{1,17},{9,25},{17,1},{25,9},{2,18},{10... | collective-permute-start | bytes 1769480 | tf_op jit(solution)/shard_map/ppermute | solution.py:296
  72.6 16.0 %collective-permute-start.4 = (bf16[576,512]{1,0:T(8,128)(2,1)S(1)}, bf16[576,512]{1,0:T(8,128)(2,1)}, u32[]{:S(2)}, u32[]{:S(2)}) collective-permute-start(bf16[576,512]{1,0:T(8,128)(2,1)S(1)} %bitcast.18), channel_id=1, source_target_pairs={{0,8},{8,0},{16,24},{24,16},{1,9},{9,1},{17,25},{25,17},{2,10},{10... | collective-permute-start | bytes 1769480 | tf_op jit(solution)/shard_map/ppermute | solution.py:296
  72.6 16.0 %collective-permute-start.5 = (bf16[576,512]{1,0:T(8,128)(2,1)}, bf16[576,512]{1,0:T(8,128)(2,1)}, u32[]{:S(2)}, u32[]{:S(2)}) collective-permute-start(bf16[576,512]{1,0:T(8,128)(2,1)} %collective-permute-done.3.refs_1_), channel_id=1, source_target_pairs={{0,8},{8,0},{16,24},{24,16},{1,9},{9,1},{17,25},{25,17},{2,10},{10... | collective-permute-start | bytes 1769480 | tf_op jit(solution)/shard_map/ppermute | solution.py:296
  73.1 27.2 %collective-permute-start.1 = (bf16[576,512]{1,0:T(8,128)(2,1)S(1)}, bf16[576,512]{1,0:T(8,128)(2,1)}, u32[]{:S(2)}, u32[]{:S(2)}) collective-permute-start(bf16[576,512]{1,0:T(8,128)(2,1)S(1)} %bitcast.14), channel_id=1, source_target_pairs={{0,8},{8,0},{16,24},{24,16},{1,9},{9,1},{17,25},{25,17},{2,10},{10... | collective-permute-start | bytes 1769480 | tf_op jit(solution)/shard_map/ppermute | solution.py:296
  85.8 14.4 %collective-permute-start.2 = (bf16[576,512]{1,0:T(8,128)(2,1)S(1)}, bf16[576,512]{1,0:T(8,128)(2,1)}, u32[]{:S(2)}, u32[]{:S(2)}) collective-permute-start(bf16[576,512]{1,0:T(8,128)(2,1)S(1)} %collective-permute-done.refs_1_), channel_id=1, source_target_pairs={{0,8},{8,0},{16,24},{24,16},{1,9},{9,1},{17,25},{25,17},{2,10},{10... | collective-permute-start | bytes 1769480 | tf_op jit(solution)/shard_map/ppermute | solution.py:296

commit v2 on v1

--- a/solution.py
+++ b/solution.py
@@ -14,7 +14,6 @@
 
 BF16 = jnp.bfloat16
 F32 = jnp.float32
-VMEM_BYTES = 50 * 1024 * 1024
 
 gelu_scale = 0.7978845608028654
 gelu_cubic = 0.044715
@@ -66,10 +65,21 @@
     return slab * slots + rest - right * slots, right
 
 
-def dispatch_kernel(slots, ids_ref, gate_ref, tok_ref, cot_ref, x_ref, d_ref, target_ref):
+def dispatch_kernel(
+    slots, ids_hbm, gate_hbm, tok_hbm, cot_hbm, x_ref, d_ref, target_ref, ids_ref, gate_ref, tok_ref, cot_ref, sems
+):
+    copies = [
+        pltpu.make_async_copy(source, here, sems.at[i])
+        for i, (source, here) in enumerate(
+            [(ids_hbm, ids_ref), (tok_hbm, tok_ref), (gate_hbm, gate_ref), (cot_hbm, cot_ref)]
+        )
+    ]
+    for copy in copies:
+        copy.start()
     count = tok_ref.shape[0]
     half = tok_ref.shape[1] // 2
     rows = x_ref.shape[0]
+    copies[0].wait()
     ids = ids_ref[...]
     first, second = ids[0:1, :], ids[1:2, :]
     expert = iota((E, count), 0)
@@ -86,20 +96,24 @@
     is_first, is_second = slot == target_first, slot == target_second
     pick = ones_where(is_first | is_second)
     is_right = right == 1
+    copies[1].wait()
     rows_x = dot(pick, tok_ref[...], ((1,), (0,)))
     x_ref[...] = jnp.where(is_right, rows_x[:, half:], rows_x[:, :half]).astype(BF16)
+    copies[2].wait()
     gates = gate_ref[...]
     gate = jnp.sum(
         jnp.where(is_first, gates[0:1, :], 0.0) + jnp.where(is_second, gates[1:2, :], 0.0),
         axis=1,
         keepdims=True,
     )
+    copies[3].wait()
     rows_d = dot(pick, cot_ref[...], ((1,), (0,)))
     d_ref[...] = (jnp.where(is_right, rows_d[:, half:], rows_d[:, :half]) * gate).astype(BF16)
 
 
-def group_rows(slab_ref, slots, held, sources):
+def regroup_kernel(slots, held, sources, slab_ref, rows_ref):
     per_expert = sources * CAP
+    half = slab_ref.shape[1]
     number = iota((held * per_expert, 1), 0)
     expert = quotient(number, per_expert)
     rest = number - expert * per_expert
@@ -107,7 +121,11 @@
     row = source * (2 * slots) + expert * CAP + rest - source * CAP
     at = iota((held * per_expert, 2 * slots * sources), 1)
     slabs = slab_ref[...]
-    return [dot(ones_where(at == row + side * slots), slabs, ((1,), (0,))) for side in (0, 1)]
+    for side in (0, 1):
+        rows = dot(ones_where(at == row + side * slots), slabs, ((1,), (0,)))
+        for k in range(held):
+            span = slice(k * per_expert, (k + 1) * per_expert)
+            rows_ref[k, :, side * half : (side + 1) * half] = rows[span].astype(BF16)
 
 
 def slab_rows(rows, slots, held, sources):
@@ -125,77 +143,91 @@
     return jnp.where(is_right, out[:, half:], out[:, :half])
 
 
-def expert_kernel(
-    slots, held, sources, forward, *refs
+def weight_copies(up_hbm, down_hbm, up_ref, down_ref, sems):
+    held = up_ref.shape[0]
+    ups = [pltpu.make_async_copy(up_hbm.at[k], up_ref.at[k], sems.at[0, k]) for k in range(held)]
+    downs = [pltpu.make_async_copy(down_hbm.at[k], down_ref.at[k], sems.at[1, k]) for k in range(held)]
+    return ups, downs
+
+
+def forward_kernel(
+    slots, held, sources, rows_ref, up_hbm, down_hbm, out_ref, act_hbm, slope_hbm, up_ref, down_ref, act_ref, slope_ref, sems
 ):
-    if forward:
-        slab_ref, up_ref, down_ref, out_ref, slope_ref, rows_ref, part_ref = refs
-    else:
-        slab_ref, slope_ref, up_ref, down_ref, out_ref, rows_ref, part_ref = refs
-    step = pl.program_id(0)
-    per_expert = sources * CAP
-    half = slab_ref.shape[1]
-
-    @pl.when(step == 0)
-    def _():
-        left, right = group_rows(slab_ref, slots, held, sources)
-        for k in range(held):
-            span = slice(k * per_expert, (k + 1) * per_expert)
-            rows_ref[k, :, :half] = left[span].astype(BF16)
-            rows_ref[k, :, half:] = right[span].astype(BF16)
-
-    hidden = dot(rows_ref[step], up_ref[...], ((1,), (1,)))
-    if forward:
-        act, slope = gelu_both(hidden)
-        slope_ref[0] = slope
-    else:
-        act = hidden * slope_ref[0]
-    part = dot(act.astype(BF16), down_ref[...], ((1,), (0,)))
-    part_ref[pl.ds(pl.multiple_of(step * per_expert, 8), per_expert), :] = part
-
-    @pl.when(step == held - 1)
-    def _():
-        out_ref[...] = slab_rows(part_ref[...].astype(BF16), slots, held, sources).astype(BF16)
-
-
-def hidden_kernel(slots, held, sources, groups, *refs):
-    slab_refs, (column_ref, up_ref, act_ref, slope_ref, own_ref, rows_ref) = refs[:groups], refs[groups:]
-    step = pl.program_id(0)
-    half = slab_refs[0].shape[1]
-    fill_rows(slab_refs, rows_ref, step, slots, held, sources)
-    hidden = dot(rows_ref[step], up_ref[...], ((1,), (1,)))
-    act, slope = gelu_both(hidden)
-    act_ref[0] = act.astype(BF16)
-    slope_ref[0] = slope.astype(BF16)
-    wide = own_ref.shape[2]
-    own_ref[0] = rows_ref[step, :, pl.ds(pl.multiple_of(column_ref[0], 128), wide)]
-
-
-def fill_rows(slab_refs, rows_ref, step, slots, held, sources):
-    per_expert = sources * CAP
-    half = slab_refs[0].shape[1]
-
-    @pl.when(step == 0)
-    def _():
-        grouped = [group_rows(ref, slots, held, sources) for ref in slab_refs]
-        for side in (0, 1):
-            for k in range(held):
-                span = slice(k * per_expert, (k + 1) * per_expert)
-                joined = jnp.concatenate([parts[side][span] for parts in grouped], axis=0)
-                rows_ref[k, :, side * half : (side + 1) * half] = joined.astype(BF16)
-
-
-def gradient_kernel(slots, held, sources, groups, factor, *refs):
-    slab_refs = refs[:groups]
-    column_ref, up_ref, act_ref, slope_ref, own_ref, grad_in_ref, grad_out_ref, rows_ref = refs[groups:]
-    step = pl.program_id(0)
-    fill_rows(slab_refs, rows_ref, step, slots, held, sources)
-    back = dot(rows_ref[step], up_ref[...], ((1,), (1,)))
-    dhid = (back * slope_ref[0].astype(F32)).astype(BF16)
-    wide = own_ref.shape[2]
-    own_d = rows_ref[step, :, pl.ds(pl.multiple_of(column_ref[0], 128), wide)]
-    grad_in_ref[...] = dot(own_ref[0], dhid, ((0,), (0,))) * factor
-    grad_out_ref[...] = dot(own_d, act_ref[0], ((0,), (0,))) * factor
+    ups, downs = weight_copies(up_hbm, down_hbm, up_ref, down_ref, sems)
+    for up, down in zip(ups, downs):
+        up.start()
+        down.start()
+    parts, stores = [], []
+    ups[0].wait()
+    hidden = dot(rows_ref[0], up_ref[0], ((1,), (1,)))
+    for k in range(held):
+        now = hidden
+        downs[k].wait()
+        if k + 1 < held:
+            ups[k + 1].wait()
+            hidden = dot(rows_ref[k + 1], up_ref[k + 1], ((1,), (1,)))
+        value, slope = gelu_both(now)
+        act = value.astype(BF16)
+        act_ref[k] = act
+        slope_ref[k] = slope.astype(BF16)
+        parts.append(dot(act, down_ref[k], ((1,), (0,))))
+        for i, (here, there) in enumerate([(act_ref, act_hbm), (slope_ref, slope_hbm)]):
+            stores.append(pltpu.make_async_copy(here.at[k], there.at[k], sems.at[2 + i, k]))
+            stores[-1].start()
+    rows = jnp.concatenate(parts, axis=0).astype(BF16)
+    out_ref[...] = slab_rows(rows, slots, held, sources).astype(BF16)
+    for store in stores:
+        store.wait()
+
+
+def backward_kernel(
+    slots, held, sources, rows_ref, slope_hbm, up_hbm, down_hbm, out_ref, dhid_hbm, up_ref, down_ref, dhid_ref, slope_ref, sems
+):
+    ups, downs = weight_copies(up_hbm, down_hbm, up_ref, down_ref, sems)
+    slopes = pltpu.make_async_copy(slope_hbm, slope_ref, sems.at[3, 0])
+    for k in range(held):
+        ups[k].start()
+        if k == 0:
+            slopes.start()
+        downs[k].start()
+    parts, stores = [], []
+    ups[0].wait()
+    back = dot(rows_ref[0], up_ref[0], ((1,), (1,)))
+    slopes.wait()
+    for k in range(held):
+        now = back
+        downs[k].wait()
+        if k + 1 < held:
+            ups[k + 1].wait()
+            back = dot(rows_ref[k + 1], up_ref[k + 1], ((1,), (1,)))
+        dhid = (now * slope_ref[k].astype(F32)).astype(BF16)
+        dhid_ref[k] = dhid
+        parts.append(dot(dhid, down_ref[k], ((1,), (0,))))
+        stores.append(pltpu.make_async_copy(dhid_ref.at[k], dhid_hbm.at[k], sems.at[2, k]))
+        stores[-1].start()
+    rows = jnp.concatenate(parts, axis=0).astype(BF16)
+    out_ref[...] = slab_rows(rows, slots, held, sources).astype(BF16)
+    for store in stores:
+        store.wait()
+
+
+def gradient_kernel(peers, factor, share_ref, *refs):
+    own_x_ref, own_d_ref, act_ref, dhid_ref, up_ref, down_ref = refs[:6]
+    x_refs, d_refs = refs[6 : 6 + peers], refs[6 + peers : 6 + 2 * peers]
+    grad_in_ref, grad_out_ref = refs[6 + 2 * peers :]
+    wide = grad_in_ref.shape[0]
+    share = pl.ds(pl.multiple_of(share_ref[0] * wide, 128), wide)
+    rows_x = jnp.concatenate([ref[0] for ref in x_refs], axis=0)
+    rows_d = jnp.concatenate([ref[0] for ref in d_refs], axis=0)
+    hidden = dot(rows_x, up_ref[0], ((1,), (1,)))
+    back = dot(rows_d, down_ref[0], ((1,), (1,)))
+    value, slope = gelu_both(hidden)
+    acts = jnp.concatenate([act_ref[0], value.astype(BF16)], axis=0)
+    cut_d = jnp.concatenate([own_d_ref[0]] + [ref[0, :, share] for ref in d_refs], axis=0)
+    grad_out_ref[...] = dot(cut_d, acts, ((0,), (0,))) * factor
+    dhids = jnp.concatenate([dhid_ref[0], (back * slope).astype(BF16)], axis=0)
+    cut_x = jnp.concatenate([own_x_ref[0]] + [ref[0, :, share] for ref in x_refs], axis=0)
+    grad_in_ref[...] = dot(cut_x, dhids, ((0,), (0,))) * factor
 
 
 def as_column(row):
@@ -246,17 +278,31 @@
         out_ref[:, side * half : (side + 1) * half] = dot(pick, back, ((1,), (0,))).astype(BF16)
 
 
-def params():
-    return pltpu.CompilerParams(vmem_limit_bytes=VMEM_BYTES)
+def params(mib=58):
+    return pltpu.CompilerParams(vmem_limit_bytes=mib * 1024 * 1024)
 
 
 def cost(flops, bytes_accessed):
     return pl.CostEstimate(flops=int(flops), bytes_accessed=int(bytes_accessed), transcendentals=0)
+
+
+def vmem_call(kernel, outs, args, name, estimate=None, mib=6):
+    vmem = pl.BlockSpec(memory_space=pltpu.VMEM)
+    return pl.pallas_call(
+        kernel,
+        out_shape=outs,
+        in_specs=[vmem] * len(args),
+        out_specs=jax.tree.map(lambda _: vmem, outs),
+        compiler_params=params(mib),
+        cost_estimate=estimate,
+        name=name,
+    )(*args)
 
 
 def local_rows(tokens, gate_values, expert_ids, cotangent, weight_in, weight_out):
     sources = lax.axis_size("seq")
     groups = lax.axis_size("dp")
+    peers = groups - 1
     count, width = tokens.shape
     half = width // 2
     held = weight_in.shape[0] // FF
@@ -265,140 +311,133 @@
     stacked = sources * 2 * slots
     factor = (E / (2.0 * count * sources * groups)) ** 0.5
     slab = jax.ShapeDtypeStruct((stacked, half), BF16)
+    rows_shape = jax.ShapeDtypeStruct((held, per_expert, width), BF16)
+    units_shape = jax.ShapeDtypeStruct((held, per_expert, FF), BF16)
+    product = 2 * held * per_expert * FF * width
     vmem = pl.BlockSpec(memory_space=pltpu.VMEM)
 
-    def whole(shape):
-        return pl.BlockSpec(shape, lambda k: (0,) * len(shape))
-
-    def by_expert(shape):
-        return pl.BlockSpec((1, *shape), lambda k: (k, 0, 0))
-
-    weights = pl.BlockSpec((FF, width), lambda k: (k, 0))
+    hbm = pl.BlockSpec(memory_space=pltpu.HBM)
+    sems = pltpu.SemaphoreType.DMA
+
     ids_rows, gate_rows = expert_ids.T, gate_values.T
     send_x, send_d, target = pl.pallas_call(
         functools.partial(dispatch_kernel, slots),
         out_shape=(slab, slab, jax.ShapeDtypeStruct((2, count), jnp.int32)),
-        in_specs=[vmem] * 4,
+        in_specs=[hbm] * 4,
         out_specs=(vmem,) * 3,
+        scratch_shapes=[
+            pltpu.VMEM((2, count), jnp.int32),
+            pltpu.VMEM((2, count), F32),
+            pltpu.VMEM((count, width), BF16),
+            pltpu.VMEM((count, width), BF16),
+            sems((4,)),
+        ],
         compiler_params=params(),
         name="dispatch",
     )(ids_rows, gate_rows, tokens, cotangent)
+    win = weight_in.reshape(held, FF, width)
+    wout = weight_out.reshape(held, FF, width)
 
     def exchange(stack):
         cut = stack.reshape(sources, 2 * slots, half)
         return lax.all_to_all(cut, "seq", split_axis=0, concat_axis=0, tiled=True).reshape(stacked, half)
 
-    def from_peers(stack):
-        got = [stack]
-        bit = groups // 2
+    def regroup(stack):
+        return vmem_call(
+            functools.partial(regroup_kernel, slots, held, sources),
+            rows_shape,
+            [stack],
+            "regroup",
+            cost(product, 4 * stacked * half),
+        )
+
+    def across(rows, bit):
+        return lax.ppermute(rows, "dp", [(i, i ^ bit) for i in range(groups)])
+
+    got_x = exchange(send_x)
+    got_d = exchange(send_d)
+    rows_x = regroup(got_x)
+    peers_x = [rows_x]
+    far = groups // 2
+    first_x = across(rows_x, far)
+
+    units = pltpu.VMEM((held, per_expert, FF), BF16)
+    experts = pltpu.VMEM((held, FF, width), BF16)
+    send_out, act, slope = pl.pallas_call(
+        functools.partial(forward_kernel, slots, held, sources),
+        out_shape=(slab, units_shape, units_shape),
+        in_specs=[vmem, hbm, hbm],
+        out_specs=(vmem, hbm, hbm),
+        scratch_shapes=[experts, experts, units, units, sems((4, held))],
+        compiler_params=params(),
+        cost_estimate=cost(4 * product, 4 * weight_in.size),
+        name="expert_forward",
+    )(rows_x, win, wout)
+    got_out = exchange(send_out)
+    got_d, first_x = lax.optimization_barrier((got_d, first_x))
+    rows_d = regroup(got_d)
+    first_d = across(rows_d, far)
+
+    def from_peers(rows, first):
+        got, bit = [rows, first], far // 2
         while bit:
-            pairs = [(i, i ^ bit) for i in range(groups)]
-            got = got + [lax.ppermute(one, "dp", pairs) for one in got]
+            got = got + [across(one, bit) for one in got]
             bit = bit // 2
         return got
 
-    product = 2 * held * per_expert * FF * width
-    weight_bytes = 2 * weight_in.size
-
-    got_x = exchange(send_x)
-    got_d = exchange(send_d)
-    all_x = from_peers(got_x)
-
-    send_out, slope = pl.pallas_call(
-        functools.partial(expert_kernel, slots, held, sources, True),
-        grid=(held,),
-        out_shape=(slab, jax.ShapeDtypeStruct((held, per_expert, FF), F32)),
-        in_specs=[whole((stacked, half)), weights, weights],
-        out_specs=(whole((stacked, half)), by_expert((per_expert, FF))),
-        scratch_shapes=[
-            pltpu.VMEM((held, per_expert, width), BF16),
-            pltpu.VMEM((held * per_expert, width), F32),
-        ],
+    all_x = from_peers(rows_x, first_x)
+    send_in, dhid = pl.pallas_call(
+        functools.partial(backward_kernel, slots, held, sources),
+        out_shape=(slab, units_shape),
+        in_specs=[vmem, hbm, hbm, hbm],
+        out_specs=(vmem, hbm),
+        scratch_shapes=[experts, experts, units, units, sems((4, held))],
         compiler_params=params(),
-        cost_estimate=cost(2 * product, 2 * weight_bytes),
-        name="expert_forward",
-    )(got_x, weight_in, weight_out)
-    got_out = exchange(send_out)
-    all_d = from_peers(got_d)
-    send_in = pl.pallas_call(
-        functools.partial(expert_kernel, slots, held, sources, False),
-        grid=(held,),
-        out_shape=slab,
-        in_specs=[whole((stacked, half)), by_expert((per_expert, FF)), weights, weights],
-        out_specs=whole((stacked, half)),
-        scratch_shapes=[
-            pltpu.VMEM((held, per_expert, width), BF16),
-            pltpu.VMEM((held * per_expert, width), F32),
-        ],
+        cost_estimate=cost(4 * product, 4 * weight_in.size),
+        name="expert_backward",
+    )(rows_d, slope, wout, win)
+    send_in, *all_x = lax.optimization_barrier((send_in, *all_x))
+    first_d, rows_d, dhid = lax.optimization_barrier((first_d, rows_d, dhid))
+    got_in = exchange(send_in)
+    all_d = from_peers(rows_d, first_d)
+
+    share = width // groups
+    index = lax.axis_index("dp").astype(jnp.int32).reshape(1)
+    gradient = jax.ShapeDtypeStruct((share, held * FF), F32)
+    parts = 2
+    some = FF // parts
+    gradient_spec = pl.BlockSpec((share, some), lambda k, f, index: (0, k * parts + f))
+    cut = pl.BlockSpec((1, per_expert, share), lambda k, f, index: (k, 0, index[0]))
+    full = pl.BlockSpec((1, per_expert, width), lambda k, f, index: (k, 0, 0))
+    own = pl.BlockSpec((1, per_expert, some), lambda k, f, index: (k, 0, f))
+    weights = pl.BlockSpec((1, some, width), lambda k, f, index: (k, f, 0))
+    weight_in_grad, weight_out_grad = pl.pallas_call(
+        functools.partial(gradient_kernel, peers, factor),
+        out_shape=(gradient, gradient),
+        grid_spec=pltpu.PrefetchScalarGridSpec(
+            num_scalar_prefetch=1,
+            grid=(held, parts),
+            in_specs=[cut, cut, own, own, weights, weights] + [full] * (2 * peers),
+            out_specs=(gradient_spec, gradient_spec),
+        ),
         compiler_params=params(),
-        cost_estimate=cost(2 * product, 2 * weight_bytes),
-        name="expert_backward",
-    )(got_d, slope, weight_out, weight_in)
-    got_in = exchange(send_in)
-
-    share = width // groups
-    column = (lax.axis_index("dp") * share).astype(jnp.int32).reshape(1)
-    scalar = pl.BlockSpec(memory_space=pltpu.SMEM)
-    group_rows_count = groups * per_expert
-    act, slope_all, own_x = pl.pallas_call(
-        functools.partial(hidden_kernel, slots, held, sources, groups),
-        grid=(held,),
-        out_shape=(
-            jax.ShapeDtypeStruct((held, group_rows_count, FF), BF16),
-            jax.ShapeDtypeStruct((held, group_rows_count, FF), BF16),
-            jax.ShapeDtypeStruct((held, group_rows_count, share), BF16),
-        ),
-        in_specs=[whole((stacked, half))] * groups + [scalar, weights],
-        out_specs=(
-            by_expert((group_rows_count, FF)),
-            by_expert((group_rows_count, FF)),
-            by_expert((group_rows_count, share)),
-        ),
-        scratch_shapes=[pltpu.VMEM((held, group_rows_count, width), BF16)],
-        compiler_params=params(),
-        cost_estimate=cost(groups * product, 2 * weight_bytes),
-        name="hidden_all",
-    )(*all_x, column, weight_in)
-    gradient = jax.ShapeDtypeStruct((share, held * FF), F32)
-    gradient_spec = pl.BlockSpec((share, FF), lambda k: (0, k))
-    weight_in_grad, weight_out_grad = pl.pallas_call(
-        functools.partial(gradient_kernel, slots, held, sources, groups, factor),
-        grid=(held,),
-        out_shape=(gradient, gradient),
-        in_specs=[whole((stacked, half))] * groups
-        + [
-            scalar,
-            weights,
-            by_expert((group_rows_count, FF)),
-            by_expert((group_rows_count, FF)),
-            by_expert((group_rows_count, share)),
-        ],
-        out_specs=(gradient_spec, gradient_spec),
-        scratch_shapes=[pltpu.VMEM((held, group_rows_count, width), BF16)],
-        compiler_params=params(),
-        cost_estimate=cost((groups + 2) * product, 4 * weight_bytes),
+        cost_estimate=cost(12 * product, 8 * weight_in.size),
         name="gradients",
-    )(*all_d, column, weight_out, act, slope_all, own_x)
-
-    layer_out, gate_grad = pl.pallas_call(
+    )(index, rows_x, rows_d, act, dhid, win, wout, *all_x[1:], *all_d[1:])
+
+    layer_out, gate_grad = vmem_call(
         functools.partial(output_kernel, slots),
-        out_shape=(
-            jax.ShapeDtypeStruct((count, width), BF16),
-            jax.ShapeDtypeStruct((2, count), F32),
-        ),
-        in_specs=[vmem] * 4,
-        out_specs=(vmem, vmem),
-        compiler_params=params(),
-        name="combine_output",
-    )(target, gate_rows, cotangent, got_out)
-    input_grad = pl.pallas_call(
+        (jax.ShapeDtypeStruct((count, width), BF16), jax.ShapeDtypeStruct((2, count), F32)),
+        [target, gate_rows, cotangent, got_out],
+        "combine_output",
+    )
+    got_in, weight_in_grad = lax.optimization_barrier((got_in, weight_in_grad))
+    input_grad = vmem_call(
         functools.partial(input_kernel, slots),
-        out_shape=jax.ShapeDtypeStruct((count, width), BF16),
-        in_specs=[vmem] * 2,
-        out_specs=vmem,
-        compiler_params=params(),
-        name="combine_input",
-    )(target, got_in)
+        jax.ShapeDtypeStruct((count, width), BF16),
+        [target, got_in],
+        "combine_input",
+    )
     return layer_out, gate_grad.T, input_grad, weight_in_grad, weight_out_grad
 
 

time: 114 us -> 91 us (0.80)
  waiting for transfers between devices: 20.6 us -> 5.59 us
  Pallas kernels: 50.4 us -> 42.3 us
  starting transfers between devices: 14.5 us -> 17.1 us
  local copies, waits for them, and re-layouts: 3.26 us -> 0.86 us
    ppermute x6, waiting for transfers between devices: 12.8 us -> 2.55 us  [across(): return lax.ppermute(rows, 'dp', [(i, i ^ bit) for i in range(groups)])]
    pallas_call x6 -> x7, Pallas kernels: 48.6 us -> 39.4 us  [the longest x1 15.6 us: local_rows(): pl.pallas_call(functools.partial(gradient_kernel, peers, factor), out_sha...]
    all_to_all x3, waiting for transfers between devices: 7.81 us -> 3.05 us  [exchange(): lax.all_to_all(cut, 'seq', split_axis=0, concat_axis=0, tiled=True)]
    unnamed x12 -> x18, local copies, waits for them, and re-layouts: 3.26 us -> 0.86 us
    all_to_all x3, starting transfers between devices: 10.9 us -> 12.9 us  [exchange(): lax.all_to_all(cut, 'seq', split_axis=0, concat_axis=0, tiled=True)]
    pallas_call x1, Pallas kernels: 1.74 us -> 2.91 us  [local_rows(): pl.pallas_call(functools.partial(dispatch_kernel, slots), out_shape=(slab...]
  transfers between devices with their start and end apart: 9 -> 9, of which waited for: 3 -> 2; matrix products, arithmetic and copies ran while one was open for 0% -> 0% of each run, Pallas kernels for 32% -> 42%
where the time goes in v2:
time: 91 us; the launch traced here: 90.5 us
  Pallas kernels  42.3 us (46%)
  blocking collectives  23.8 us (26%)
  starting transfers between devices  17.1 us (19%)
  waiting for transfers between devices  5.59 us (6%)
    all_to_all x1, blocking collectives, exchange(): lax.all_to_all(cut, 'seq', split_axis=0, concat_axis=0, tiled=True)  23.8 us
    pallas_call x1, Pallas kernels, local_rows(): pl.pallas_call(functools.partial(gradient_kernel, peers, factor), out_sha...  15.6 us
    all_to_all x3, starting transfers between devices, exchange(): lax.all_to_all(cut, 'seq', split_axis=0, concat_axis=0, tiled=True)  12.9 us
    pallas_call x1, Pallas kernels, local_rows(): pl.pallas_call(functools.partial(backward_kernel, slots, held, sources),...  9.94 us
    pallas_call x1, Pallas kernels, local_rows(): pl.pallas_call(functools.partial(forward_kernel, slots, held, sources), o...  9.87 us
    ppermute x6, starting transfers between devices, across(): return lax.ppermute(rows, 'dp', [(i, i ^ bit) for i in range(groups)])  4.19 us
    pallas_call x4, Pallas kernels, vmem_call(): pl.pallas_call(kernel, out_shape=outs, in_specs=[vmem] * len(args), out_s...  4.01 us
    all_to_all x3, waiting for transfers between devices, exchange(): lax.all_to_all(cut, 'seq', split_axis=0, concat_axis=0, tiled=True)  3.05 us
  transfers between devices with their start and end apart: 9, of which 2 were waited for; matrix products, arithmetic and copies ran while one was open for 0% of the time, Pallas kernels for 42%

profile of v2, /device:TPU:0, one launch (start us, length us, event | category | flops | bytes accessed | tf_op | source)
XLA Modules:
  0.0 90.5 jit_solution(5656805117689313004)
XLA Ops:
  0.6 2.9 %dispatch.1 = (bf16[576,512]{1,0:T(8,128)(2,1)}, bf16[576,512]{1,0:T(8,128)(2,1)}, s32[2,128]{1,0:T(2,128)}) custom-call(s32[2,128]{1,0:T(2,128)} %bitcast.30, f32[2,128]{1,0:T(2,128)} %bitcast.18, bf16[128,1024]{1,0:T(8,128)(2,1)} %tok_hbm.1, bf16[128,1024]{1,0:T(8,128)(2,1)} %cot_ref.1), custom_call_target="tpu_custom_call" | custom-call | tf_op jit(solution)/shard_map/dispatch/pallas_call | solution.py:323
  3.6 23.8 %all_to_all.20 = bf16[8,72,512]{2,1,0:T(8,128)(2,1)S(1)} all-to-all(bf16[8,72,512]{2,1,0:T(8,128)(2,1)} %bitcast.29), channel_id=1, replica_groups=mesh['dp'=4,'seq'=8] {'seq'}, dimensions={0} | all-to-all | bytes 1179648 | tf_op jit(solution)/shard_map/all_to_all | solution.py:343
  27.4 3.5 %all-to-all-start.2 = ((bf16[8,72,512]{2,1,0:T(8,128)(2,1)}), bf16[8,72,512]{2,1,0:T(8,128)(2,1)S(1)}, u32[]{:S(2)}, u32[]{:S(2)}) async-start(bf16[8,72,512]{2,1,0:T(8,128)(2,1)} %bitcast.28), calls=%async_computation.2 | async-start | bytes 1179648 | tf_op jit(solution)/shard_map/all_to_all | solution.py:343
  30.9 0.6 regroup.2.rows_ref.refs_0_
  31.6 0.0 copy-start.1
  31.6 1.6 %collective-permute-start = (bf16[4,72,1024]{2,1,0:T(8,128)(2,1)S(1)}, bf16[4,72,1024]{2,1,0:T(8,128)(2,1)S(1)}, u32[]{:S(2)}, u32[]{:S(2)}) collective-permute-start(bf16[4,72,1024]{2,1,0:T(8,128)(2,1)S(1)} %regroup.2.rows_ref.refs_0_), channel_id=1, source_target_pairs={{0,16},{8,24},{16,0},{24,8},{1,17},{9,25},{17,1},{25,9},{2,18},{10... | collective-permute-start | bytes 1769480 | tf_op jit(solution)/shard_map/ppermute | solution.py:355
  33.2 0.0 copy-done.1
  33.2 9.9 %expert_forward.1 = (bf16[576,512]{1,0:T(8,128)(2,1)}, bf16[4,72,1024]{2,1,0:T(8,128)(2,1)}, bf16[4,72,1024]{2,1,0:T(8,128)(2,1)}) custom-call(bf16[4,72,1024]{2,1,0:T(8,128)(2,1)} %copy-done.1, bf16[4,1024,1024]{2,1,0:T(8,128)(2,1)} %bitcast.20, bf16[4,1024,1024]{2,1,0:T(8,128)(2,1)} %bitcast.23), custom_call_target="tpu_custom_call" | custom-call | flops 2415919104 | bytes 16777216 | tf_op jit(solution)/shard_map/expert_forward/pallas_call | solution.py:366
  43.1 3.0 %all-to-all-done.2 = bf16[8,72,512]{2,1,0:T(8,128)(2,1)S(1)} async-done(((bf16[8,72,512]{2,1,0:T(8,128)(2,1)}), bf16[8,72,512]{2,1,0:T(8,128)(2,1)S(1)}, u32[]{:S(2)}, u32[]{:S(2)}) %all-to-all-start.2) | async-done | bytes 589856 | tf_op jit(solution)/shard_map/all_to_all | solution.py:343
  46.1 3.6 %all-to-all-start.1 = ((bf16[8,72,512]{2,1,0:T(8,128)(2,1)}), bf16[8,72,512]{2,1,0:T(8,128)(2,1)S(1)}, u32[]{:S(2)}, u32[]{:S(2)}) async-start(bf16[8,72,512]{2,1,0:T(8,128)(2,1)} %bitcast.27), calls=%async_computation.1 | async-start | bytes 1179648 | tf_op jit(solution)/shard_map/all_to_all | solution.py:343
  49.7 0.0 collective-permute-done.refs_6_
  49.7 0.0 copy-start.5
  49.8 0.6 regroup.3.rows_ref.refs_1_
  50.4 0.0 copy-start.2
  50.4 1.6 %collective-permute-start.3 = (bf16[4,72,1024]{2,1,0:T(8,128)(2,1)S(1)}, bf16[4,72,1024]{2,1,0:T(8,128)(2,1)S(1)}, u32[]{:S(2)}, u32[]{:S(2)}) collective-permute-start(bf16[4,72,1024]{2,1,0:T(8,128)(2,1)S(1)} %regroup.3.rows_ref.refs_1_), channel_id=1, source_target_pairs={{0,16},{8,24},{16,0},{24,8},{1,17},{9,25},{17,1},{25,9},{2,18},{10... | collective-permute-start | bytes 1769480 | tf_op jit(solution)/shard_map/ppermute | solution.py:355
  52.0 0.0 collective-permute-start.1
  52.0 0.5 collective-permute-start.2
  52.5 0.0 copy-done.2
  52.5 0.0 copy-start
  52.5 0.0 copy-start.3
  52.5 0.0 copy-start.4
  52.5 9.9 %expert_backward.1 = (bf16[576,512]{1,0:T(8,128)(2,1)}, bf16[4,72,1024]{2,1,0:T(8,128)(2,1)}) custom-call(bf16[4,72,1024]{2,1,0:T(8,128)(2,1)} %copy-done.2, bf16[4,72,1024]{2,1,0:T(8,128)(2,1)} %get-tuple-element.35.slope_hbm, bf16[4,1024,1024]{2,1,0:T(8,128)(2,1)} %bitcast.24, bf16[4,1024,1024]{2,1,0:T(8,128)(2,1)} %bitcast.21), custom_call_target="tpu_custom_call" | custom-call | flops 2415919104 | bytes 16777216 | tf_op jit(solution)/shard_map/expert_backward/pallas_call | solution.py:389
  62.5 0.0 copy-done.5
  62.5 2.5 %collective-permute-done.3.refs_9_ = bf16[4,72,1024]{2,1,0:T(8,128)(2,1)S(1)} collective-permute-done((bf16[4,72,1024]{2,1,0:T(8,128)(2,1)S(1)}, bf16[4,72,1024]{2,1,0:T(8,128)(2,1)S(1)}, u32[]{:S(2)}, u32[]{:S(2)}) %collective-permute-start.3) | collective-permute-done | bytes 589856 | tf_op jit(solution)/shard_map/ppermute | solution.py:355
  65.0 0.0 copy-start.6
  65.0 0.0 collective-permute-start.4
  65.0 0.5 collective-permute-start.5
  65.5 0.0 collective-permute-done.1.refs_7_
  65.5 0.0 copy-start.7
  65.5 0.0 collective-permute-done.2.refs_8_
  65.5 0.0 copy-start.8
  65.5 0.0 all-to-all-done.1
  65.6 0.8 copy-done.8
  66.4 5.7 %all-to-all-start.3 = ((bf16[8,72,512]{2,1,0:T(8,128)(2,1)}), bf16[8,72,512]{2,1,0:T(8,128)(2,1)S(1)}, u32[]{:S(2)}, u32[]{:S(2)}) async-start(bf16[8,72,512]{2,1,0:T(8,128)(2,1)} %bitcast.26), calls=%async_computation.3 | async-start | bytes 1179648 | tf_op jit(solution)/shard_map/all_to_all | solution.py:343
  72.1 0.0 copy-done
  72.1 0.0 copy-done.3
  72.1 0.0 copy-done.4
  72.1 1.5 %combine_output.1 = (bf16[128,1024]{1,0:T(8,128)(2,1)}, f32[2,128]{1,0:T(2,128)}) custom-call(s32[2,128]{1,0:T(2,128)S(1)} %copy-done.4, f32[2,128]{1,0:T(2,128)S(1)} %bitcast.19, bf16[128,1024]{1,0:T(8,128)(2,1)S(1)} %copy-done, bf16[576,512]{1,0:T(8,128)(2,1)S(1)} %bitcast.14), custom_call_target="tpu_custom_call" | custom-call | tf_op jit(solution)/shard_map/combine_output/pallas_call | solution.py:291
  73.6 0.0 collective-permute-done.4.refs_10_
  73.6 0.0 collective-permute-done.5.refs_11_
  73.6 0.0 copy-done.6
  73.6 0.0 copy-done.7
  73.6 15.6 %gradients.1 = (f32[256,4096]{1,0:T(8,128)}, f32[256,4096]{1,0:T(8,128)}) custom-call(s32[1]{0:T(128)} %bitcast.13.share_ref, bf16[4,72,1024]{2,1,0:T(8,128)(2,1)} %copy-done.1, bf16[4,72,1024]{2,1,0:T(8,128)(2,1)} %copy-done.2, bf16[4,72,1024]{2,1,0:T(8,128)(2,1)} %get-tuple-element.41.refs_2_, bf16[4,72,1024]{2,1,0:T(8,128)(2,1)} %get-tuple-element.42.refs_3_, ...), custom_call_target="tpu_custom_call" | custom-call | flops 7247757312 | bytes 33554432 | tf_op jit(solution)/shard_map/gradients/pallas_call | solution.py:414
  89.2 0.0 all-to-all-done.3
  89.2 1.3 %combine_input.1 = bf16[128,1024]{1,0:T(8,128)(2,1)} custom-call(s32[2,128]{1,0:T(2,128)S(1)} %copy-done.4, bf16[576,512]{1,0:T(8,128)(2,1)S(1)} %bitcast.15), custom_call_target="tpu_custom_call" | custom-call | tf_op jit(solution)/shard_map/combine_input/pallas_call | solution.py:291
Async XLA Ops:
  27.4 18.7 %all-to-all-start.2 = ((bf16[8,72,512]{2,1,0:T(8,128)(2,1)}), bf16[8,72,512]{2,1,0:T(8,128)(2,1)S(1)}, u32[]{:S(2)}, u32[]{:S(2)}) async-start(bf16[8,72,512]{2,1,0:T(8,128)(2,1)} %bitcast.28), calls=%async_computation.2 | async-start | bytes 1179648 | tf_op jit(solution)/shard_map/all_to_all | solution.py:343
  31.6 1.6 %copy-start.1 = (bf16[4,72,1024]{2,1,0:T(8,128)(2,1)}, bf16[4,72,1024]{2,1,0:T(8,128)(2,1)S(1)}, u32[]{:S(2)}) copy-start(bf16[4,72,1024]{2,1,0:T(8,128)(2,1)S(1)} %regroup.2.rows_ref.refs_0_) | copy-start | bytes 1769476
  31.6 18.2 %collective-permute-start = (bf16[4,72,1024]{2,1,0:T(8,128)(2,1)S(1)}, bf16[4,72,1024]{2,1,0:T(8,128)(2,1)S(1)}, u32[]{:S(2)}, u32[]{:S(2)}) collective-permute-start(bf16[4,72,1024]{2,1,0:T(8,128)(2,1)S(1)} %regroup.2.rows_ref.refs_0_), channel_id=1, source_target_pairs={{0,16},{8,24},{16,0},{24,8},{1,17},{9,25},{17,1},{25,9},{2,18},{10... | collective-permute-start | bytes 1769480 | tf_op jit(solution)/shard_map/ppermute | solution.py:355
  46.1 19.4 %all-to-all-start.1 = ((bf16[8,72,512]{2,1,0:T(8,128)(2,1)}), bf16[8,72,512]{2,1,0:T(8,128)(2,1)S(1)}, u32[]{:S(2)}, u32[]{:S(2)}) async-start(bf16[8,72,512]{2,1,0:T(8,128)(2,1)} %bitcast.27), calls=%async_computation.1 | async-start | bytes 1179648 | tf_op jit(solution)/shard_map/all_to_all | solution.py:343
  49.7 12.7 %copy-start.5 = (bf16[4,72,1024]{2,1,0:T(8,128)(2,1)}, bf16[4,72,1024]{2,1,0:T(8,128)(2,1)S(1)}, u32[]{:S(2)}) copy-start(bf16[4,72,1024]{2,1,0:T(8,128)(2,1)S(1)} %collective-permute-done.refs_6_) | copy-start | bytes 1769476
  50.4 2.1 %copy-start.2 = (bf16[4,72,1024]{2,1,0:T(8,128)(2,1)}, bf16[4,72,1024]{2,1,0:T(8,128)(2,1)S(1)}, u32[]{:S(2)}) copy-start(bf16[4,72,1024]{2,1,0:T(8,128)(2,1)S(1)} %regroup.3.rows_ref.refs_1_) | copy-start | bytes 1769476
  50.4 14.6 %collective-permute-start.3 = (bf16[4,72,1024]{2,1,0:T(8,128)(2,1)S(1)}, bf16[4,72,1024]{2,1,0:T(8,128)(2,1)S(1)}, u32[]{:S(2)}, u32[]{:S(2)}) collective-permute-start(bf16[4,72,1024]{2,1,0:T(8,128)(2,1)S(1)} %regroup.3.rows_ref.refs_1_), channel_id=1, source_target_pairs={{0,16},{8,24},{16,0},{24,8},{1,17},{9,25},{17,1},{25,9},{2,18},{10... | collective-permute-start | bytes 1769480 | tf_op jit(solution)/shard_map/ppermute | solution.py:355
  52.0 13.5 %collective-permute-start.1 = (bf16[4,72,1024]{2,1,0:T(8,128)(2,1)}, bf16[4,72,1024]{2,1,0:T(8,128)(2,1)S(1)}, u32[]{:S(2)}, u32[]{:S(2)}) collective-permute-start(bf16[4,72,1024]{2,1,0:T(8,128)(2,1)} %copy-done.1), channel_id=1, source_target_pairs={{0,8},{8,0},{16,24},{24,16},{1,9},{9,1},{17,25},{25,17},{2,10},{10... | collective-permute-start | bytes 1769480 | tf_op jit(solution)/shard_map/ppermute | solution.py:355
  52.0 13.5 %collective-permute-start.2 = (bf16[4,72,1024]{2,1,0:T(8,128)(2,1)S(1)}, bf16[4,72,1024]{2,1,0:T(8,128)(2,1)S(1)}, u32[]{:S(2)}, u32[]{:S(2)}) collective-permute-start(bf16[4,72,1024]{2,1,0:T(8,128)(2,1)S(1)} %collective-permute-done.refs_6_), channel_id=1, source_target_pairs={{0,8},{8,0},{16,24},{24,16},{1,9},{9,1},{17,25},{25,17},{2,10},{10... | collective-permute-start | bytes 1769480 | tf_op jit(solution)/shard_map/ppermute | solution.py:355
  52.5 19.6 %copy-start = (bf16[128,1024]{1,0:T(8,128)(2,1)S(1)}, bf16[128,1024]{1,0:T(8,128)(2,1)}, u32[]{:S(2)}) copy-start(bf16[128,1024]{1,0:T(8,128)(2,1)} %cot_ref.1) | copy-start | bytes 786436
  52.5 19.6 %copy-start.3 = (f32[128,2]{0,1:T(2,128)S(1)}, f32[128,2]{0,1:T(2,128)}, u32[]{:S(2)}) copy-start(f32[128,2]{0,1:T(2,128)} %param.7) | copy-start | bytes 3076
  52.5 19.6 %copy-start.4 = (s32[2,128]{1,0:T(2,128)S(1)}, s32[2,128]{1,0:T(2,128)}, u32[]{:S(2)}) copy-start(s32[2,128]{1,0:T(2,128)} %get-tuple-element.28.target_ref) | copy-start | bytes 3076
  65.0 8.6 %copy-start.6 = (bf16[4,72,1024]{2,1,0:T(8,128)(2,1)}, bf16[4,72,1024]{2,1,0:T(8,128)(2,1)S(1)}, u32[]{:S(2)}) copy-start(bf16[4,72,1024]{2,1,0:T(8,128)(2,1)S(1)} %collective-permute-done.3.refs_9_) | copy-start | bytes 1769476
  65.0 8.6 %collective-permute-start.4 = (bf16[4,72,1024]{2,1,0:T(8,128)(2,1)}, bf16[4,72,1024]{2,1,0:T(8,128)(2,1)}, u32[]{:S(2)}, u32[]{:S(2)}) collective-permute-start(bf16[4,72,1024]{2,1,0:T(8,128)(2,1)} %copy-done.2), channel_id=1, source_target_pairs={{0,8},{8,0},{16,24},{24,16},{1,9},{9,1},{17,25},{25,17},{2,10},{10... | collective-permute-start | bytes 1769480 | tf_op jit(solution)/shard_map/ppermute | solution.py:355
  65.0 8.6 %collective-permute-start.5 = (bf16[4,72,1024]{2,1,0:T(8,128)(2,1)S(1)}, bf16[4,72,1024]{2,1,0:T(8,128)(2,1)}, u32[]{:S(2)}, u32[]{:S(2)}) collective-permute-start(bf16[4,72,1024]{2,1,0:T(8,128)(2,1)S(1)} %collective-permute-done.3.refs_9_), channel_id=1, source_target_pairs={{0,8},{8,0},{16,24},{24,16},{1,9},{9,1},{17,25},{25,17},{2,10},{10... | collective-permute-start | bytes 1769480 | tf_op jit(solution)/shard_map/ppermute | solution.py:355
  65.5 8.1 %copy-start.7 = (bf16[4,72,1024]{2,1,0:T(8,128)(2,1)}, bf16[4,72,1024]{2,1,0:T(8,128)(2,1)S(1)}, u32[]{:S(2)}) copy-start(bf16[4,72,1024]{2,1,0:T(8,128)(2,1)S(1)} %collective-permute-done.1.refs_7_) | copy-start | bytes 1769476
  65.5 0.8 copy-start.8
  66.4 22.8 %all-to-all-start.3 = ((bf16[8,72,512]{2,1,0:T(8,128)(2,1)}), bf16[8,72,512]{2,1,0:T(8,128)(2,1)S(1)}, u32[]{:S(2)}, u32[]{:S(2)}) async-start(bf16[8,72,512]{2,1,0:T(8,128)(2,1)} %bitcast.26), calls=%async_computation.3 | async-start | bytes 1179648 | tf_op jit(solution)/shard_map/all_to_all | solution.py:343

commit v3 on v2

--- a/solution.py
+++ b/solution.py
@@ -61,30 +61,30 @@
 def slab_slot(numbers, slots):
     slab = quotient(numbers, 2 * slots)
     rest = numbers - slab * (2 * slots)
-    right = (rest >= slots).astype(jnp.int32)
-    return slab * slots + rest - right * slots, right
-
-
-def dispatch_kernel(
-    slots, ids_hbm, gate_hbm, tok_hbm, cot_hbm, x_ref, d_ref, target_ref, ids_ref, gate_ref, tok_ref, cot_ref, sems
-):
-    copies = [
-        pltpu.make_async_copy(source, here, sems.at[i])
-        for i, (source, here) in enumerate(
-            [(ids_hbm, ids_ref), (tok_hbm, tok_ref), (gate_hbm, gate_ref), (cot_hbm, cot_ref)]
-        )
-    ]
-    for copy in copies:
-        copy.start()
+    right = rest >= slots
+    return slab, jnp.where(right, rest - slots, rest), right
+
+
+def here(axis):
+    return lax.axis_index(axis).astype(jnp.int32)
+
+
+def token_kernel(slots, sources, ids_hbm, tok_hbm, *refs):
+    slab_refs, (target_ref, ids_ref, tok_ref, sems) = refs[:sources], refs[sources:]
+    ids_copy = pltpu.make_async_copy(ids_hbm, ids_ref, sems.at[0])
+    tok_copy = pltpu.make_async_copy(tok_hbm, tok_ref, sems.at[1])
+    ids_copy.start()
+    tok_copy.start()
     count = tok_ref.shape[0]
     half = tok_ref.shape[1] // 2
-    rows = x_ref.shape[0]
-    copies[0].wait()
+    expert = iota((E, count), 0)
+    earlier = ones_where(iota((count, count), 0) < iota((count, count), 1))
+    slab, slot, right = slab_slot(iota((sources * 2 * slots, 1), 0), slots)
+    slot = (slab ^ here("seq")) * slots + slot
+    ids_copy.wait()
     ids = ids_ref[...]
     first, second = ids[0:1, :], ids[1:2, :]
-    expert = iota((E, count), 0)
     hot_first, hot_second = expert == first, expert == second
-    earlier = ones_where(iota((count, count), 0) < iota((count, count), 1))
     before = dot(ones_where(hot_first | hot_second), earlier, ((1,), (0,)))
     slot_first = jnp.sum(jnp.where(hot_first, before, 0.0), axis=0, keepdims=True)
     slot_second = jnp.sum(jnp.where(hot_second, before, 0.0), axis=0, keepdims=True)
@@ -92,35 +92,43 @@
     target_second = second * CAP + slot_second.astype(jnp.int32)
     target_ref[0:1, :] = target_first
     target_ref[1:2, :] = target_second
-    slot, right = slab_slot(iota((rows, 1), 0), slots)
-    is_first, is_second = slot == target_first, slot == target_second
-    pick = ones_where(is_first | is_second)
-    is_right = right == 1
-    copies[1].wait()
-    rows_x = dot(pick, tok_ref[...], ((1,), (0,)))
-    x_ref[...] = jnp.where(is_right, rows_x[:, half:], rows_x[:, :half]).astype(BF16)
-    copies[2].wait()
-    gates = gate_ref[...]
+    pick = ones_where((slot == target_first) | (slot == target_second))
+    tok_copy.wait()
+    rows = dot(pick, tok_ref[...], ((1,), (0,)))
+    rows = jnp.where(right, rows[:, half:], rows[:, :half]).astype(BF16)
+    for j, slab_ref in enumerate(slab_refs):
+        slab_ref[...] = rows[j * 2 * slots : (j + 1) * 2 * slots]
+
+
+def cotangent_kernel(slots, target_ref, gate_ref, cot_hbm, slab_ref, cot_ref, sem):
+    copy = pltpu.make_async_copy(cot_hbm, cot_ref, sem)
+    copy.start()
+    half = cot_ref.shape[1] // 2
+    slab, slot, right = slab_slot(iota((slab_ref.shape[0], 1), 0), slots)
+    slot = slab * slots + slot
+    is_first, is_second = slot == target_ref[0:1, :], slot == target_ref[1:2, :]
     gate = jnp.sum(
-        jnp.where(is_first, gates[0:1, :], 0.0) + jnp.where(is_second, gates[1:2, :], 0.0),
+        jnp.where(is_first, gate_ref[0:1, :], 0.0) + jnp.where(is_second, gate_ref[1:2, :], 0.0),
         axis=1,
         keepdims=True,
     )
-    copies[3].wait()
-    rows_d = dot(pick, cot_ref[...], ((1,), (0,)))
-    d_ref[...] = (jnp.where(is_right, rows_d[:, half:], rows_d[:, :half]) * gate).astype(BF16)
-
-
-def regroup_kernel(slots, held, sources, slab_ref, rows_ref):
+    copy.wait()
+    rows = dot(ones_where(is_first | is_second), cot_ref[...], ((1,), (0,)))
+    slab_ref[...] = (jnp.where(right, rows[:, half:], rows[:, :half]) * gate).astype(BF16)
+
+
+def regroup_kernel(slots, held, sources, *refs):
+    slab_refs, rows_ref = refs[:-1], refs[-1]
     per_expert = sources * CAP
-    half = slab_ref.shape[1]
+    half = slab_refs[0].shape[1]
     number = iota((held * per_expert, 1), 0)
     expert = quotient(number, per_expert)
     rest = number - expert * per_expert
     source = quotient(rest, CAP)
-    row = source * (2 * slots) + expert * CAP + rest - source * CAP
+    slab = source ^ here("seq") if len(slab_refs) > 1 else source
+    row = slab * (2 * slots) + expert * CAP + rest - source * CAP
     at = iota((held * per_expert, 2 * slots * sources), 1)
-    slabs = slab_ref[...]
+    slabs = jnp.concatenate([ref[...] for ref in slab_refs], axis=0)
     for side in (0, 1):
         rows = dot(ones_where(at == row + side * slots), slabs, ((1,), (0,)))
         for k in range(held):
@@ -128,19 +136,15 @@
             rows_ref[k, :, side * half : (side + 1) * half] = rows[span].astype(BF16)
 
 
-def slab_rows(rows, slots, held, sources):
+def slab_rows(parts, slots, held, sources):
     per_expert = sources * CAP
+    rows = jnp.concatenate(parts, axis=0).astype(BF16)
     half = rows.shape[1] // 2
-    number = iota((2 * slots * sources, 1), 0)
-    source = quotient(number, 2 * slots)
-    rest = number - source * (2 * slots)
-    is_right = rest >= slots
-    rest = jnp.where(is_right, rest - slots, rest)
-    expert = quotient(rest, CAP)
-    row = expert * per_expert + source * CAP + rest - expert * CAP
-    at = iota((2 * slots * sources, held * per_expert), 1)
-    out = dot(ones_where(at == row), rows, ((1,), (0,)))
-    return jnp.where(is_right, out[:, half:], out[:, :half])
+    source, slot, right = slab_slot(iota((2 * slots * sources, 1), 0), slots)
+    expert = quotient(slot, CAP)
+    row = expert * per_expert + source * CAP + slot - expert * CAP
+    out = dot(ones_where(iota((2 * slots * sources, held * per_expert), 1) == row), rows, ((1,), (0,)))
+    return jnp.where(right, out[:, half:], out[:, :half]).astype(BF16)
 
 
 def weight_copies(up_hbm, down_hbm, up_ref, down_ref, sems):
@@ -174,8 +178,7 @@
         for i, (here, there) in enumerate([(act_ref, act_hbm), (slope_ref, slope_hbm)]):
             stores.append(pltpu.make_async_copy(here.at[k], there.at[k], sems.at[2 + i, k]))
             stores[-1].start()
-    rows = jnp.concatenate(parts, axis=0).astype(BF16)
-    out_ref[...] = slab_rows(rows, slots, held, sources).astype(BF16)
+    out_ref[...] = slab_rows(parts, slots, held, sources)
     for store in stores:
         store.wait()
 
@@ -205,8 +208,7 @@
         parts.append(dot(dhid, down_ref[k], ((1,), (0,))))
         stores.append(pltpu.make_async_copy(dhid_ref.at[k], dhid_hbm.at[k], sems.at[2, k]))
         stores[-1].start()
-    rows = jnp.concatenate(parts, axis=0).astype(BF16)
-    out_ref[...] = slab_rows(rows, slots, held, sources).astype(BF16)
+    out_ref[...] = slab_rows(parts, slots, held, sources)
     for store in stores:
         store.wait()
 
@@ -243,9 +245,10 @@
 
 
 def picked(target_ref, slots, rows):
-    slot, right = slab_slot(iota((1, rows), 1), slots)
+    slab, slot, right = slab_slot(iota((1, rows), 1), slots)
+    slot = slab * slots + slot
     columns = [as_column(target_ref[k : k + 1, :].astype(F32)).astype(jnp.int32) for k in (0, 1)]
-    return [[(slot == column) & (right == side) for side in (0, 1)] for column in columns]
+    return [[(slot == column) & ~right, (slot == column) & right] for column in columns]
 
 
 def output_kernel(slots, target_ref, gate_ref, cot_ref, back_ref, out_ref, gate_grad_ref):
@@ -313,28 +316,27 @@
     slab = jax.ShapeDtypeStruct((stacked, half), BF16)
     rows_shape = jax.ShapeDtypeStruct((held, per_expert, width), BF16)
     units_shape = jax.ShapeDtypeStruct((held, per_expert, FF), BF16)
+    peers_shape = jax.ShapeDtypeStruct((held, peers * per_expert, FF), BF16)
     product = 2 * held * per_expert * FF * width
     vmem = pl.BlockSpec(memory_space=pltpu.VMEM)
 
     hbm = pl.BlockSpec(memory_space=pltpu.HBM)
     sems = pltpu.SemaphoreType.DMA
 
+    def by_expert(shape):
+        return pl.BlockSpec((1, *shape), lambda k, *_: (k, 0, 0))
+
     ids_rows, gate_rows = expert_ids.T, gate_values.T
-    send_x, send_d, target = pl.pallas_call(
-        functools.partial(dispatch_kernel, slots),
-        out_shape=(slab, slab, jax.ShapeDtypeStruct((2, count), jnp.int32)),
-        in_specs=[hbm] * 4,
-        out_specs=(vmem,) * 3,
-        scratch_shapes=[
-            pltpu.VMEM((2, count), jnp.int32),
-            pltpu.VMEM((2, count), F32),
-            pltpu.VMEM((count, width), BF16),
-            pltpu.VMEM((count, width), BF16),
-            sems((4,)),
-        ],
+    piece = jax.ShapeDtypeStruct((2 * slots, half), BF16)
+    *pieces, target = pl.pallas_call(
+        functools.partial(token_kernel, slots, sources),
+        out_shape=(piece,) * sources + (jax.ShapeDtypeStruct((2, count), jnp.int32),),
+        in_specs=[hbm] * 2,
+        out_specs=(vmem,) * (sources + 1),
+        scratch_shapes=[pltpu.VMEM((2, count), jnp.int32), pltpu.VMEM((count, width), BF16), sems((2,))],
         compiler_params=params(),
-        name="dispatch",
-    )(ids_rows, gate_rows, tokens, cotangent)
+        name="dispatch_tokens",
+    )(ids_rows, tokens)
     win = weight_in.reshape(held, FF, width)
     wout = weight_out.reshape(held, FF, width)
 
@@ -342,24 +344,43 @@
         cut = stack.reshape(sources, 2 * slots, half)
         return lax.all_to_all(cut, "seq", split_axis=0, concat_axis=0, tiled=True).reshape(stacked, half)
 
-    def regroup(stack):
+    def regroup(*stacks):
         return vmem_call(
             functools.partial(regroup_kernel, slots, held, sources),
             rows_shape,
-            [stack],
+            stacks,
             "regroup",
             cost(product, 4 * stacked * half),
         )
 
-    def across(rows, bit):
-        return lax.ppermute(rows, "dp", [(i, i ^ bit) for i in range(groups)])
-
-    got_x = exchange(send_x)
+    def across(rows, axis, bit):
+        return lax.ppermute(rows, axis, [(i, i ^ bit) for i in range(lax.axis_size(axis))])
+
+    def from_peers(rows, first):
+        got, bit = [rows, first], far // 2
+        while bit:
+            got = got + [across(one, "dp", bit) for one in got]
+            bit = bit // 2
+        return got
+
+    far = groups // 2
+    arrived = [pieces[0]] + [across(pieces[j], "seq", j) for j in range(1, sources)]
+    send_d = pl.pallas_call(
+        functools.partial(cotangent_kernel, slots),
+        out_shape=slab,
+        in_specs=[vmem, vmem, hbm],
+        out_specs=vmem,
+        scratch_shapes=[pltpu.VMEM((count, width), BF16), sems],
+        compiler_params=params(),
+        name="dispatch_cotangents",
+    )(target, gate_rows, cotangent)
+    order = (7,6,5,4,3,2,1)
+    send_d, *moved = lax.optimization_barrier((send_d, *[arrived[j] for j in order]))
+    for j, one in zip(order, moved):
+        arrived[j] = one
     got_d = exchange(send_d)
-    rows_x = regroup(got_x)
-    peers_x = [rows_x]
-    far = groups // 2
-    first_x = across(rows_x, far)
+    rows_x = regroup(*arrived)
+    first_x = across(rows_x, "dp", far)
 
     units = pltpu.VMEM((held, per_expert, FF), BF16)
     experts = pltpu.VMEM((held, FF, width), BF16)
@@ -374,17 +395,9 @@
         name="expert_forward",
     )(rows_x, win, wout)
     got_out = exchange(send_out)
-    got_d, first_x = lax.optimization_barrier((got_d, first_x))
+    first_x, rows_x, act = lax.optimization_barrier((first_x, rows_x, act))
     rows_d = regroup(got_d)
-    first_d = across(rows_d, far)
-
-    def from_peers(rows, first):
-        got, bit = [rows, first], far // 2
-        while bit:
-            got = got + [across(one, bit) for one in got]
-            bit = bit // 2
-        return got
-
+    first_d = across(rows_d, "dp", far)
     all_x = from_peers(rows_x, first_x)
     send_in, dhid = pl.pallas_call(
         functools.partial(backward_kernel, slots, held, sources),
@@ -404,7 +417,7 @@
     share = width // groups
     index = lax.axis_index("dp").astype(jnp.int32).reshape(1)
     gradient = jax.ShapeDtypeStruct((share, held * FF), F32)
-    parts = 2
+    parts = 1
     some = FF // parts
     gradient_spec = pl.BlockSpec((share, some), lambda k, f, index: (0, k * parts + f))
     cut = pl.BlockSpec((1, per_expert, share), lambda k, f, index: (k, 0, index[0]))
@@ -554,11 +567,10 @@
 
 def local(tokens, gate_values, expert_ids, cotangent, weight_in, weight_out):
     units = weight_in.shape[0]
-    row_values = lax.axis_size("seq") * max(units // FF, 1) * CAP * lax.axis_size("dp")
-    if units % FF == 0 and row_values < units:
-        plan = local_rows
-    else:
-        plan = local_sums
+    sources, groups = lax.axis_size("seq"), lax.axis_size("dp")
+    row_values = sources * max(units // FF, 1) * CAP * groups
+    paired = sources & (sources - 1) == 0 and groups & (groups - 1) == 0 and groups > 1
+    plan = local_rows if units % FF == 0 and row_values < units and paired else local_sums
     return plan(tokens, gate_values, expert_ids, cotangent, weight_in, weight_out)
 
 

time: 91 us -> 83.6 us (0.919)
  blocking collectives: 23.8 us -> 0 us
  starting transfers between devices: 17.1 us -> 34.5 us
  waiting for transfers between devices: 5.59 us -> 3.57 us
    all_to_all x1 -> x0, blocking collectives: 23.8 us -> none  [exchange(): lax.all_to_all(cut, 'seq', split_axis=0, concat_axis=0, tiled=True)]
    ppermute x6 -> x13, starting transfers between devices: 4.19 us -> 17.8 us  [across(): lax.ppermute(rows, axis, [(i, i ^ bit) for i in range(lax.axis_size(axis))])]
    all_to_all x3, starting transfers between devices: 12.9 us -> 16.8 us  [exchange(): lax.all_to_all(cut, 'seq', split_axis=0, concat_axis=0, tiled=True)]
    pallas_call x1 -> x2, Pallas kernels: 2.91 us -> 5.05 us  [the longest x1 2.93 us: local_rows(): pl.pallas_call(functools.partial(cotangent_kernel, slots), out_shape=slab...]
    pallas_call x1, Pallas kernels: 15.6 us -> 13.6 us  [local_rows(): pl.pallas_call(functools.partial(gradient_kernel, peers, factor), out_sha...]
    all_to_all x3, waiting for transfers between devices: 3.05 us -> 1.52 us  [exchange(): lax.all_to_all(cut, 'seq', split_axis=0, concat_axis=0, tiled=True)]
    ppermute x6 -> x13, waiting for transfers between devices: 2.55 us -> 2.05 us  [across(): lax.ppermute(rows, axis, [(i, i ^ bit) for i in range(lax.axis_size(axis))])]
  transfers between devices with their start and end apart: 9 -> 16, of which waited for: 2 -> 6; matrix products, arithmetic and copies ran while one was open for 0% -> 0% of each run, Pallas kernels for 42% -> 47%
where the time goes in v3:
time: 83.6 us; the launch traced here: 83.1 us
  Pallas kernels  42.5 us (51%)
  starting transfers between devices  34.5 us (41%)
  waiting for transfers between devices  3.57 us (4%)
  local copies, waits for them, and re-layouts  1.73 us (2%)
    ppermute x13, starting transfers between devices, across(): lax.ppermute(rows, axis, [(i, i ^ bit) for i in range(lax.axis_size(axis))])  17.8 us
    all_to_all x3, starting transfers between devices, exchange(): lax.all_to_all(cut, 'seq', split_axis=0, concat_axis=0, tiled=True)  16.8 us
    pallas_call x1, Pallas kernels, local_rows(): pl.pallas_call(functools.partial(gradient_kernel, peers, factor), out_sha...  13.6 us
    pallas_call x1, Pallas kernels, local_rows(): pl.pallas_call(functools.partial(backward_kernel, slots, held, sources),...  9.92 us
    pallas_call x1, Pallas kernels, local_rows(): pl.pallas_call(functools.partial(forward_kernel, slots, held, sources), o...  9.88 us
    pallas_call x4, Pallas kernels, vmem_call(): pl.pallas_call(kernel, out_shape=outs, in_specs=[vmem] * len(args), out_s...  4.02 us
    pallas_call x1, Pallas kernels, local_rows(): pl.pallas_call(functools.partial(cotangent_kernel, slots), out_shape=slab...  2.93 us
    pallas_call x1, Pallas kernels, local_rows(): pl.pallas_call(functools.partial(token_kernel, slots, sources), out_shape...  2.12 us
  transfers between devices with their start and end apart: 16, of which 6 were waited for; matrix products, arithmetic and copies ran while one was open for 0% of the time, Pallas kernels for 47%

profile of v3, /device:TPU:0, one launch (start us, length us, event | category | flops | bytes accessed | tf_op | source)
XLA Modules:
  0.0 83.1 jit_solution(14895302294025395457)
XLA Ops:
  0.6 2.1 %dispatch_tokens.1 = (bf16[72,512]{1,0:T(8,128)(2,1)}, bf16[72,512]{1,0:T(8,128)(2,1)}, bf16[72,512]{1,0:T(8,128)(2,1)}, bf16[72,512]{1,0:T(8,128)(2,1)}, bf16[7...) custom-call(s32[2,128]{1,0:T(2,128)} %bitcast.26, ...), custom_call_target="tpu_custom_call" | custom-call | tf_op jit(solution)/shard_map/dispatch_tokens/pallas_call | solution.py:331
  2.8 6.0 %collective-permute-start = (bf16[72,512]{1,0:T(8,128)(2,1)}, bf16[72,512]{1,0:T(8,128)(2,1)S(1)}, u32[]{:S(2)}, u32[]{:S(2)}) collective-permute-start(bf16[72,512]{1,0:T(8,128)(2,1)} %get-tuple-element.45), channel_id=1, source_target_pairs={{0,7},{1,6},{2,5},{3,4},{4,3},{5,2},{6,1},{7,0},{8,15},{9,14},{10,... | collective-permute-start | bytes 221192 | tf_op jit(solution)/shard_map/ppermute | solution.py:357
  8.8 0.2 collective-permute-start.1
  9.0 0.8 collective-permute-start.2
  9.8 2.0 %collective-permute-start.3 = (bf16[72,512]{1,0:T(8,128)(2,1)}, bf16[72,512]{1,0:T(8,128)(2,1)S(1)}, u32[]{:S(2)}, u32[]{:S(2)}) collective-permute-start(bf16[72,512]{1,0:T(8,128)(2,1)} %get-tuple-element.48), channel_id=1, source_target_pairs={{0,4},{1,5},{2,6},{3,7},{4,0},{5,1},{6,2},{7,3},{8,12},{9,13},{10,... | collective-permute-start | bytes 221192 | tf_op jit(solution)/shard_map/ppermute | solution.py:357
  11.8 2.3 %collective-permute-start.4 = (bf16[72,512]{1,0:T(8,128)(2,1)}, bf16[72,512]{1,0:T(8,128)(2,1)S(1)}, u32[]{:S(2)}, u32[]{:S(2)}) collective-permute-start(bf16[72,512]{1,0:T(8,128)(2,1)} %get-tuple-element.49), channel_id=1, source_target_pairs={{0,3},{1,2},{2,1},{3,0},{4,7},{5,6},{6,5},{7,4},{8,11},{9,10},{10,... | collective-permute-start | bytes 221192 | tf_op jit(solution)/shard_map/ppermute | solution.py:357
  14.1 0.0 collective-permute-done.refs_7_
  14.1 2.6 %collective-permute-start.5 = (bf16[72,512]{1,0:T(8,128)(2,1)}, bf16[72,512]{1,0:T(8,128)(2,1)S(1)}, u32[]{:S(2)}, u32[]{:S(2)}) collective-permute-start(bf16[72,512]{1,0:T(8,128)(2,1)} %get-tuple-element.50), channel_id=1, source_target_pairs={{0,2},{1,3},{2,0},{3,1},{4,6},{5,7},{6,4},{7,5},{8,10},{9,11},{10,... | collective-permute-start | bytes 221192 | tf_op jit(solution)/shard_map/ppermute | solution.py:357
  16.7 0.0 collective-permute-done.1.refs_6_
  16.7 0.5 collective-permute-start.6
  17.2 2.9 %dispatch_cotangents.1 = bf16[576,512]{1,0:T(8,128)(2,1)} custom-call(s32[2,128]{1,0:T(2,128)} %get-tuple-element.43.target_ref, f32[2,128]{1,0:T(2,128)} %bitcast.15, bf16[128,1024]{1,0:T(8,128)(2,1)} %cot_ref.1), custom_call_target="tpu_custom_call" | custom-call | tf_op jit(solution)/shard_map/dispatch_cotangents/pallas_call | solution.py:368
  20.2 0.5 collective-permute-done.2.refs_5_
  20.7 0.9 %collective-permute-done.3.refs_4_ = bf16[72,512]{1,0:T(8,128)(2,1)S(1)} collective-permute-done((bf16[72,512]{1,0:T(8,128)(2,1)}, bf16[72,512]{1,0:T(8,128)(2,1)S(1)}, u32[]{:S(2)}, u32[]{:S(2)}) %collective-permute-start.3) | collective-permute-done | bytes 73760 | tf_op jit(solution)/shard_map/ppermute | solution.py:357
  21.6 0.0 collective-permute-done.4.refs_3_
  21.6 0.2 collective-permute-done.5.refs_2_
  21.8 0.0 collective-permute-done.6.refs_1_
  21.8 5.5 %all-to-all-start.1 = ((bf16[8,72,512]{2,1,0:T(8,128)(2,1)}), bf16[8,72,512]{2,1,0:T(8,128)(2,1)S(1)}, u32[]{:S(2)}, u32[]{:S(2)}) async-start(bf16[8,72,512]{2,1,0:T(8,128)(2,1)} %bitcast.23), calls=%async_computation.1 | async-start | bytes 1179648 | tf_op jit(solution)/shard_map/all_to_all | solution.py:345
  27.3 0.9 %copy-done.5 = bf16[72,512]{1,0:T(8,128)(2,1)S(1)} copy-done((bf16[72,512]{1,0:T(8,128)(2,1)S(1)}, bf16[72,512]{1,0:T(8,128)(2,1)}, u32[]{:S(2)}) %copy-start.5) | copy-done | bytes 73752
  28.2 0.6 regroup.2.rows_ref.refs_0_
  28.9 0.0 copy-start.1
  28.9 1.5 %collective-permute-start.7 = (bf16[4,72,1024]{2,1,0:T(8,128)(2,1)S(1)}, bf16[4,72,1024]{2,1,0:T(8,128)(2,1)S(1)}, u32[]{:S(2)}, u32[]{:S(2)}) collective-permute-start(bf16[4,72,1024]{2,1,0:T(8,128)(2,1)S(1)} %regroup.2.rows_ref.refs_0_), channel_id=1, source_target_pairs={{0,16},{8,24},{16,0},{24,8},{1,17},{9,25},{17,1},{25,9},{2,18},{10... | collective-permute-start | bytes 1769480 | tf_op jit(solution)/shard_map/ppermute | solution.py:357
  30.3 0.0 copy-done.1
  30.3 9.9 %expert_forward.1 = (bf16[576,512]{1,0:T(8,128)(2,1)}, bf16[4,72,1024]{2,1,0:T(8,128)(2,1)}, bf16[4,72,1024]{2,1,0:T(8,128)(2,1)}) custom-call(bf16[4,72,1024]{2,1,0:T(8,128)(2,1)} %copy-done.1, bf16[4,1024,1024]{2,1,0:T(8,128)(2,1)} %bitcast.17, bf16[4,1024,1024]{2,1,0:T(8,128)(2,1)} %bitcast.20), custom_call_target="tpu_custom_call" | custom-call | flops 2415919104 | bytes 16777216 | tf_op jit(solution)/shard_map/expert_forward/pallas_call | solution.py:387
  40.2 0.5 all-to-all-done.1
  40.7 5.5 %all-to-all-start = ((bf16[8,72,512]{2,1,0:T(8,128)(2,1)}), bf16[8,72,512]{2,1,0:T(8,128)(2,1)S(1)}, u32[]{:S(2)}, u32[]{:S(2)}) async-start(bf16[8,72,512]{2,1,0:T(8,128)(2,1)} %bitcast.25), calls=%async_computation | async-start | bytes 1179648 | tf_op jit(solution)/shard_map/all_to_all | solution.py:345
  46.3 0.6 regroup.3.rows_ref.refs_1_
  46.9 0.8 collective-permute-start.10
  47.7 0.0 collective-permute-done.7.refs_6_
  47.7 0.0 collective-permute-start.9
  47.7 0.5 collective-permute-start.8
  48.3 0.0 copy-done.2
  48.3 9.9 %expert_backward.1 = (bf16[576,512]{1,0:T(8,128)(2,1)}, bf16[4,72,1024]{2,1,0:T(8,128)(2,1)}) custom-call(bf16[4,72,1024]{2,1,0:T(8,128)(2,1)} %copy-done.2, bf16[4,72,1024]{2,1,0:T(8,128)(2,1)} %get-tuple-element.63.slope_hbm, bf16[4,1024,1024]{2,1,0:T(8,128)(2,1)} %bitcast.21, bf16[4,1024,1024]{2,1,0:T(8,128)(2,1)} %bitcast.18), custom_call_target="tpu_custom_call" | custom-call | flops 2415919104 | bytes 16777216 | tf_op jit(solution)/shard_map/expert_backward/pallas_call | solution.py:402
  58.2 0.3 collective-permute-done.10.refs_9_
  58.6 0.0 collective-permute-start.11
  58.6 0.5 collective-permute-start.12
  59.1 0.0 collective-permute-done.9.refs_8_
  59.1 0.0 collective-permute-done.8.refs_7_
  59.1 0.0 all-to-all-done
  59.1 0.8 copy-done.9
  59.9 5.7 %all-to-all-start.2 = ((bf16[8,72,512]{2,1,0:T(8,128)(2,1)}), bf16[8,72,512]{2,1,0:T(8,128)(2,1)S(1)}, u32[]{:S(2)}, u32[]{:S(2)}) async-start(bf16[8,72,512]{2,1,0:T(8,128)(2,1)} %bitcast.24), calls=%async_computation.2 | async-start | bytes 1179648 | tf_op jit(solution)/shard_map/all_to_all | solution.py:345
  65.6 0.0 copy-done
  65.7 1.5 %combine_output.1 = (bf16[128,1024]{1,0:T(8,128)(2,1)}, f32[2,128]{1,0:T(2,128)}) custom-call(s32[2,128]{1,0:T(2,128)S(1)} %copy-done.3, f32[2,128]{1,0:T(2,128)S(1)} %bitcast.16, bf16[128,1024]{1,0:T(8,128)(2,1)S(1)} %copy-done, bf16[576,512]{1,0:T(8,128)(2,1)S(1)} %bitcast.12), custom_call_target="tpu_custom_call" | custom-call | tf_op jit(solution)/shard_map/combine_output/pallas_call | solution.py:294
  67.1 0.0 collective-permute-done.11.refs_10_
  67.1 0.0 collective-permute-done.12.refs_11_
  67.1 0.0 copy-done.8
  67.1 13.6 %gradients.1 = (f32[256,4096]{1,0:T(8,128)}, f32[256,4096]{1,0:T(8,128)}) custom-call(s32[1]{0:T(128)} %bitcast.11.share_ref, bf16[4,72,1024]{2,1,0:T(8,128)(2,1)} %copy-done.1, bf16[4,72,1024]{2,1,0:T(8,128)(2,1)} %copy-done.2, bf16[4,72,1024]{2,1,0:T(8,128)(2,1)} %get-tuple-element.71.refs_2_, bf16[4,72,1024]{2,1,0:T(8,128)(2,1)} %get-tuple-element.72.refs_3_, ...), custom_call_target="tpu_custom_call" | custom-call | flops 7247757312 | bytes 33554432 | tf_op jit(solution)/shard_map/gradients/pallas_call | solution.py:427
  80.7 1.0 %all-to-all-done.2 = bf16[8,72,512]{2,1,0:T(8,128)(2,1)S(1)} async-done(((bf16[8,72,512]{2,1,0:T(8,128)(2,1)}), bf16[8,72,512]{2,1,0:T(8,128)(2,1)S(1)}, u32[]{:S(2)}, u32[]{:S(2)}) %all-to-all-start.2) | async-done | bytes 589856 | tf_op jit(solution)/shard_map/all_to_all | solution.py:345
  81.8 1.3 %combine_input.1 = bf16[128,1024]{1,0:T(8,128)(2,1)} custom-call(s32[2,128]{1,0:T(2,128)S(1)} %copy-done.3, bf16[576,512]{1,0:T(8,128)(2,1)S(1)} %bitcast.13), custom_call_target="tpu_custom_call" | custom-call | tf_op jit(solution)/shard_map/combine_input/pallas_call | solution.py:294
  (13 shorter events, 0.0 us)
Async XLA Ops:
  2.8 11.3 %collective-permute-start = (bf16[72,512]{1,0:T(8,128)(2,1)}, bf16[72,512]{1,0:T(8,128)(2,1)S(1)}, u32[]{:S(2)}, u32[]{:S(2)}) collective-permute-start(bf16[72,512]{1,0:T(8,128)(2,1)} %get-tuple-element.45), channel_id=1, source_target_pairs={{0,7},{1,6},{2,5},{3,4},{4,3},{5,2},{6,1},{7,0},{8,15},{9,14},{10,... | collective-permute-start | bytes 221192 | tf_op jit(solution)/shard_map/ppermute | solution.py:357
  8.8 7.9 %collective-permute-start.1 = (bf16[72,512]{1,0:T(8,128)(2,1)}, bf16[72,512]{1,0:T(8,128)(2,1)S(1)}, u32[]{:S(2)}, u32[]{:S(2)}) collective-permute-start(bf16[72,512]{1,0:T(8,128)(2,1)} %get-tuple-element.46), channel_id=1, source_target_pairs={{0,6},{1,7},{2,4},{3,5},{4,2},{5,3},{6,0},{7,1},{8,14},{9,15},{10,... | collective-permute-start | bytes 221192 | tf_op jit(solution)/shard_map/ppermute | solution.py:357
  9.0 11.6 %collective-permute-start.2 = (bf16[72,512]{1,0:T(8,128)(2,1)}, bf16[72,512]{1,0:T(8,128)(2,1)S(1)}, u32[]{:S(2)}, u32[]{:S(2)}) collective-permute-start(bf16[72,512]{1,0:T(8,128)(2,1)} %get-tuple-element.47), channel_id=1, source_target_pairs={{0,5},{1,4},{2,7},{3,6},{4,1},{5,0},{6,3},{7,2},{8,13},{9,12},{10,... | collective-permute-start | bytes 221192 | tf_op jit(solution)/shard_map/ppermute | solution.py:357
  9.8 11.8 %collective-permute-start.3 = (bf16[72,512]{1,0:T(8,128)(2,1)}, bf16[72,512]{1,0:T(8,128)(2,1)S(1)}, u32[]{:S(2)}, u32[]{:S(2)}) collective-permute-start(bf16[72,512]{1,0:T(8,128)(2,1)} %get-tuple-element.48), channel_id=1, source_target_pairs={{0,4},{1,5},{2,6},{3,7},{4,0},{5,1},{6,2},{7,3},{8,12},{9,13},{10,... | collective-permute-start | bytes 221192 | tf_op jit(solution)/shard_map/ppermute | solution.py:357
  11.8 9.8 %collective-permute-start.4 = (bf16[72,512]{1,0:T(8,128)(2,1)}, bf16[72,512]{1,0:T(8,128)(2,1)S(1)}, u32[]{:S(2)}, u32[]{:S(2)}) collective-permute-start(bf16[72,512]{1,0:T(8,128)(2,1)} %get-tuple-element.49), channel_id=1, source_target_pairs={{0,3},{1,2},{2,1},{3,0},{4,7},{5,6},{6,5},{7,4},{8,11},{9,10},{10,... | collective-permute-start | bytes 221192 | tf_op jit(solution)/shard_map/ppermute | solution.py:357
  14.1 7.7 %collective-permute-start.5 = (bf16[72,512]{1,0:T(8,128)(2,1)}, bf16[72,512]{1,0:T(8,128)(2,1)S(1)}, u32[]{:S(2)}, u32[]{:S(2)}) collective-permute-start(bf16[72,512]{1,0:T(8,128)(2,1)} %get-tuple-element.50), channel_id=1, source_target_pairs={{0,2},{1,3},{2,0},{3,1},{4,6},{5,7},{6,4},{7,5},{8,10},{9,11},{10,... | collective-permute-start | bytes 221192 | tf_op jit(solution)/shard_map/ppermute | solution.py:357
  16.7 5.1 %collective-permute-start.6 = (bf16[72,512]{1,0:T(8,128)(2,1)}, bf16[72,512]{1,0:T(8,128)(2,1)S(1)}, u32[]{:S(2)}, u32[]{:S(2)}) collective-permute-start(bf16[72,512]{1,0:T(8,128)(2,1)} %get-tuple-element.51), channel_id=1, source_target_pairs={{0,1},{1,0},{2,3},{3,2},{4,5},{5,4},{6,7},{7,6},{8,9},{9,8},{10,11... | collective-permute-start | bytes 221192 | tf_op jit(solution)/shard_map/ppermute | solution.py:357
  21.8 18.9 %all-to-all-start.1 = ((bf16[8,72,512]{2,1,0:T(8,128)(2,1)}), bf16[8,72,512]{2,1,0:T(8,128)(2,1)S(1)}, u32[]{:S(2)}, u32[]{:S(2)}) async-start(bf16[8,72,512]{2,1,0:T(8,128)(2,1)} %bitcast.23), calls=%async_computation.1 | async-start | bytes 1179648 | tf_op jit(solution)/shard_map/all_to_all | solution.py:345
  27.3 0.9 %copy-start.5 = (bf16[72,512]{1,0:T(8,128)(2,1)S(1)}, bf16[72,512]{1,0:T(8,128)(2,1)}, u32[]{:S(2)}) copy-start(bf16[72,512]{1,0:T(8,128)(2,1)} %get-tuple-element.44.refs_0_) | copy-start | bytes 221188
  28.9 1.5 %copy-start.1 = (bf16[4,72,1024]{2,1,0:T(8,128)(2,1)}, bf16[4,72,1024]{2,1,0:T(8,128)(2,1)S(1)}, u32[]{:S(2)}) copy-start(bf16[4,72,1024]{2,1,0:T(8,128)(2,1)S(1)} %regroup.2.rows_ref.refs_0_) | copy-start | bytes 1769476
  28.9 18.9 %collective-permute-start.7 = (bf16[4,72,1024]{2,1,0:T(8,128)(2,1)S(1)}, bf16[4,72,1024]{2,1,0:T(8,128)(2,1)S(1)}, u32[]{:S(2)}, u32[]{:S(2)}) collective-permute-start(bf16[4,72,1024]{2,1,0:T(8,128)(2,1)S(1)} %regroup.2.rows_ref.refs_0_), channel_id=1, source_target_pairs={{0,16},{8,24},{16,0},{24,8},{1,17},{9,25},{17,1},{25,9},{2,18},{10... | collective-permute-start | bytes 1769480 | tf_op jit(solution)/shard_map/ppermute | solution.py:357
  40.7 18.4 %all-to-all-start = ((bf16[8,72,512]{2,1,0:T(8,128)(2,1)}), bf16[8,72,512]{2,1,0:T(8,128)(2,1)S(1)}, u32[]{:S(2)}, u32[]{:S(2)}) async-start(bf16[8,72,512]{2,1,0:T(8,128)(2,1)} %bitcast.25), calls=%async_computation | async-start | bytes 1179648 | tf_op jit(solution)/shard_map/all_to_all | solution.py:345
  46.9 1.4 %copy-start.2 = (bf16[4,72,1024]{2,1,0:T(8,128)(2,1)}, bf16[4,72,1024]{2,1,0:T(8,128)(2,1)S(1)}, u32[]{:S(2)}) copy-start(bf16[4,72,1024]{2,1,0:T(8,128)(2,1)S(1)} %regroup.3.rows_ref.refs_1_) | copy-start | bytes 1769476
  46.9 11.6 %collective-permute-start.10 = (bf16[4,72,1024]{2,1,0:T(8,128)(2,1)S(1)}, bf16[4,72,1024]{2,1,0:T(8,128)(2,1)S(1)}, u32[]{:S(2)}, u32[]{:S(2)}) collective-permute-start(bf16[4,72,1024]{2,1,0:T(8,128)(2,1)S(1)} %regroup.3.rows_ref.refs_1_), channel_id=1, source_target_pairs={{0,16},{8,24},{16,0},{24,8},{1,17},{9,25},{17,1},{25,9},{2,18},{10... | collective-permute-start | bytes 1769480 | tf_op jit(solution)/shard_map/ppermute | solution.py:357
  47.7 10.5 %copy-start.6 = (bf16[4,72,1024]{2,1,0:T(8,128)(2,1)}, bf16[4,72,1024]{2,1,0:T(8,128)(2,1)S(1)}, u32[]{:S(2)}) copy-start(bf16[4,72,1024]{2,1,0:T(8,128)(2,1)S(1)} %collective-permute-done.7.refs_6_) | copy-start | bytes 1769476
  47.7 11.3 %collective-permute-start.9 = (bf16[4,72,1024]{2,1,0:T(8,128)(2,1)S(1)}, bf16[4,72,1024]{2,1,0:T(8,128)(2,1)S(1)}, u32[]{:S(2)}, u32[]{:S(2)}) collective-permute-start(bf16[4,72,1024]{2,1,0:T(8,128)(2,1)S(1)} %collective-permute-done.7.refs_6_), channel_id=1, source_target_pairs={{0,8},{8,0},{16,24},{24,16},{1,9},{9,1},{17,25},{25,17},{2,10},{10... | collective-permute-start | bytes 1769480 | tf_op jit(solution)/shard_map/ppermute | solution.py:357
  47.7 11.3 %collective-permute-start.8 = (bf16[4,72,1024]{2,1,0:T(8,128)(2,1)}, bf16[4,72,1024]{2,1,0:T(8,128)(2,1)S(1)}, u32[]{:S(2)}, u32[]{:S(2)}) collective-permute-start(bf16[4,72,1024]{2,1,0:T(8,128)(2,1)} %copy-done.1), channel_id=1, source_target_pairs={{0,8},{8,0},{16,24},{24,16},{1,9},{9,1},{17,25},{25,17},{2,10},{10... | collective-permute-start | bytes 1769480 | tf_op jit(solution)/shard_map/ppermute | solution.py:357
  48.3 17.4 %copy-start = (bf16[128,1024]{1,0:T(8,128)(2,1)S(1)}, bf16[128,1024]{1,0:T(8,128)(2,1)}, u32[]{:S(2)}) copy-start(bf16[128,1024]{1,0:T(8,128)(2,1)} %cot_ref.1) | copy-start | bytes 786436
  48.3 17.4 %copy-start.3 = (s32[2,128]{1,0:T(2,128)S(1)}, s32[2,128]{1,0:T(2,128)}, u32[]{:S(2)}) copy-start(s32[2,128]{1,0:T(2,128)} %get-tuple-element.43.target_ref) | copy-start | bytes 3076
  48.3 17.4 %copy-start.4 = (f32[128,2]{0,1:T(2,128)S(1)}, f32[128,2]{0,1:T(2,128)}, u32[]{:S(2)}) copy-start(f32[128,2]{0,1:T(2,128)} %param.7) | copy-start | bytes 3076
  58.5 8.6 %copy-start.7 = (bf16[4,72,1024]{2,1,0:T(8,128)(2,1)}, bf16[4,72,1024]{2,1,0:T(8,128)(2,1)S(1)}, u32[]{:S(2)}) copy-start(bf16[4,72,1024]{2,1,0:T(8,128)(2,1)S(1)} %collective-permute-done.10.refs_9_) | copy-start | bytes 1769476
  58.6 8.6 %collective-permute-start.11 = (bf16[4,72,1024]{2,1,0:T(8,128)(2,1)}, bf16[4,72,1024]{2,1,0:T(8,128)(2,1)}, u32[]{:S(2)}, u32[]{:S(2)}) collective-permute-start(bf16[4,72,1024]{2,1,0:T(8,128)(2,1)} %copy-done.2), channel_id=1, source_target_pairs={{0,8},{8,0},{16,24},{24,16},{1,9},{9,1},{17,25},{25,17},{2,10},{10... | collective-permute-start | bytes 1769480 | tf_op jit(solution)/shard_map/ppermute | solution.py:357
  58.6 8.6 %collective-permute-start.12 = (bf16[4,72,1024]{2,1,0:T(8,128)(2,1)S(1)}, bf16[4,72,1024]{2,1,0:T(8,128)(2,1)}, u32[]{:S(2)}, u32[]{:S(2)}) collective-permute-start(bf16[4,72,1024]{2,1,0:T(8,128)(2,1)S(1)} %collective-permute-done.10.refs_9_), channel_id=1, source_target_pairs={{0,8},{8,0},{16,24},{24,16},{1,9},{9,1},{17,25},{25,17},{2,10},{10... | collective-permute-start | bytes 1769480 | tf_op jit(solution)/shard_map/ppermute | solution.py:357
  59.1 8.1 %copy-start.8 = (bf16[4,72,1024]{2,1,0:T(8,128)(2,1)}, bf16[4,72,1024]{2,1,0:T(8,128)(2,1)S(1)}, u32[]{:S(2)}) copy-start(bf16[4,72,1024]{2,1,0:T(8,128)(2,1)S(1)} %collective-permute-done.9.refs_8_) | copy-start | bytes 1769476
  59.1 0.8 %copy-start.9 = (bf16[4,72,1024]{2,1,0:T(8,128)(2,1)}, bf16[4,72,1024]{2,1,0:T(8,128)(2,1)S(1)}, u32[]{:S(2)}) copy-start(bf16[4,72,1024]{2,1,0:T(8,128)(2,1)S(1)} %collective-permute-done.8.refs_7_) | copy-start | bytes 1769476
  59.9 21.9 %all-to-all-start.2 = ((bf16[8,72,512]{2,1,0:T(8,128)(2,1)}), bf16[8,72,512]{2,1,0:T(8,128)(2,1)S(1)}, u32[]{:S(2)}, u32[]{:S(2)}) async-start(bf16[8,72,512]{2,1,0:T(8,128)(2,1)} %bitcast.24), calls=%async_computation.2 | async-start | bytes 1179648 | tf_op jit(solution)/shard_map/all_to_all | solution.py:345

commit v4 on v3

--- a/solution.py
+++ b/solution.py
@@ -100,12 +100,12 @@
         slab_ref[...] = rows[j * 2 * slots : (j + 1) * 2 * slots]
 
 
-def cotangent_kernel(slots, target_ref, gate_ref, cot_hbm, slab_ref, cot_ref, sem):
+def cotangent_kernel(slots, mask, target_ref, gate_ref, cot_hbm, slab_ref, cot_ref, sem):
     copy = pltpu.make_async_copy(cot_hbm, cot_ref, sem)
     copy.start()
     half = cot_ref.shape[1] // 2
     slab, slot, right = slab_slot(iota((slab_ref.shape[0], 1), 0), slots)
-    slot = slab * slots + slot
+    slot = (slab ^ mask) * slots + slot
     is_first, is_second = slot == target_ref[0:1, :], slot == target_ref[1:2, :]
     gate = jnp.sum(
         jnp.where(is_first, gate_ref[0:1, :], 0.0) + jnp.where(is_second, gate_ref[1:2, :], 0.0),
@@ -117,17 +117,21 @@
     slab_ref[...] = (jnp.where(right, rows[:, half:], rows[:, :half]) * gate).astype(BF16)
 
 
-def regroup_kernel(slots, held, sources, *refs):
-    slab_refs, rows_ref = refs[:-1], refs[-1]
+def regroup_kernel(slots, held, sources, mask, *refs):
+    slab_refs, (rows_ref, own_ref, sem) = list(refs[:-3]), refs[-3:]
+    own = pltpu.make_async_copy(slab_refs[0], own_ref, sem)
+    own.start()
+    slab_refs[0] = own_ref
     per_expert = sources * CAP
-    half = slab_refs[0].shape[1]
+    half = own_ref.shape[1]
     number = iota((held * per_expert, 1), 0)
     expert = quotient(number, per_expert)
     rest = number - expert * per_expert
     source = quotient(rest, CAP)
-    slab = source ^ here("seq") if len(slab_refs) > 1 else source
+    slab = source ^ (here("seq") if len(slab_refs) > 1 else mask)
     row = slab * (2 * slots) + expert * CAP + rest - source * CAP
     at = iota((held * per_expert, 2 * slots * sources), 1)
+    own.wait()
     slabs = jnp.concatenate([ref[...] for ref in slab_refs], axis=0)
     for side in (0, 1):
         rows = dot(ones_where(at == row + side * slots), slabs, ((1,), (0,)))
@@ -136,79 +140,82 @@
             rows_ref[k, :, side * half : (side + 1) * half] = rows[span].astype(BF16)
 
 
-def slab_rows(parts, slots, held, sources):
+def send_slabs(parts, slots, held, sources, mask, out_hbm, out_ref, sems):
     per_expert = sources * CAP
     rows = jnp.concatenate(parts, axis=0).astype(BF16)
     half = rows.shape[1] // 2
-    source, slot, right = slab_slot(iota((2 * slots * sources, 1), 0), slots)
-    expert = quotient(slot, CAP)
-    row = expert * per_expert + source * CAP + slot - expert * CAP
-    out = dot(ones_where(iota((2 * slots * sources, held * per_expert), 1) == row), rows, ((1,), (0,)))
-    return jnp.where(right, out[:, half:], out[:, :half]).astype(BF16)
-
-
-def weight_copies(up_hbm, down_hbm, up_ref, down_ref, sems):
-    held = up_ref.shape[0]
-    ups = [pltpu.make_async_copy(up_hbm.at[k], up_ref.at[k], sems.at[0, k]) for k in range(held)]
-    downs = [pltpu.make_async_copy(down_hbm.at[k], down_ref.at[k], sems.at[1, k]) for k in range(held)]
-    return ups, downs
-
-
-def forward_kernel(
-    slots, held, sources, rows_ref, up_hbm, down_hbm, out_ref, act_hbm, slope_hbm, up_ref, down_ref, act_ref, slope_ref, sems
-):
-    ups, downs = weight_copies(up_hbm, down_hbm, up_ref, down_ref, sems)
-    for up, down in zip(ups, downs):
-        up.start()
-        down.start()
-    parts, stores = [], []
-    ups[0].wait()
-    hidden = dot(rows_ref[0], up_ref[0], ((1,), (1,)))
+    size = slots * sources
+    copies = []
+    for piece in (0, 1):
+        span = pl.ds(piece * size, size)
+        source, slot, right = slab_slot(iota((size, 1), 0) + piece * size, slots)
+        expert = quotient(slot, CAP)
+        row = expert * per_expert + (source ^ mask) * CAP + slot - expert * CAP
+        out = dot(ones_where(iota((size, held * per_expert), 1) == row), rows, ((1,), (0,)))
+        out_ref[span] = jnp.where(right, out[:, half:], out[:, :half]).astype(BF16)
+        copies.append(pltpu.make_async_copy(out_ref.at[span], out_hbm.at[span], sems.at[piece]))
+        copies[piece].start()
+    return copies
+
+
+def loads_of(sources_and_targets, sems):
+    copies = []
+    for i, (there, near) in enumerate(sources_and_targets):
+        copies.append([pltpu.make_async_copy(there.at[k], near.at[k], sems.at[i, k]) for k in range(near.shape[0])])
+        for copy in copies[i]:
+            copy.start()
+    return copies
+
+
+def forward_kernel(slots, held, sources, mask, rows_hbm, up_hbm, down_hbm, out_hbm, act_hbm, slope_hbm, *scratch):
+    rows_ref, up_ref, down_ref, act_ref, slope_ref, out_ref, sems = scratch
+    own, ups, downs = loads_of([(rows_hbm, rows_ref), (up_hbm, up_ref), (down_hbm, down_ref)], sems)
+    stores = []
+
+    def product(k):
+        own[k].wait()
+        ups[k].wait()
+        return dot(rows_ref[k], up_ref[k], ((1,), (1,)))
+
+    hidden = product(0)
     for k in range(held):
         now = hidden
+        if k + 1 < held:
+            hidden = product(k + 1)
+        value, slope = gelu_both(now)
+        act_ref[k] = value.astype(BF16)
+        slope_ref[k] = slope.astype(BF16)
+        for i, (near, there) in enumerate([(act_ref, act_hbm), (slope_ref, slope_hbm)]):
+            stores.append(pltpu.make_async_copy(near.at[k], there.at[k], sems.at[3 + i, k]))
+            stores[-1].start()
+    parts = []
+    for k in range(held):
         downs[k].wait()
-        if k + 1 < held:
-            ups[k + 1].wait()
-            hidden = dot(rows_ref[k + 1], up_ref[k + 1], ((1,), (1,)))
-        value, slope = gelu_both(now)
-        act = value.astype(BF16)
-        act_ref[k] = act
-        slope_ref[k] = slope.astype(BF16)
-        parts.append(dot(act, down_ref[k], ((1,), (0,))))
-        for i, (here, there) in enumerate([(act_ref, act_hbm), (slope_ref, slope_hbm)]):
-            stores.append(pltpu.make_async_copy(here.at[k], there.at[k], sems.at[2 + i, k]))
-            stores[-1].start()
-    out_ref[...] = slab_rows(parts, slots, held, sources)
+        parts.append(dot(act_ref[k], down_ref[k], ((1,), (0,))))
+    stores = stores + send_slabs(parts, slots, held, sources, mask, out_hbm, out_ref, sems.at[5])
     for store in stores:
         store.wait()
 
 
-def backward_kernel(
-    slots, held, sources, rows_ref, slope_hbm, up_hbm, down_hbm, out_ref, dhid_hbm, up_ref, down_ref, dhid_ref, slope_ref, sems
-):
-    ups, downs = weight_copies(up_hbm, down_hbm, up_ref, down_ref, sems)
-    slopes = pltpu.make_async_copy(slope_hbm, slope_ref, sems.at[3, 0])
+def backward_kernel(slots, held, sources, mask, rows_hbm, slope_hbm, up_hbm, down_hbm, out_hbm, dhid_hbm, *scratch):
+    rows_ref, up_ref, down_ref, dhid_ref, slope_ref, out_ref, sems = scratch
+    own, slopes, ups, downs = loads_of(
+        [(rows_hbm, rows_ref), (slope_hbm, slope_ref), (up_hbm, up_ref), (down_hbm, down_ref)], sems
+    )
+    stores = []
     for k in range(held):
-        ups[k].start()
-        if k == 0:
-            slopes.start()
-        downs[k].start()
-    parts, stores = [], []
-    ups[0].wait()
-    back = dot(rows_ref[0], up_ref[0], ((1,), (1,)))
-    slopes.wait()
+        own[k].wait()
+        slopes[k].wait()
+        ups[k].wait()
+        back = dot(rows_ref[k], up_ref[k], ((1,), (1,)))
+        dhid_ref[k] = (back * slope_ref[k].astype(F32)).astype(BF16)
+        stores.append(pltpu.make_async_copy(dhid_ref.at[k], dhid_hbm.at[k], sems.at[4, k]))
+        stores[-1].start()
+    parts = []
     for k in range(held):
-        now = back
         downs[k].wait()
-        if k + 1 < held:
-            ups[k + 1].wait()
-            back = dot(rows_ref[k + 1], up_ref[k + 1], ((1,), (1,)))
-        dhid = (now * slope_ref[k].astype(F32)).astype(BF16)
-        dhid_ref[k] = dhid
-        parts.append(dot(dhid, down_ref[k], ((1,), (0,))))
-        stores.append(pltpu.make_async_copy(dhid_ref.at[k], dhid_hbm.at[k], sems.at[2, k]))
-        stores[-1].start()
-    out_ref[...] = slab_rows(parts, slots, held, sources)
+        parts.append(dot(dhid_ref[k], down_ref[k], ((1,), (0,))))
+    stores = stores + send_slabs(parts, slots, held, sources, mask, out_hbm, out_ref, sems.at[5])
     for store in stores:
         store.wait()
 
@@ -244,17 +251,17 @@
     return jnp.sum(jnp.where(same, column, 0.0), axis=0, keepdims=True)
 
 
-def picked(target_ref, slots, rows):
+def picked(target_ref, slots, rows, mask):
     slab, slot, right = slab_slot(iota((1, rows), 1), slots)
-    slot = slab * slots + slot
+    slot = (slab ^ mask) * slots + slot
     columns = [as_column(target_ref[k : k + 1, :].astype(F32)).astype(jnp.int32) for k in (0, 1)]
     return [[(slot == column) & ~right, (slot == column) & right] for column in columns]
 
 
-def output_kernel(slots, target_ref, gate_ref, cot_ref, back_ref, out_ref, gate_grad_ref):
-    half = back_ref.shape[1]
-    masks = picked(target_ref, slots, back_ref.shape[0])
-    back = back_ref[...]
+def combine_kernel(slots, mask, target_ref, gate_ref, cot_ref, out_ref, in_ref, layer_ref, gate_grad_ref, input_ref):
+    half = out_ref.shape[1]
+    picks = picked(target_ref, slots, out_ref.shape[0], mask)
+    outs, ins = out_ref[...], in_ref[...]
     gates = gate_ref[...]
     cot = cot_ref[...].astype(F32)
     layer, dots = [0.0, 0.0], []
@@ -262,23 +269,17 @@
         gate = as_column(gates[k : k + 1, :])
         grad = 0.0
         for side in (0, 1):
-            rows = dot(ones_where(masks[k][side]), back, ((1,), (0,)))
+            rows = dot(ones_where(picks[k][side]), outs, ((1,), (0,)))
             layer[side] = layer[side] + gate * rows
             part = cot[:, side * half : (side + 1) * half] * rows
             grad = grad + jnp.sum(part, axis=1, keepdims=True)
         dots.append(as_row(grad))
+    gate_grad_ref[...] = jnp.concatenate(dots, axis=0)
     for side in (0, 1):
-        out_ref[:, side * half : (side + 1) * half] = layer[side].astype(BF16)
-    gate_grad_ref[...] = jnp.concatenate(dots, axis=0)
-
-
-def input_kernel(slots, target_ref, back_ref, out_ref):
-    half = back_ref.shape[1]
-    masks = picked(target_ref, slots, back_ref.shape[0])
-    back = back_ref[...]
-    for side in (0, 1):
-        pick = ones_where(masks[0][side] | masks[1][side])
-        out_ref[:, side * half : (side + 1) * half] = dot(pick, back, ((1,), (0,))).astype(BF16)
+        span = slice(side * half, (side + 1) * half)
+        layer_ref[:, span] = layer[side].astype(BF16)
+        pick = ones_where(picks[0][side] | picks[1][side])
+        input_ref[:, span] = dot(pick, ins, ((1,), (0,))).astype(BF16)
 
 
 def params(mib=58):
@@ -287,19 +288,6 @@
 
 def cost(flops, bytes_accessed):
     return pl.CostEstimate(flops=int(flops), bytes_accessed=int(bytes_accessed), transcendentals=0)
-
-
-def vmem_call(kernel, outs, args, name, estimate=None, mib=6):
-    vmem = pl.BlockSpec(memory_space=pltpu.VMEM)
-    return pl.pallas_call(
-        kernel,
-        out_shape=outs,
-        in_specs=[vmem] * len(args),
-        out_specs=jax.tree.map(lambda _: vmem, outs),
-        compiler_params=params(mib),
-        cost_estimate=estimate,
-        name=name,
-    )(*args)
 
 
 def local_rows(tokens, gate_values, expert_ids, cotangent, weight_in, weight_out):
@@ -314,6 +302,7 @@
     stacked = sources * 2 * slots
     factor = (E / (2.0 * count * sources * groups)) ** 0.5
     slab = jax.ShapeDtypeStruct((stacked, half), BF16)
+    mask = sources // 4
     rows_shape = jax.ShapeDtypeStruct((held, per_expert, width), BF16)
     units_shape = jax.ShapeDtypeStruct((held, per_expert, FF), BF16)
     peers_shape = jax.ShapeDtypeStruct((held, peers * per_expert, FF), BF16)
@@ -342,16 +331,21 @@
 
     def exchange(stack):
         cut = stack.reshape(sources, 2 * slots, half)
-        return lax.all_to_all(cut, "seq", split_axis=0, concat_axis=0, tiled=True).reshape(stacked, half)
+        order = [[j ^ mask for j in range(sources)]]
+        got = lax.all_to_all(cut, "seq", split_axis=0, concat_axis=0, tiled=True, axis_index_groups=order)
+        return got.reshape(stacked, half)
 
     def regroup(*stacks):
-        return vmem_call(
-            functools.partial(regroup_kernel, slots, held, sources),
-            rows_shape,
-            stacks,
-            "regroup",
-            cost(product, 4 * stacked * half),
-        )
+        return pl.pallas_call(
+            functools.partial(regroup_kernel, slots, held, sources, mask),
+            out_shape=rows_shape,
+            in_specs=[pl.BlockSpec(memory_space=pl.ANY)] + [vmem] * (len(stacks) - 1),
+            out_specs=vmem,
+            scratch_shapes=[pltpu.VMEM(stacks[0].shape, BF16), sems],
+            compiler_params=params(6),
+            cost_estimate=cost(product, 4 * stacked * half),
+            name="regroup",
+        )(*stacks)
 
     def across(rows, axis, bit):
         return lax.ppermute(rows, axis, [(i, i ^ bit) for i in range(lax.axis_size(axis))])
@@ -366,7 +360,7 @@
     far = groups // 2
     arrived = [pieces[0]] + [across(pieces[j], "seq", j) for j in range(1, sources)]
     send_d = pl.pallas_call(
-        functools.partial(cotangent_kernel, slots),
+        functools.partial(cotangent_kernel, slots, mask),
         out_shape=slab,
         in_specs=[vmem, vmem, hbm],
         out_specs=vmem,
@@ -374,7 +368,7 @@
         compiler_params=params(),
         name="dispatch_cotangents",
     )(target, gate_rows, cotangent)
-    order = (7,6,5,4,3,2,1)
+    order = range(sources - 1, 0, -1)
     send_d, *moved = lax.optimization_barrier((send_d, *[arrived[j] for j in order]))
     for j, one in zip(order, moved):
         arrived[j] = one
@@ -384,12 +378,14 @@
 
     units = pltpu.VMEM((held, per_expert, FF), BF16)
     experts = pltpu.VMEM((held, FF, width), BF16)
+    near_rows = pltpu.VMEM((held, per_expert, width), BF16)
+    near_slab = pltpu.VMEM((stacked, half), BF16)
     send_out, act, slope = pl.pallas_call(
-        functools.partial(forward_kernel, slots, held, sources),
+        functools.partial(forward_kernel, slots, held, sources, mask),
         out_shape=(slab, units_shape, units_shape),
-        in_specs=[vmem, hbm, hbm],
-        out_specs=(vmem, hbm, hbm),
-        scratch_shapes=[experts, experts, units, units, sems((4, held))],
+        in_specs=[hbm] * 3,
+        out_specs=(hbm,) * 3,
+        scratch_shapes=[near_rows, experts, experts, units, units, near_slab, sems((6, max(held, 2)))],
         compiler_params=params(),
         cost_estimate=cost(4 * product, 4 * weight_in.size),
         name="expert_forward",
@@ -400,16 +396,15 @@
     first_d = across(rows_d, "dp", far)
     all_x = from_peers(rows_x, first_x)
     send_in, dhid = pl.pallas_call(
-        functools.partial(backward_kernel, slots, held, sources),
+        functools.partial(backward_kernel, slots, held, sources, mask),
         out_shape=(slab, units_shape),
-        in_specs=[vmem, hbm, hbm, hbm],
-        out_specs=(vmem, hbm),
-        scratch_shapes=[experts, experts, units, units, sems((4, held))],
+        in_specs=[hbm] * 4,
+        out_specs=(hbm,) * 2,
+        scratch_shapes=[near_rows, experts, experts, units, units, near_slab, sems((6, max(held, 2)))],
         compiler_params=params(),
         cost_estimate=cost(4 * product, 4 * weight_in.size),
         name="expert_backward",
     )(rows_d, slope, wout, win)
-    send_in, *all_x = lax.optimization_barrier((send_in, *all_x))
     first_d, rows_d, dhid = lax.optimization_barrier((first_d, rows_d, dhid))
     got_in = exchange(send_in)
     all_d = from_peers(rows_d, first_d)
@@ -438,19 +433,16 @@
         name="gradients",
     )(index, rows_x, rows_d, act, dhid, win, wout, *all_x[1:], *all_d[1:])
 
-    layer_out, gate_grad = vmem_call(
-        functools.partial(output_kernel, slots),
-        (jax.ShapeDtypeStruct((count, width), BF16), jax.ShapeDtypeStruct((2, count), F32)),
-        [target, gate_rows, cotangent, got_out],
-        "combine_output",
-    )
-    got_in, weight_in_grad = lax.optimization_barrier((got_in, weight_in_grad))
-    input_grad = vmem_call(
-        functools.partial(input_kernel, slots),
-        jax.ShapeDtypeStruct((count, width), BF16),
-        [target, got_in],
-        "combine_input",
-    )
+    got_in, got_out, weight_in_grad = lax.optimization_barrier((got_in, got_out, weight_in_grad))
+    token_shape = jax.ShapeDtypeStruct((count, width), BF16)
+    layer_out, gate_grad, input_grad = pl.pallas_call(
+        functools.partial(combine_kernel, slots, mask),
+        out_shape=(token_shape, jax.ShapeDtypeStruct((2, count), F32), token_shape),
+        in_specs=[vmem] * 5,
+        out_specs=(vmem,) * 3,
+        compiler_params=params(6),
+        name="combine",
+    )(target, gate_rows, cotangent, got_out, got_in)
     return layer_out, gate_grad.T, input_grad, weight_in_grad, weight_out_grad
 
 

time: 83.6 us -> 79.8 us (0.955)
  Pallas kernels: 42.5 us -> 40 us
  waiting for transfers between devices: 3.57 us -> 2.6 us
    pallas_call x7 -> x6, Pallas kernels: 26.8 us -> 24.3 us  [the longest x1 9.31 us: local_rows(): pl.pallas_call(functools.partial(forward_kernel, slots, held, sources, ma...]
    all_to_all x3, waiting for transfers between devices: 1.52 us -> 0.01 us  [exchange(): lax.all_to_all(cut, 'seq', split_axis=0, concat_axis=0, tiled=True, axis_...]
  transfers between devices with their start and end apart: 16 -> 16, of which waited for: 6 -> 4; matrix products, arithmetic and copies ran while one was open for 0% -> 0% of each run, Pallas kernels for 47% -> 46%
where the time goes in v4:
time: 79.8 us; the launch traced here: 79.3 us
  Pallas kernels  40 us (50%)
  starting transfers between devices  34 us (43%)
  waiting for transfers between devices  2.6 us (3%)
  local copies, waits for them, and re-layouts  1.88 us (2%)
  between operations  0.8 us (1%)
    ppermute x13, starting transfers between devices, across(): lax.ppermute(rows, axis, [(i, i ^ bit) for i in range(lax.axis_size(axis))])  17.8 us
    all_to_all x3, starting transfers between devices, exchange(): lax.all_to_all(cut, 'seq', split_axis=0, concat_axis=0, tiled=True, axis_...  16.2 us
    pallas_call x1, Pallas kernels, local_rows(): pl.pallas_call(functools.partial(gradient_kernel, peers, factor), out_sha...  13.6 us
    pallas_call x1, Pallas kernels, local_rows(): pl.pallas_call(functools.partial(forward_kernel, slots, held, sources, ma...  9.31 us
    pallas_call x1, Pallas kernels, local_rows(): pl.pallas_call(functools.partial(backward_kernel, slots, held, sources, m...  8.75 us
    pallas_call x1, Pallas kernels, local_rows(): pl.pallas_call(functools.partial(cotangent_kernel, slots, mask), out_shap...  2.93 us
    ppermute x13, waiting for transfers between devices, across(): lax.ppermute(rows, axis, [(i, i ^ bit) for i in range(lax.axis_size(axis))])  2.59 us
    pallas_call x1, Pallas kernels, local_rows(): pl.pallas_call(functools.partial(token_kernel, slots, sources), out_shape...  2.12 us
  transfers between devices with their start and end apart: 16, of which 4 were waited for; matrix products, arithmetic and copies ran while one was open for 0% of the time, Pallas kernels for 46%

profile of v4, /device:TPU:0, one launch (start us, length us, event | category | flops | bytes accessed | tf_op | source)
XLA Modules:
  0.0 79.3 jit_solution(10181837205388971315)
XLA Ops:
  0.6 2.1 %dispatch_tokens.1 = (bf16[72,512]{1,0:T(8,128)(2,1)}, bf16[72,512]{1,0:T(8,128)(2,1)}, bf16[72,512]{1,0:T(8,128)(2,1)}, bf16[72,512]{1,0:T(8,128)(2,1)}, bf16[7...) custom-call(s32[2,128]{1,0:T(2,128)} %bitcast.26, ...), custom_call_target="tpu_custom_call" | custom-call | tf_op jit(solution)/shard_map/dispatch_tokens/pallas_call | solution.py:320
  2.8 6.0 %collective-permute-start = (bf16[72,512]{1,0:T(8,128)(2,1)}, bf16[72,512]{1,0:T(8,128)(2,1)S(1)}, u32[]{:S(2)}, u32[]{:S(2)}) collective-permute-start(bf16[72,512]{1,0:T(8,128)(2,1)} %get-tuple-element.42), channel_id=1, source_target_pairs={{0,7},{1,6},{2,5},{3,4},{4,3},{5,2},{6,1},{7,0},{8,15},{9,14},{10,... | collective-permute-start | bytes 221192 | tf_op jit(solution)/shard_map/ppermute | solution.py:351
  8.8 0.2 collective-permute-start.1
  9.0 0.8 collective-permute-start.2
  9.8 2.0 %collective-permute-start.3 = (bf16[72,512]{1,0:T(8,128)(2,1)}, bf16[72,512]{1,0:T(8,128)(2,1)S(1)}, u32[]{:S(2)}, u32[]{:S(2)}) collective-permute-start(bf16[72,512]{1,0:T(8,128)(2,1)} %get-tuple-element.45), channel_id=1, source_target_pairs={{0,4},{1,5},{2,6},{3,7},{4,0},{5,1},{6,2},{7,3},{8,12},{9,13},{10,... | collective-permute-start | bytes 221192 | tf_op jit(solution)/shard_map/ppermute | solution.py:351
  11.8 2.3 %collective-permute-start.4 = (bf16[72,512]{1,0:T(8,128)(2,1)}, bf16[72,512]{1,0:T(8,128)(2,1)S(1)}, u32[]{:S(2)}, u32[]{:S(2)}) collective-permute-start(bf16[72,512]{1,0:T(8,128)(2,1)} %get-tuple-element.46), channel_id=1, source_target_pairs={{0,3},{1,2},{2,1},{3,0},{4,7},{5,6},{6,5},{7,4},{8,11},{9,10},{10,... | collective-permute-start | bytes 221192 | tf_op jit(solution)/shard_map/ppermute | solution.py:351
  14.1 0.0 collective-permute-done.refs_7_
  14.1 2.6 %collective-permute-start.5 = (bf16[72,512]{1,0:T(8,128)(2,1)}, bf16[72,512]{1,0:T(8,128)(2,1)S(1)}, u32[]{:S(2)}, u32[]{:S(2)}) collective-permute-start(bf16[72,512]{1,0:T(8,128)(2,1)} %get-tuple-element.47), channel_id=1, source_target_pairs={{0,2},{1,3},{2,0},{3,1},{4,6},{5,7},{6,4},{7,5},{8,10},{9,11},{10,... | collective-permute-start | bytes 221192 | tf_op jit(solution)/shard_map/ppermute | solution.py:351
  16.7 0.0 collective-permute-done.1.refs_6_
  16.7 0.5 collective-permute-start.6
  17.2 2.9 %dispatch_cotangents.1 = bf16[576,512]{1,0:T(8,128)(2,1)} custom-call(s32[2,128]{1,0:T(2,128)} %get-tuple-element.41.target_ref, f32[2,128]{1,0:T(2,128)} %bitcast.15, bf16[128,1024]{1,0:T(8,128)(2,1)} %cot_ref.1), custom_call_target="tpu_custom_call" | custom-call | tf_op jit(solution)/shard_map/dispatch_cotangents/pallas_call | solution.py:362
  20.2 0.5 collective-permute-done.2.refs_5_
  20.7 0.9 %collective-permute-done.3.refs_4_ = bf16[72,512]{1,0:T(8,128)(2,1)S(1)} collective-permute-done((bf16[72,512]{1,0:T(8,128)(2,1)}, bf16[72,512]{1,0:T(8,128)(2,1)S(1)}, u32[]{:S(2)}, u32[]{:S(2)}) %collective-permute-start.3) | collective-permute-done | bytes 73760 | tf_op jit(solution)/shard_map/ppermute | solution.py:351
  21.6 0.0 collective-permute-done.4.refs_3_
  21.6 0.2 collective-permute-done.5.refs_2_
  21.8 0.0 collective-permute-done.6.refs_1_
  21.8 6.0 %all-to-all-start = ((bf16[8,72,512]{2,1,0:T(8,128)(2,1)}), bf16[8,72,512]{2,1,0:T(8,128)(2,1)S(1)}, u32[]{:S(2)}, u32[]{:S(2)}) async-start(bf16[8,72,512]{2,1,0:T(8,128)(2,1)} %bitcast.23), calls=%async_computation | async-start | bytes 1179648 | tf_op jit(solution)/shard_map/all_to_all | solution.py:335
  27.9 0.9 %copy-done.5 = bf16[72,512]{1,0:T(8,128)(2,1)S(1)} copy-done((bf16[72,512]{1,0:T(8,128)(2,1)S(1)}, bf16[72,512]{1,0:T(8,128)(2,1)}, u32[]{:S(2)}) %copy-start.5) | copy-done | bytes 73752
  28.8 0.8 %regroup.3.rows_hbm.refs_0_ = bf16[4,72,1024]{2,1,0:T(8,128)(2,1)S(1)} custom-call(bf16[72,512]{1,0:T(8,128)(2,1)S(1)} %copy-done.5, bf16[72,512]{1,0:T(8,128)(2,1)S(1)} %collective-permute-done.6.refs_1_, bf16[72,512]{1,0:T(8,128)(2,1)S(1)} %collective-permute-done.5.refs_2_, bf16[72,512]{1,0:T(8,128)(2,1)S(1)} %collective-permute-done.4.refs_3_, ...), custom_call_target="tpu_custom_call" | custom-call | flops 603979776 | bytes 1179648 | tf_op jit(solution)/shard_map/regroup/pallas_call | solution.py:339
  29.6 0.0 copy-start.1
  29.6 1.5 %collective-permute-start.7 = (bf16[4,72,1024]{2,1,0:T(8,128)(2,1)S(1)}, bf16[4,72,1024]{2,1,0:T(8,128)(2,1)S(1)}, u32[]{:S(2)}, u32[]{:S(2)}) collective-permute-start(bf16[4,72,1024]{2,1,0:T(8,128)(2,1)S(1)} %regroup.3.rows_hbm.refs_0_), channel_id=1, source_target_pairs={{0,16},{8,24},{16,0},{24,8},{1,17},{9,25},{17,1},{25,9},{2,18},{10... | collective-permute-start | bytes 1769480 | tf_op jit(solution)/shard_map/ppermute | solution.py:351
  31.1 0.0 copy-done.1
  31.1 9.3 %expert_forward.1 = (bf16[576,512]{1,0:T(8,128)(2,1)}, bf16[4,72,1024]{2,1,0:T(8,128)(2,1)}, bf16[4,72,1024]{2,1,0:T(8,128)(2,1)}) custom-call(bf16[4,72,1024]{2,1,0:T(8,128)(2,1)} %copy-done.1, bf16[4,1024,1024]{2,1,0:T(8,128)(2,1)} %bitcast.17, bf16[4,1024,1024]{2,1,0:T(8,128)(2,1)} %bitcast.20), custom_call_target="tpu_custom_call" | custom-call | flops 2415919104 | bytes 16777216 | tf_op jit(solution)/shard_map/expert_forward/pallas_call | solution.py:383
  40.4 0.0 all-to-all-done
  40.4 5.1 %all-to-all-start.2 = ((bf16[8,72,512]{2,1,0:T(8,128)(2,1)}), bf16[8,72,512]{2,1,0:T(8,128)(2,1)S(1)}, u32[]{:S(2)}, u32[]{:S(2)}) async-start(bf16[8,72,512]{2,1,0:T(8,128)(2,1)} %bitcast.25), calls=%async_computation.2 | async-start | bytes 1179648 | tf_op jit(solution)/shard_map/all_to_all | solution.py:335
  45.5 0.9 %regroup.2.rows_hbm.refs_1_ = bf16[4,72,1024]{2,1,0:T(8,128)(2,1)S(1)} custom-call(bf16[576,512]{1,0:T(8,128)(2,1)S(1)} %bitcast.14), custom_call_target="tpu_custom_call" | custom-call | flops 603979776 | bytes 1179648 | tf_op jit(solution)/shard_map/regroup/pallas_call | solution.py:339
  46.4 0.0 copy-start.2
  46.4 0.8 %collective-permute-start.8 = (bf16[4,72,1024]{2,1,0:T(8,128)(2,1)S(1)}, bf16[4,72,1024]{2,1,0:T(8,128)(2,1)S(1)}, u32[]{:S(2)}, u32[]{:S(2)}) collective-permute-start(bf16[4,72,1024]{2,1,0:T(8,128)(2,1)S(1)} %regroup.2.rows_hbm.refs_1_), channel_id=1, source_target_pairs={{0,16},{8,24},{16,0},{24,8},{1,17},{9,25},{17,1},{25,9},{2,18},{10... | collective-permute-start | bytes 1769480 | tf_op jit(solution)/shard_map/ppermute | solution.py:351
  47.2 0.0 collective-permute-done.7.refs_6_
  47.2 0.0 collective-permute-start.9
  47.2 0.5 collective-permute-start.10
  47.7 0.0 copy-done.2
  47.7 8.8 %expert_backward.1 = (bf16[576,512]{1,0:T(8,128)(2,1)}, bf16[4,72,1024]{2,1,0:T(8,128)(2,1)}) custom-call(bf16[4,72,1024]{2,1,0:T(8,128)(2,1)} %copy-done.2, bf16[4,72,1024]{2,1,0:T(8,128)(2,1)} %get-tuple-element.58.slope_hbm, bf16[4,1024,1024]{2,1,0:T(8,128)(2,1)} %bitcast.21, bf16[4,1024,1024]{2,1,0:T(8,128)(2,1)} %bitcast.18), custom_call_target="tpu_custom_call" | custom-call | flops 2415919104 | bytes 16777216 | tf_op jit(solution)/shard_map/expert_backward/pallas_call | solution.py:398
  56.5 0.9 %collective-permute-done.8.refs_9_ = bf16[4,72,1024]{2,1,0:T(8,128)(2,1)S(1)} collective-permute-done((bf16[4,72,1024]{2,1,0:T(8,128)(2,1)S(1)}, bf16[4,72,1024]{2,1,0:T(8,128)(2,1)S(1)}, u32[]{:S(2)}, u32[]{:S(2)}) %collective-permute-start.8) | collective-permute-done | bytes 589856 | tf_op jit(solution)/shard_map/ppermute | solution.py:351
  57.4 0.0 collective-permute-start.11
  57.4 0.5 collective-permute-start.12
  57.9 0.0 all-to-all-done.2
  57.9 5.1 %all-to-all-start.1 = ((bf16[8,72,512]{2,1,0:T(8,128)(2,1)}), bf16[8,72,512]{2,1,0:T(8,128)(2,1)S(1)}, u32[]{:S(2)}, u32[]{:S(2)}) async-start(bf16[8,72,512]{2,1,0:T(8,128)(2,1)} %bitcast.24), calls=%async_computation.1 | async-start | bytes 1179648 | tf_op jit(solution)/shard_map/all_to_all | solution.py:335
  63.0 0.0 collective-permute-done.9.refs_7_
  63.0 0.0 collective-permute-done.10.refs_8_
  63.0 0.0 collective-permute-done.11.refs_10_
  63.0 0.0 collective-permute-done.12.refs_11_
  63.1 0.8 %copy-done.9 = bf16[4,72,1024]{2,1,0:T(8,128)(2,1)} copy-done((bf16[4,72,1024]{2,1,0:T(8,128)(2,1)}, bf16[4,72,1024]{2,1,0:T(8,128)(2,1)S(1)}, u32[]{:S(2)}) %copy-start.9) | copy-done | bytes 589848
  63.9 0.0 copy-done.7
  63.9 0.1 copy-done.8
  64.0 13.6 %gradients.1 = (f32[256,4096]{1,0:T(8,128)}, f32[256,4096]{1,0:T(8,128)}) custom-call(s32[1]{0:T(128)} %bitcast.10.share_ref, bf16[4,72,1024]{2,1,0:T(8,128)(2,1)} %copy-done.1, bf16[4,72,1024]{2,1,0:T(8,128)(2,1)} %copy-done.2, bf16[4,72,1024]{2,1,0:T(8,128)(2,1)} %get-tuple-element.65.refs_2_, bf16[4,72,1024]{2,1,0:T(8,128)(2,1)} %get-tuple-element.66.refs_3_, ...), custom_call_target="tpu_custom_call" | custom-call | flops 7247757312 | bytes 33554432 | tf_op jit(solution)/shard_map/gradients/pallas_call | solution.py:422
  77.6 0.0 all-to-all-done.1
  77.7 1.6 %combine.1 = (bf16[128,1024]{1,0:T(8,128)(2,1)}, f32[2,128]{1,0:T(2,128)}, bf16[128,1024]{1,0:T(8,128)(2,1)}) custom-call(s32[2,128]{1,0:T(2,128)S(1)} %copy-done.4, f32[2,128]{1,0:T(2,128)S(1)} %bitcast.16, bf16[128,1024]{1,0:T(8,128)(2,1)S(1)} %copy-done, bf16[576,512]{1,0:T(8,128)(2,1)S(1)} %bitcast.12, bf16[576,512]{1,0:T(8,128)(2,1)S(1)} %bitcast.13), custom_call_target="tpu_custom_call" | custom-call | tf_op jit(solution)/shard_map/combine/pallas_call | solution.py:438
  (12 shorter events, 0.0 us)
Async XLA Ops:
  2.8 11.3 %collective-permute-start = (bf16[72,512]{1,0:T(8,128)(2,1)}, bf16[72,512]{1,0:T(8,128)(2,1)S(1)}, u32[]{:S(2)}, u32[]{:S(2)}) collective-permute-start(bf16[72,512]{1,0:T(8,128)(2,1)} %get-tuple-element.42), channel_id=1, source_target_pairs={{0,7},{1,6},{2,5},{3,4},{4,3},{5,2},{6,1},{7,0},{8,15},{9,14},{10,... | collective-permute-start | bytes 221192 | tf_op jit(solution)/shard_map/ppermute | solution.py:351
  8.8 7.9 %collective-permute-start.1 = (bf16[72,512]{1,0:T(8,128)(2,1)}, bf16[72,512]{1,0:T(8,128)(2,1)S(1)}, u32[]{:S(2)}, u32[]{:S(2)}) collective-permute-start(bf16[72,512]{1,0:T(8,128)(2,1)} %get-tuple-element.43), channel_id=1, source_target_pairs={{0,6},{1,7},{2,4},{3,5},{4,2},{5,3},{6,0},{7,1},{8,14},{9,15},{10,... | collective-permute-start | bytes 221192 | tf_op jit(solution)/shard_map/ppermute | solution.py:351
  9.0 11.6 %collective-permute-start.2 = (bf16[72,512]{1,0:T(8,128)(2,1)}, bf16[72,512]{1,0:T(8,128)(2,1)S(1)}, u32[]{:S(2)}, u32[]{:S(2)}) collective-permute-start(bf16[72,512]{1,0:T(8,128)(2,1)} %get-tuple-element.44), channel_id=1, source_target_pairs={{0,5},{1,4},{2,7},{3,6},{4,1},{5,0},{6,3},{7,2},{8,13},{9,12},{10,... | collective-permute-start | bytes 221192 | tf_op jit(solution)/shard_map/ppermute | solution.py:351
  9.8 11.8 %collective-permute-start.3 = (bf16[72,512]{1,0:T(8,128)(2,1)}, bf16[72,512]{1,0:T(8,128)(2,1)S(1)}, u32[]{:S(2)}, u32[]{:S(2)}) collective-permute-start(bf16[72,512]{1,0:T(8,128)(2,1)} %get-tuple-element.45), channel_id=1, source_target_pairs={{0,4},{1,5},{2,6},{3,7},{4,0},{5,1},{6,2},{7,3},{8,12},{9,13},{10,... | collective-permute-start | bytes 221192 | tf_op jit(solution)/shard_map/ppermute | solution.py:351
  11.8 9.8 %collective-permute-start.4 = (bf16[72,512]{1,0:T(8,128)(2,1)}, bf16[72,512]{1,0:T(8,128)(2,1)S(1)}, u32[]{:S(2)}, u32[]{:S(2)}) collective-permute-start(bf16[72,512]{1,0:T(8,128)(2,1)} %get-tuple-element.46), channel_id=1, source_target_pairs={{0,3},{1,2},{2,1},{3,0},{4,7},{5,6},{6,5},{7,4},{8,11},{9,10},{10,... | collective-permute-start | bytes 221192 | tf_op jit(solution)/shard_map/ppermute | solution.py:351
  14.1 7.7 %collective-permute-start.5 = (bf16[72,512]{1,0:T(8,128)(2,1)}, bf16[72,512]{1,0:T(8,128)(2,1)S(1)}, u32[]{:S(2)}, u32[]{:S(2)}) collective-permute-start(bf16[72,512]{1,0:T(8,128)(2,1)} %get-tuple-element.47), channel_id=1, source_target_pairs={{0,2},{1,3},{2,0},{3,1},{4,6},{5,7},{6,4},{7,5},{8,10},{9,11},{10,... | collective-permute-start | bytes 221192 | tf_op jit(solution)/shard_map/ppermute | solution.py:351
  16.7 5.1 %collective-permute-start.6 = (bf16[72,512]{1,0:T(8,128)(2,1)}, bf16[72,512]{1,0:T(8,128)(2,1)S(1)}, u32[]{:S(2)}, u32[]{:S(2)}) collective-permute-start(bf16[72,512]{1,0:T(8,128)(2,1)} %get-tuple-element.48), channel_id=1, source_target_pairs={{0,1},{1,0},{2,3},{3,2},{4,5},{5,4},{6,7},{7,6},{8,9},{9,8},{10,11... | collective-permute-start | bytes 221192 | tf_op jit(solution)/shard_map/ppermute | solution.py:351
  21.8 18.6 %all-to-all-start = ((bf16[8,72,512]{2,1,0:T(8,128)(2,1)}), bf16[8,72,512]{2,1,0:T(8,128)(2,1)S(1)}, u32[]{:S(2)}, u32[]{:S(2)}) async-start(bf16[8,72,512]{2,1,0:T(8,128)(2,1)} %bitcast.23), calls=%async_computation | async-start | bytes 1179648 | tf_op jit(solution)/shard_map/all_to_all | solution.py:335
  27.9 0.9 %copy-start.5 = (bf16[72,512]{1,0:T(8,128)(2,1)S(1)}, bf16[72,512]{1,0:T(8,128)(2,1)}, u32[]{:S(2)}) copy-start(bf16[72,512]{1,0:T(8,128)(2,1)} %get-tuple-element.50.refs_0_) | copy-start | bytes 221188
  29.6 1.5 %copy-start.1 = (bf16[4,72,1024]{2,1,0:T(8,128)(2,1)}, bf16[4,72,1024]{2,1,0:T(8,128)(2,1)S(1)}, u32[]{:S(2)}) copy-start(bf16[4,72,1024]{2,1,0:T(8,128)(2,1)S(1)} %regroup.3.rows_hbm.refs_0_) | copy-start | bytes 1769476
  29.6 17.6 %collective-permute-start.7 = (bf16[4,72,1024]{2,1,0:T(8,128)(2,1)S(1)}, bf16[4,72,1024]{2,1,0:T(8,128)(2,1)S(1)}, u32[]{:S(2)}, u32[]{:S(2)}) collective-permute-start(bf16[4,72,1024]{2,1,0:T(8,128)(2,1)S(1)} %regroup.3.rows_hbm.refs_0_), channel_id=1, source_target_pairs={{0,16},{8,24},{16,0},{24,8},{1,17},{9,25},{17,1},{25,9},{2,18},{10... | collective-permute-start | bytes 1769480 | tf_op jit(solution)/shard_map/ppermute | solution.py:351
  40.4 17.5 %all-to-all-start.2 = ((bf16[8,72,512]{2,1,0:T(8,128)(2,1)}), bf16[8,72,512]{2,1,0:T(8,128)(2,1)S(1)}, u32[]{:S(2)}, u32[]{:S(2)}) async-start(bf16[8,72,512]{2,1,0:T(8,128)(2,1)} %bitcast.25), calls=%async_computation.2 | async-start | bytes 1179648 | tf_op jit(solution)/shard_map/all_to_all | solution.py:335
  46.4 1.4 %copy-start.2 = (bf16[4,72,1024]{2,1,0:T(8,128)(2,1)}, bf16[4,72,1024]{2,1,0:T(8,128)(2,1)S(1)}, u32[]{:S(2)}) copy-start(bf16[4,72,1024]{2,1,0:T(8,128)(2,1)S(1)} %regroup.2.rows_hbm.refs_1_) | copy-start | bytes 1769476
  46.4 11.0 %collective-permute-start.8 = (bf16[4,72,1024]{2,1,0:T(8,128)(2,1)S(1)}, bf16[4,72,1024]{2,1,0:T(8,128)(2,1)S(1)}, u32[]{:S(2)}, u32[]{:S(2)}) collective-permute-start(bf16[4,72,1024]{2,1,0:T(8,128)(2,1)S(1)} %regroup.2.rows_hbm.refs_1_), channel_id=1, source_target_pairs={{0,16},{8,24},{16,0},{24,8},{1,17},{9,25},{17,1},{25,9},{2,18},{10... | collective-permute-start | bytes 1769480 | tf_op jit(solution)/shard_map/ppermute | solution.py:351
  47.2 9.3 %copy-start.6 = (bf16[4,72,1024]{2,1,0:T(8,128)(2,1)}, bf16[4,72,1024]{2,1,0:T(8,128)(2,1)S(1)}, u32[]{:S(2)}) copy-start(bf16[4,72,1024]{2,1,0:T(8,128)(2,1)S(1)} %collective-permute-done.7.refs_6_) | copy-start | bytes 1769476
  47.2 15.8 %collective-permute-start.9 = (bf16[4,72,1024]{2,1,0:T(8,128)(2,1)}, bf16[4,72,1024]{2,1,0:T(8,128)(2,1)S(1)}, u32[]{:S(2)}, u32[]{:S(2)}) collective-permute-start(bf16[4,72,1024]{2,1,0:T(8,128)(2,1)} %copy-done.1), channel_id=1, source_target_pairs={{0,8},{8,0},{16,24},{24,16},{1,9},{9,1},{17,25},{25,17},{2,10},{10... | collective-permute-start | bytes 1769480 | tf_op jit(solution)/shard_map/ppermute | solution.py:351
  47.2 15.8 %collective-permute-start.10 = (bf16[4,72,1024]{2,1,0:T(8,128)(2,1)S(1)}, bf16[4,72,1024]{2,1,0:T(8,128)(2,1)S(1)}, u32[]{:S(2)}, u32[]{:S(2)}) collective-permute-start(bf16[4,72,1024]{2,1,0:T(8,128)(2,1)S(1)} %collective-permute-done.7.refs_6_), channel_id=1, source_target_pairs={{0,8},{8,0},{16,24},{24,16},{1,9},{9,1},{17,25},{25,17},{2,10},{10... | collective-permute-start | bytes 1769480 | tf_op jit(solution)/shard_map/ppermute | solution.py:351
  57.4 6.5 %copy-start.7 = (bf16[4,72,1024]{2,1,0:T(8,128)(2,1)}, bf16[4,72,1024]{2,1,0:T(8,128)(2,1)S(1)}, u32[]{:S(2)}) copy-start(bf16[4,72,1024]{2,1,0:T(8,128)(2,1)S(1)} %collective-permute-done.8.refs_9_) | copy-start | bytes 1769476
  57.4 5.6 %collective-permute-start.11 = (bf16[4,72,1024]{2,1,0:T(8,128)(2,1)}, bf16[4,72,1024]{2,1,0:T(8,128)(2,1)}, u32[]{:S(2)}, u32[]{:S(2)}) collective-permute-start(bf16[4,72,1024]{2,1,0:T(8,128)(2,1)} %copy-done.2), channel_id=1, source_target_pairs={{0,8},{8,0},{16,24},{24,16},{1,9},{9,1},{17,25},{25,17},{2,10},{10... | collective-permute-start | bytes 1769480 | tf_op jit(solution)/shard_map/ppermute | solution.py:351
  57.4 5.6 %collective-permute-start.12 = (bf16[4,72,1024]{2,1,0:T(8,128)(2,1)S(1)}, bf16[4,72,1024]{2,1,0:T(8,128)(2,1)}, u32[]{:S(2)}, u32[]{:S(2)}) collective-permute-start(bf16[4,72,1024]{2,1,0:T(8,128)(2,1)S(1)} %collective-permute-done.8.refs_9_), channel_id=1, source_target_pairs={{0,8},{8,0},{16,24},{24,16},{1,9},{9,1},{17,25},{25,17},{2,10},{10... | collective-permute-start | bytes 1769480 | tf_op jit(solution)/shard_map/ppermute | solution.py:351
  57.9 19.7 %all-to-all-start.1 = ((bf16[8,72,512]{2,1,0:T(8,128)(2,1)}), bf16[8,72,512]{2,1,0:T(8,128)(2,1)S(1)}, u32[]{:S(2)}, u32[]{:S(2)}) async-start(bf16[8,72,512]{2,1,0:T(8,128)(2,1)} %bitcast.24), calls=%async_computation.1 | async-start | bytes 1179648 | tf_op jit(solution)/shard_map/all_to_all | solution.py:335
  63.0 1.0 %copy-start.8 = (bf16[4,72,1024]{2,1,0:T(8,128)(2,1)}, bf16[4,72,1024]{2,1,0:T(8,128)(2,1)S(1)}, u32[]{:S(2)}) copy-start(bf16[4,72,1024]{2,1,0:T(8,128)(2,1)S(1)} %collective-permute-done.9.refs_7_) | copy-start | bytes 1769476
  63.0 0.9 %copy-start.9 = (bf16[4,72,1024]{2,1,0:T(8,128)(2,1)}, bf16[4,72,1024]{2,1,0:T(8,128)(2,1)S(1)}, u32[]{:S(2)}) copy-start(bf16[4,72,1024]{2,1,0:T(8,128)(2,1)S(1)} %collective-permute-done.10.refs_8_) | copy-start | bytes 1769476
  64.0 13.6 %copy-start = (bf16[128,1024]{1,0:T(8,128)(2,1)S(1)}, bf16[128,1024]{1,0:T(8,128)(2,1)}, u32[]{:S(2)}) copy-start(bf16[128,1024]{1,0:T(8,128)(2,1)} %cot_ref.1) | copy-start | bytes 786436
  64.0 13.6 %copy-start.3 = (f32[128,2]{0,1:T(2,128)S(1)}, f32[128,2]{0,1:T(2,128)}, u32[]{:S(2)}) copy-start(f32[128,2]{0,1:T(2,128)} %param.7) | copy-start | bytes 3076
  64.0 13.6 %copy-start.4 = (s32[2,128]{1,0:T(2,128)S(1)}, s32[2,128]{1,0:T(2,128)}, u32[]{:S(2)}) copy-start(s32[2,128]{1,0:T(2,128)} %get-tuple-element.41.target_ref) | copy-start | bytes 3076

commit v5 on v4

--- a/solution.py
+++ b/solution.py
@@ -69,12 +69,14 @@
     return lax.axis_index(axis).astype(jnp.int32)
 
 
-def token_kernel(slots, sources, ids_hbm, tok_hbm, *refs):
-    slab_refs, (target_ref, ids_ref, tok_ref, sems) = refs[:sources], refs[sources:]
+def token_kernel(slots, sources, ids_hbm, gate_hbm, tok_hbm, *refs):
+    slab_refs, (target_ref, ids_ref, gate_ref, tok_ref, sems) = refs[: sources - 1], refs[sources - 1 :]
+    gate_copy = pltpu.make_async_copy(gate_hbm, gate_ref, sems.at[2])
     ids_copy = pltpu.make_async_copy(ids_hbm, ids_ref, sems.at[0])
     tok_copy = pltpu.make_async_copy(tok_hbm, tok_ref, sems.at[1])
     ids_copy.start()
     tok_copy.start()
+    gate_copy.start()
     count = tok_ref.shape[0]
     half = tok_ref.shape[1] // 2
     expert = iota((E, count), 0)
@@ -90,40 +92,42 @@
     slot_second = jnp.sum(jnp.where(hot_second, before, 0.0), axis=0, keepdims=True)
     target_first = first * CAP + slot_first.astype(jnp.int32)
     target_second = second * CAP + slot_second.astype(jnp.int32)
-    target_ref[0:1, :] = target_first
-    target_ref[1:2, :] = target_second
+    gate_copy.wait()
+    target_ref[0:1, :] = target_first.astype(F32)
+    target_ref[1:2, :] = target_second.astype(F32)
+    target_ref[2:4, :] = gate_ref[...]
     pick = ones_where((slot == target_first) | (slot == target_second))
     tok_copy.wait()
     rows = dot(pick, tok_ref[...], ((1,), (0,)))
     rows = jnp.where(right, rows[:, half:], rows[:, :half]).astype(BF16)
     for j, slab_ref in enumerate(slab_refs):
-        slab_ref[...] = rows[j * 2 * slots : (j + 1) * 2 * slots]
-
-
-def cotangent_kernel(slots, mask, target_ref, gate_ref, cot_hbm, slab_ref, cot_ref, sem):
-    copy = pltpu.make_async_copy(cot_hbm, cot_ref, sem)
-    copy.start()
+        slab_ref[...] = rows[(j + 1) * 2 * slots : (j + 2) * 2 * slots]
+
+
+def cotangent_kernel(slots, mask, target_ref, cot_ref, tok_ref, slab_ref, own_ref):
     half = cot_ref.shape[1] // 2
+    targets = target_ref[0:2, :].astype(jnp.int32)
     slab, slot, right = slab_slot(iota((slab_ref.shape[0], 1), 0), slots)
     slot = (slab ^ mask) * slots + slot
-    is_first, is_second = slot == target_ref[0:1, :], slot == target_ref[1:2, :]
+    is_first, is_second = slot == targets[0:1, :], slot == targets[1:2, :]
     gate = jnp.sum(
-        jnp.where(is_first, gate_ref[0:1, :], 0.0) + jnp.where(is_second, gate_ref[1:2, :], 0.0),
+        jnp.where(is_first, target_ref[2:3, :], 0.0) + jnp.where(is_second, target_ref[3:4, :], 0.0),
         axis=1,
         keepdims=True,
     )
-    copy.wait()
     rows = dot(ones_where(is_first | is_second), cot_ref[...], ((1,), (0,)))
     slab_ref[...] = (jnp.where(right, rows[:, half:], rows[:, :half]) * gate).astype(BF16)
+    slab, slot, right = slab_slot(iota((own_ref.shape[0], 1), 0), slots)
+    slot = here("seq") * slots + slot
+    pick = ones_where((slot == targets[0:1, :]) | (slot == targets[1:2, :]))
+    rows = dot(pick, tok_ref[...], ((1,), (0,)))
+    own_ref[...] = jnp.where(right, rows[:, half:], rows[:, :half]).astype(BF16)
 
 
 def regroup_kernel(slots, held, sources, mask, *refs):
-    slab_refs, (rows_ref, own_ref, sem) = list(refs[:-3]), refs[-3:]
-    own = pltpu.make_async_copy(slab_refs[0], own_ref, sem)
-    own.start()
-    slab_refs[0] = own_ref
+    slab_refs, rows_ref = refs[:-1], refs[-1]
     per_expert = sources * CAP
-    half = own_ref.shape[1]
+    half = slab_refs[0].shape[1]
     number = iota((held * per_expert, 1), 0)
     expert = quotient(number, per_expert)
     rest = number - expert * per_expert
@@ -131,7 +135,6 @@
     slab = source ^ (here("seq") if len(slab_refs) > 1 else mask)
     row = slab * (2 * slots) + expert * CAP + rest - source * CAP
     at = iota((held * per_expert, 2 * slots * sources), 1)
-    own.wait()
     slabs = jnp.concatenate([ref[...] for ref in slab_refs], axis=0)
     for side in (0, 1):
         rows = dot(ones_where(at == row + side * slots), slabs, ((1,), (0,)))
@@ -254,15 +257,15 @@
 def picked(target_ref, slots, rows, mask):
     slab, slot, right = slab_slot(iota((1, rows), 1), slots)
     slot = (slab ^ mask) * slots + slot
-    columns = [as_column(target_ref[k : k + 1, :].astype(F32)).astype(jnp.int32) for k in (0, 1)]
+    columns = [as_column(target_ref[k : k + 1, :]).astype(jnp.int32) for k in (0, 1)]
     return [[(slot == column) & ~right, (slot == column) & right] for column in columns]
 
 
-def combine_kernel(slots, mask, target_ref, gate_ref, cot_ref, out_ref, in_ref, layer_ref, gate_grad_ref, input_ref):
+def combine_kernel(slots, mask, target_ref, cot_ref, out_ref, in_ref, layer_ref, gate_grad_ref, input_ref):
     half = out_ref.shape[1]
     picks = picked(target_ref, slots, out_ref.shape[0], mask)
     outs, ins = out_ref[...], in_ref[...]
-    gates = gate_ref[...]
+    gates = target_ref[2:4, :]
     cot = cot_ref[...].astype(F32)
     layer, dots = [0.0, 0.0], []
     for k in (0, 1):
@@ -319,13 +322,18 @@
     piece = jax.ShapeDtypeStruct((2 * slots, half), BF16)
     *pieces, target = pl.pallas_call(
         functools.partial(token_kernel, slots, sources),
-        out_shape=(piece,) * sources + (jax.ShapeDtypeStruct((2, count), jnp.int32),),
-        in_specs=[hbm] * 2,
-        out_specs=(vmem,) * (sources + 1),
-        scratch_shapes=[pltpu.VMEM((2, count), jnp.int32), pltpu.VMEM((count, width), BF16), sems((2,))],
+        out_shape=(piece,) * (sources - 1) + (jax.ShapeDtypeStruct((4, count), F32),),
+        in_specs=[hbm] * 3,
+        out_specs=(vmem,) * sources,
+        scratch_shapes=[
+            pltpu.VMEM((2, count), jnp.int32),
+            pltpu.VMEM((2, count), F32),
+            pltpu.VMEM((count, width), BF16),
+            sems((3,)),
+        ],
         compiler_params=params(),
         name="dispatch_tokens",
-    )(ids_rows, tokens)
+    )(ids_rows, gate_rows, tokens)
     win = weight_in.reshape(held, FF, width)
     wout = weight_out.reshape(held, FF, width)
 
@@ -339,9 +347,8 @@
         return pl.pallas_call(
             functools.partial(regroup_kernel, slots, held, sources, mask),
             out_shape=rows_shape,
-            in_specs=[pl.BlockSpec(memory_space=pl.ANY)] + [vmem] * (len(stacks) - 1),
+            in_specs=[vmem] * len(stacks),
             out_specs=vmem,
-            scratch_shapes=[pltpu.VMEM(stacks[0].shape, BF16), sems],
             compiler_params=params(6),
             cost_estimate=cost(product, 4 * stacked * half),
             name="regroup",
@@ -358,16 +365,15 @@
         return got
 
     far = groups // 2
-    arrived = [pieces[0]] + [across(pieces[j], "seq", j) for j in range(1, sources)]
-    send_d = pl.pallas_call(
+    send_d, own_piece = pl.pallas_call(
         functools.partial(cotangent_kernel, slots, mask),
-        out_shape=slab,
-        in_specs=[vmem, vmem, hbm],
-        out_specs=vmem,
-        scratch_shapes=[pltpu.VMEM((count, width), BF16), sems],
-        compiler_params=params(),
+        out_shape=(slab, piece),
+        in_specs=[vmem] * 3,
+        out_specs=(vmem, vmem),
+        compiler_params=params(6),
         name="dispatch_cotangents",
-    )(target, gate_rows, cotangent)
+    )(target, cotangent, tokens)
+    arrived = [own_piece] + [across(pieces[j - 1], "seq", j) for j in range(1, sources)]
     order = range(sources - 1, 0, -1)
     send_d, *moved = lax.optimization_barrier((send_d, *[arrived[j] for j in order]))
     for j, one in zip(order, moved):
@@ -438,11 +444,11 @@
     layer_out, gate_grad, input_grad = pl.pallas_call(
         functools.partial(combine_kernel, slots, mask),
         out_shape=(token_shape, jax.ShapeDtypeStruct((2, count), F32), token_shape),
-        in_specs=[vmem] * 5,
+        in_specs=[vmem] * 4,
         out_specs=(vmem,) * 3,
         compiler_params=params(6),
         name="combine",
-    )(target, gate_rows, cotangent, got_out, got_in)
+    )(target, cotangent, got_out, got_in)
     return layer_out, gate_grad.T, input_grad, weight_in_grad, weight_out_grad
 
 

time: 79.8 us -> 78.5 us (0.984)
  Pallas kernels: 40 us -> 38 us
  local copies, waits for them, and re-layouts: 1.88 us -> 3.57 us
  waiting for transfers between devices: 2.6 us -> 0.96 us
    unnamed x20 -> x22, local copies, waits for them, and re-layouts: 1.88 us -> 3.57 us
    ppermute x13, waiting for transfers between devices: 2.59 us -> 0.95 us  [across(): lax.ppermute(rows, axis, [(i, i ^ bit) for i in range(lax.axis_size(axis))])]
    pallas_call x1, Pallas kernels: 2.93 us -> 1.32 us  [local_rows(): pl.pallas_call(functools.partial(cotangent_kernel, slots, mask), out_shap...]
  transfers between devices with their start and end apart: 16 -> 16, of which waited for: 4 -> 3; matrix products, arithmetic and copies ran while one was open for 0% -> 0% of each run, Pallas kernels for 46% -> 44%
where the time goes in v5:
time: 78.5 us; the launch traced here: 78 us
  Pallas kernels  38 us (48%)
  starting transfers between devices  34.7 us (44%)
  local copies, waits for them, and re-layouts  3.57 us (5%)
  waiting for transfers between devices  0.96 us (1%)
  between operations  0.79 us (1%)
    ppermute x13, starting transfers between devices, across(): lax.ppermute(rows, axis, [(i, i ^ bit) for i in range(lax.axis_size(axis))])  18.1 us
    all_to_all x3, starting transfers between devices, exchange(): lax.all_to_all(cut, 'seq', split_axis=0, concat_axis=0, tiled=True, axis_...  16.6 us
    pallas_call x1, Pallas kernels, local_rows(): pl.pallas_call(functools.partial(gradient_kernel, peers, factor), out_sha...  13.6 us
    pallas_call x1, Pallas kernels, local_rows(): pl.pallas_call(functools.partial(forward_kernel, slots, held, sources, ma...  9.31 us
    pallas_call x1, Pallas kernels, local_rows(): pl.pallas_call(functools.partial(backward_kernel, slots, held, sources, m...  8.75 us
    unnamed x22, local copies, waits for them, and re-layouts  3.57 us
    pallas_call x1, Pallas kernels, local_rows(): pl.pallas_call(functools.partial(token_kernel, slots, sources), out_shape...  2.13 us
    pallas_call x1, Pallas kernels, local_rows(): pl.pallas_call(functools.partial(combine_kernel, slots, mask), out_shape=...  1.64 us
  transfers between devices with their start and end apart: 16, of which 3 were waited for; matrix products, arithmetic and copies ran while one was open for 0% of the time, Pallas kernels for 44%

profile of v5, /device:TPU:0, one launch (start us, length us, event | category | flops | bytes accessed | tf_op | source)
XLA Modules:
  0.0 78.0 jit_solution(8095229209131882712)
XLA Ops:
  0.6 2.1 %dispatch_tokens.1 = (bf16[72,512]{1,0:T(8,128)(2,1)}, bf16[72,512]{1,0:T(8,128)(2,1)}, bf16[72,512]{1,0:T(8,128)(2,1)}, bf16[72,512]{1,0:T(8,128)(2,1)}, bf16[7...) custom-call(s32[2,128]{1,0:T(2,128)} %bitcast.23, ...), custom_call_target="tpu_custom_call" | custom-call | tf_op jit(solution)/shard_map/dispatch_tokens/pallas_call | solution.py:323
  2.8 6.0 %collective-permute-start = (bf16[72,512]{1,0:T(8,128)(2,1)}, bf16[72,512]{1,0:T(8,128)(2,1)S(1)}, u32[]{:S(2)}, u32[]{:S(2)}) collective-permute-start(bf16[72,512]{1,0:T(8,128)(2,1)} %get-tuple-element.44), channel_id=1, source_target_pairs={{0,7},{1,6},{2,5},{3,4},{4,3},{5,2},{6,1},{7,0},{8,15},{9,14},{10,... | collective-permute-start | bytes 221192 | tf_op jit(solution)/shard_map/ppermute | solution.py:358
  8.8 0.2 collective-permute-start.1
  9.0 0.8 collective-permute-start.2
  9.8 2.0 %collective-permute-start.3 = (bf16[72,512]{1,0:T(8,128)(2,1)}, bf16[72,512]{1,0:T(8,128)(2,1)S(1)}, u32[]{:S(2)}, u32[]{:S(2)}) collective-permute-start(bf16[72,512]{1,0:T(8,128)(2,1)} %get-tuple-element.47), channel_id=1, source_target_pairs={{0,4},{1,5},{2,6},{3,7},{4,0},{5,1},{6,2},{7,3},{8,12},{9,13},{10,... | collective-permute-start | bytes 221192 | tf_op jit(solution)/shard_map/ppermute | solution.py:358
  11.8 2.3 %collective-permute-start.4 = (bf16[72,512]{1,0:T(8,128)(2,1)}, bf16[72,512]{1,0:T(8,128)(2,1)S(1)}, u32[]{:S(2)}, u32[]{:S(2)}) collective-permute-start(bf16[72,512]{1,0:T(8,128)(2,1)} %get-tuple-element.48), channel_id=1, source_target_pairs={{0,3},{1,2},{2,1},{3,0},{4,7},{5,6},{6,5},{7,4},{8,11},{9,10},{10,... | collective-permute-start | bytes 221192 | tf_op jit(solution)/shard_map/ppermute | solution.py:358
  14.1 0.0 collective-permute-done.refs_7_
  14.1 2.6 %collective-permute-start.5 = (bf16[72,512]{1,0:T(8,128)(2,1)}, bf16[72,512]{1,0:T(8,128)(2,1)S(1)}, u32[]{:S(2)}, u32[]{:S(2)}) collective-permute-start(bf16[72,512]{1,0:T(8,128)(2,1)} %get-tuple-element.49), channel_id=1, source_target_pairs={{0,2},{1,3},{2,0},{3,1},{4,6},{5,7},{6,4},{7,5},{8,10},{9,11},{10,... | collective-permute-start | bytes 221192 | tf_op jit(solution)/shard_map/ppermute | solution.py:358
  16.7 0.0 collective-permute-done.1.refs_6_
  16.7 0.7 collective-permute-start.6
  17.4 0.9 %copy-done = bf16[128,1024]{1,0:T(8,128)(2,1)S(1)} copy-done((bf16[128,1024]{1,0:T(8,128)(2,1)S(1)}, bf16[128,1024]{1,0:T(8,128)(2,1)}, u32[]{:S(2)}) %copy-start) | copy-done | bytes 262168
  18.3 0.9 %copy-done.1 = bf16[128,1024]{1,0:T(8,128)(2,1)S(1)} copy-done((bf16[128,1024]{1,0:T(8,128)(2,1)S(1)}, bf16[128,1024]{1,0:T(8,128)(2,1)}, u32[]{:S(2)}) %copy-start.1) | copy-done | bytes 262168
  19.3 0.7 copy-done.5
  20.0 1.3 %dispatch_cotangents.1 = (bf16[576,512]{1,0:T(8,128)(2,1)}, bf16[72,512]{1,0:T(8,128)(2,1)S(1)}) custom-call(f32[4,128]{1,0:T(4,128)S(1)} %copy-done.5, bf16[128,1024]{1,0:T(8,128)(2,1)S(1)} %copy-done.1, bf16[128,1024]{1,0:T(8,128)(2,1)S(1)} %copy-done), custom_call_target="tpu_custom_call" | custom-call | tf_op jit(solution)/shard_map/dispatch_cotangents/pallas_call | solution.py:368
  21.3 0.0 collective-permute-done.2.refs_5_
  21.3 0.3 collective-permute-done.3.refs_4_
  21.6 0.0 collective-permute-done.4.refs_3_
  21.6 0.2 collective-permute-done.5.refs_2_
  21.8 0.0 collective-permute-done.6.refs_1_
  21.8 6.4 %all-to-all-start = ((bf16[8,72,512]{2,1,0:T(8,128)(2,1)}), bf16[8,72,512]{2,1,0:T(8,128)(2,1)S(1)}, u32[]{:S(2)}, u32[]{:S(2)}) async-start(bf16[8,72,512]{2,1,0:T(8,128)(2,1)} %bitcast.2), calls=%async_computation | async-start | bytes 1179648 | tf_op jit(solution)/shard_map/all_to_all | solution.py:343
  28.2 0.7 regroup.3.rows_hbm.refs_0_
  28.9 0.0 copy-start.3
  28.9 1.6 %collective-permute-start.7 = (bf16[4,72,1024]{2,1,0:T(8,128)(2,1)S(1)}, bf16[4,72,1024]{2,1,0:T(8,128)(2,1)S(1)}, u32[]{:S(2)}, u32[]{:S(2)}) collective-permute-start(bf16[4,72,1024]{2,1,0:T(8,128)(2,1)S(1)} %regroup.3.rows_hbm.refs_0_), channel_id=1, source_target_pairs={{0,16},{8,24},{16,0},{24,8},{1,17},{9,25},{17,1},{25,9},{2,18},{10... | collective-permute-start | bytes 1769480 | tf_op jit(solution)/shard_map/ppermute | solution.py:358
  30.5 0.0 copy-done.3
  30.5 9.3 %expert_forward.1 = (bf16[576,512]{1,0:T(8,128)(2,1)}, bf16[4,72,1024]{2,1,0:T(8,128)(2,1)}, bf16[4,72,1024]{2,1,0:T(8,128)(2,1)}) custom-call(bf16[4,72,1024]{2,1,0:T(8,128)(2,1)} %copy-done.3, bf16[4,1024,1024]{2,1,0:T(8,128)(2,1)} %bitcast.15, bf16[4,1024,1024]{2,1,0:T(8,128)(2,1)} %bitcast.18), custom_call_target="tpu_custom_call" | custom-call | flops 2415919104 | bytes 16777216 | tf_op jit(solution)/shard_map/expert_forward/pallas_call | solution.py:389
  39.8 0.0 all-to-all-done
  39.8 5.1 %all-to-all-start.2 = ((bf16[8,72,512]{2,1,0:T(8,128)(2,1)}), bf16[8,72,512]{2,1,0:T(8,128)(2,1)S(1)}, u32[]{:S(2)}, u32[]{:S(2)}) async-start(bf16[8,72,512]{2,1,0:T(8,128)(2,1)} %bitcast.22), calls=%async_computation.2 | async-start | bytes 1179648 | tf_op jit(solution)/shard_map/all_to_all | solution.py:343
  44.9 0.6 regroup.2.rows_hbm.refs_1_
  45.6 0.0 copy-start.4
  45.6 0.8 %collective-permute-start.8 = (bf16[4,72,1024]{2,1,0:T(8,128)(2,1)S(1)}, bf16[4,72,1024]{2,1,0:T(8,128)(2,1)S(1)}, u32[]{:S(2)}, u32[]{:S(2)}) collective-permute-start(bf16[4,72,1024]{2,1,0:T(8,128)(2,1)S(1)} %regroup.2.rows_hbm.refs_1_), channel_id=1, source_target_pairs={{0,16},{8,24},{16,0},{24,8},{1,17},{9,25},{17,1},{25,9},{2,18},{10... | collective-permute-start | bytes 1769480 | tf_op jit(solution)/shard_map/ppermute | solution.py:358
  46.4 0.0 collective-permute-done.7.refs_6_
  46.5 0.0 collective-permute-start.9
  46.5 0.5 collective-permute-start.10
  47.0 8.7 %expert_backward.1 = (bf16[576,512]{1,0:T(8,128)(2,1)}, bf16[4,72,1024]{2,1,0:T(8,128)(2,1)}) custom-call(bf16[4,72,1024]{2,1,0:T(8,128)(2,1)} %copy-done.4, bf16[4,72,1024]{2,1,0:T(8,128)(2,1)} %get-tuple-element.60.slope_hbm, bf16[4,1024,1024]{2,1,0:T(8,128)(2,1)} %bitcast.19, bf16[4,1024,1024]{2,1,0:T(8,128)(2,1)} %bitcast.16), custom_call_target="tpu_custom_call" | custom-call | flops 2415919104 | bytes 16777216 | tf_op jit(solution)/shard_map/expert_backward/pallas_call | solution.py:404
  55.7 0.4 collective-permute-done.8.refs_9_
  56.1 0.0 collective-permute-start.11
  56.1 0.5 collective-permute-start.12
  56.6 0.0 all-to-all-done.2
  56.6 5.1 %all-to-all-start.1 = ((bf16[8,72,512]{2,1,0:T(8,128)(2,1)}), bf16[8,72,512]{2,1,0:T(8,128)(2,1)S(1)}, u32[]{:S(2)}, u32[]{:S(2)}) async-start(bf16[8,72,512]{2,1,0:T(8,128)(2,1)} %bitcast.21), calls=%async_computation.1 | async-start | bytes 1179648 | tf_op jit(solution)/shard_map/all_to_all | solution.py:343
  61.7 0.0 collective-permute-done.9.refs_7_
  61.7 0.0 collective-permute-done.10.refs_8_
  61.8 0.0 collective-permute-done.11.refs_10_
  61.8 0.0 collective-permute-done.12.refs_11_
  61.8 0.9 %copy-done.10 = bf16[4,72,1024]{2,1,0:T(8,128)(2,1)} copy-done((bf16[4,72,1024]{2,1,0:T(8,128)(2,1)}, bf16[4,72,1024]{2,1,0:T(8,128)(2,1)S(1)}, u32[]{:S(2)}) %copy-start.10) | copy-done | bytes 589848
  62.7 0.1 copy-done.9
  62.8 13.6 %gradients.1 = (f32[256,4096]{1,0:T(8,128)}, f32[256,4096]{1,0:T(8,128)}) custom-call(s32[1]{0:T(128)} %bitcast.10.share_ref, bf16[4,72,1024]{2,1,0:T(8,128)(2,1)} %copy-done.3, bf16[4,72,1024]{2,1,0:T(8,128)(2,1)} %copy-done.4, bf16[4,72,1024]{2,1,0:T(8,128)(2,1)} %get-tuple-element.67.refs_2_, bf16[4,72,1024]{2,1,0:T(8,128)(2,1)} %get-tuple-element.68.refs_3_, ...), custom_call_target="tpu_custom_call" | custom-call | flops 7247757312 | bytes 33554432 | tf_op jit(solution)/shard_map/gradients/pallas_call | solution.py:428
  76.4 0.0 all-to-all-done.1
  76.4 1.6 %combine.1 = (bf16[128,1024]{1,0:T(8,128)(2,1)}, f32[2,128]{1,0:T(2,128)}, bf16[128,1024]{1,0:T(8,128)(2,1)}) custom-call(f32[4,128]{1,0:T(4,128)S(1)} %copy-done.6, bf16[128,1024]{1,0:T(8,128)(2,1)S(1)} %copy-done.2, bf16[576,512]{1,0:T(8,128)(2,1)S(1)} %bitcast.12, bf16[576,512]{1,0:T(8,128)(2,1)S(1)} %bitcast.13), custom_call_target="tpu_custom_call" | custom-call | tf_op jit(solution)/shard_map/combine/pallas_call | solution.py:444
  (14 shorter events, 0.0 us)
Async XLA Ops:
  2.8 11.3 %collective-permute-start = (bf16[72,512]{1,0:T(8,128)(2,1)}, bf16[72,512]{1,0:T(8,128)(2,1)S(1)}, u32[]{:S(2)}, u32[]{:S(2)}) collective-permute-start(bf16[72,512]{1,0:T(8,128)(2,1)} %get-tuple-element.44), channel_id=1, source_target_pairs={{0,7},{1,6},{2,5},{3,4},{4,3},{5,2},{6,1},{7,0},{8,15},{9,14},{10,... | collective-permute-start | bytes 221192 | tf_op jit(solution)/shard_map/ppermute | solution.py:358
  8.8 7.9 %collective-permute-start.1 = (bf16[72,512]{1,0:T(8,128)(2,1)}, bf16[72,512]{1,0:T(8,128)(2,1)S(1)}, u32[]{:S(2)}, u32[]{:S(2)}) collective-permute-start(bf16[72,512]{1,0:T(8,128)(2,1)} %get-tuple-element.45), channel_id=1, source_target_pairs={{0,6},{1,7},{2,4},{3,5},{4,2},{5,3},{6,0},{7,1},{8,14},{9,15},{10,... | collective-permute-start | bytes 221192 | tf_op jit(solution)/shard_map/ppermute | solution.py:358
  9.0 12.3 %collective-permute-start.2 = (bf16[72,512]{1,0:T(8,128)(2,1)}, bf16[72,512]{1,0:T(8,128)(2,1)S(1)}, u32[]{:S(2)}, u32[]{:S(2)}) collective-permute-start(bf16[72,512]{1,0:T(8,128)(2,1)} %get-tuple-element.46), channel_id=1, source_target_pairs={{0,5},{1,4},{2,7},{3,6},{4,1},{5,0},{6,3},{7,2},{8,13},{9,12},{10,... | collective-permute-start | bytes 221192 | tf_op jit(solution)/shard_map/ppermute | solution.py:358
  9.8 11.8 %collective-permute-start.3 = (bf16[72,512]{1,0:T(8,128)(2,1)}, bf16[72,512]{1,0:T(8,128)(2,1)S(1)}, u32[]{:S(2)}, u32[]{:S(2)}) collective-permute-start(bf16[72,512]{1,0:T(8,128)(2,1)} %get-tuple-element.47), channel_id=1, source_target_pairs={{0,4},{1,5},{2,6},{3,7},{4,0},{5,1},{6,2},{7,3},{8,12},{9,13},{10,... | collective-permute-start | bytes 221192 | tf_op jit(solution)/shard_map/ppermute | solution.py:358
  11.8 9.8 %collective-permute-start.4 = (bf16[72,512]{1,0:T(8,128)(2,1)}, bf16[72,512]{1,0:T(8,128)(2,1)S(1)}, u32[]{:S(2)}, u32[]{:S(2)}) collective-permute-start(bf16[72,512]{1,0:T(8,128)(2,1)} %get-tuple-element.48), channel_id=1, source_target_pairs={{0,3},{1,2},{2,1},{3,0},{4,7},{5,6},{6,5},{7,4},{8,11},{9,10},{10,... | collective-permute-start | bytes 221192 | tf_op jit(solution)/shard_map/ppermute | solution.py:358
  14.1 7.7 %collective-permute-start.5 = (bf16[72,512]{1,0:T(8,128)(2,1)}, bf16[72,512]{1,0:T(8,128)(2,1)S(1)}, u32[]{:S(2)}, u32[]{:S(2)}) collective-permute-start(bf16[72,512]{1,0:T(8,128)(2,1)} %get-tuple-element.49), channel_id=1, source_target_pairs={{0,2},{1,3},{2,0},{3,1},{4,6},{5,7},{6,4},{7,5},{8,10},{9,11},{10,... | collective-permute-start | bytes 221192 | tf_op jit(solution)/shard_map/ppermute | solution.py:358
  16.7 5.1 %collective-permute-start.6 = (bf16[72,512]{1,0:T(8,128)(2,1)}, bf16[72,512]{1,0:T(8,128)(2,1)S(1)}, u32[]{:S(2)}, u32[]{:S(2)}) collective-permute-start(bf16[72,512]{1,0:T(8,128)(2,1)} %get-tuple-element.50), channel_id=1, source_target_pairs={{0,1},{1,0},{2,3},{3,2},{4,5},{5,4},{6,7},{7,6},{8,9},{9,8},{10,11... | collective-permute-start | bytes 221192 | tf_op jit(solution)/shard_map/ppermute | solution.py:358
  17.4 0.9 %copy-start = (bf16[128,1024]{1,0:T(8,128)(2,1)S(1)}, bf16[128,1024]{1,0:T(8,128)(2,1)}, u32[]{:S(2)}) copy-start(bf16[128,1024]{1,0:T(8,128)(2,1)} %tok_ref.1) | copy-start | bytes 786436
  18.3 0.9 %copy-start.1 = (bf16[128,1024]{1,0:T(8,128)(2,1)S(1)}, bf16[128,1024]{1,0:T(8,128)(2,1)}, u32[]{:S(2)}) copy-start(bf16[128,1024]{1,0:T(8,128)(2,1)} %cot_ref.3) | copy-start | bytes 786436
  19.3 0.7 copy-start.5
  21.8 18.0 %all-to-all-start = ((bf16[8,72,512]{2,1,0:T(8,128)(2,1)}), bf16[8,72,512]{2,1,0:T(8,128)(2,1)S(1)}, u32[]{:S(2)}, u32[]{:S(2)}) async-start(bf16[8,72,512]{2,1,0:T(8,128)(2,1)} %bitcast.2), calls=%async_computation | async-start | bytes 1179648 | tf_op jit(solution)/shard_map/all_to_all | solution.py:343
  28.9 1.6 %copy-start.3 = (bf16[4,72,1024]{2,1,0:T(8,128)(2,1)}, bf16[4,72,1024]{2,1,0:T(8,128)(2,1)S(1)}, u32[]{:S(2)}) copy-start(bf16[4,72,1024]{2,1,0:T(8,128)(2,1)S(1)} %regroup.3.rows_hbm.refs_0_) | copy-start | bytes 1769476
  28.9 17.5 %collective-permute-start.7 = (bf16[4,72,1024]{2,1,0:T(8,128)(2,1)S(1)}, bf16[4,72,1024]{2,1,0:T(8,128)(2,1)S(1)}, u32[]{:S(2)}, u32[]{:S(2)}) collective-permute-start(bf16[4,72,1024]{2,1,0:T(8,128)(2,1)S(1)} %regroup.3.rows_hbm.refs_0_), channel_id=1, source_target_pairs={{0,16},{8,24},{16,0},{24,8},{1,17},{9,25},{17,1},{25,9},{2,18},{10... | collective-permute-start | bytes 1769480 | tf_op jit(solution)/shard_map/ppermute | solution.py:358
  39.8 16.8 %all-to-all-start.2 = ((bf16[8,72,512]{2,1,0:T(8,128)(2,1)}), bf16[8,72,512]{2,1,0:T(8,128)(2,1)S(1)}, u32[]{:S(2)}, u32[]{:S(2)}) async-start(bf16[8,72,512]{2,1,0:T(8,128)(2,1)} %bitcast.22), calls=%async_computation.2 | async-start | bytes 1179648 | tf_op jit(solution)/shard_map/all_to_all | solution.py:343
  45.6 1.4 %copy-start.4 = (bf16[4,72,1024]{2,1,0:T(8,128)(2,1)}, bf16[4,72,1024]{2,1,0:T(8,128)(2,1)S(1)}, u32[]{:S(2)}) copy-start(bf16[4,72,1024]{2,1,0:T(8,128)(2,1)S(1)} %regroup.2.rows_hbm.refs_1_) | copy-start | bytes 1769476
  45.6 10.5 %collective-permute-start.8 = (bf16[4,72,1024]{2,1,0:T(8,128)(2,1)S(1)}, bf16[4,72,1024]{2,1,0:T(8,128)(2,1)S(1)}, u32[]{:S(2)}, u32[]{:S(2)}) collective-permute-start(bf16[4,72,1024]{2,1,0:T(8,128)(2,1)S(1)} %regroup.2.rows_hbm.refs_1_), channel_id=1, source_target_pairs={{0,16},{8,24},{16,0},{24,8},{1,17},{9,25},{17,1},{25,9},{2,18},{10... | collective-permute-start | bytes 1769480 | tf_op jit(solution)/shard_map/ppermute | solution.py:358
  46.5 9.3 %copy-start.7 = (bf16[4,72,1024]{2,1,0:T(8,128)(2,1)}, bf16[4,72,1024]{2,1,0:T(8,128)(2,1)S(1)}, u32[]{:S(2)}) copy-start(bf16[4,72,1024]{2,1,0:T(8,128)(2,1)S(1)} %collective-permute-done.7.refs_6_) | copy-start | bytes 1769476
  46.5 15.3 %collective-permute-start.9 = (bf16[4,72,1024]{2,1,0:T(8,128)(2,1)}, bf16[4,72,1024]{2,1,0:T(8,128)(2,1)S(1)}, u32[]{:S(2)}, u32[]{:S(2)}) collective-permute-start(bf16[4,72,1024]{2,1,0:T(8,128)(2,1)} %copy-done.3), channel_id=1, source_target_pairs={{0,8},{8,0},{16,24},{24,16},{1,9},{9,1},{17,25},{25,17},{2,10},{10... | collective-permute-start | bytes 1769480 | tf_op jit(solution)/shard_map/ppermute | solution.py:358
  46.5 15.3 %collective-permute-start.10 = (bf16[4,72,1024]{2,1,0:T(8,128)(2,1)S(1)}, bf16[4,72,1024]{2,1,0:T(8,128)(2,1)S(1)}, u32[]{:S(2)}, u32[]{:S(2)}) collective-permute-start(bf16[4,72,1024]{2,1,0:T(8,128)(2,1)S(1)} %collective-permute-done.7.refs_6_), channel_id=1, source_target_pairs={{0,8},{8,0},{16,24},{24,16},{1,9},{9,1},{17,25},{25,17},{2,10},{10... | collective-permute-start | bytes 1769480 | tf_op jit(solution)/shard_map/ppermute | solution.py:358
  56.1 6.5 %copy-start.8 = (bf16[4,72,1024]{2,1,0:T(8,128)(2,1)}, bf16[4,72,1024]{2,1,0:T(8,128)(2,1)S(1)}, u32[]{:S(2)}) copy-start(bf16[4,72,1024]{2,1,0:T(8,128)(2,1)S(1)} %collective-permute-done.8.refs_9_) | copy-start | bytes 1769476
  56.1 5.6 %collective-permute-start.11 = (bf16[4,72,1024]{2,1,0:T(8,128)(2,1)}, bf16[4,72,1024]{2,1,0:T(8,128)(2,1)}, u32[]{:S(2)}, u32[]{:S(2)}) collective-permute-start(bf16[4,72,1024]{2,1,0:T(8,128)(2,1)} %copy-done.4), channel_id=1, source_target_pairs={{0,8},{8,0},{16,24},{24,16},{1,9},{9,1},{17,25},{25,17},{2,10},{10... | collective-permute-start | bytes 1769480 | tf_op jit(solution)/shard_map/ppermute | solution.py:358
  56.1 5.7 %collective-permute-start.12 = (bf16[4,72,1024]{2,1,0:T(8,128)(2,1)S(1)}, bf16[4,72,1024]{2,1,0:T(8,128)(2,1)}, u32[]{:S(2)}, u32[]{:S(2)}) collective-permute-start(bf16[4,72,1024]{2,1,0:T(8,128)(2,1)S(1)} %collective-permute-done.8.refs_9_), channel_id=1, source_target_pairs={{0,8},{8,0},{16,24},{24,16},{1,9},{9,1},{17,25},{25,17},{2,10},{10... | collective-permute-start | bytes 1769480 | tf_op jit(solution)/shard_map/ppermute | solution.py:358
  56.6 19.7 %all-to-all-start.1 = ((bf16[8,72,512]{2,1,0:T(8,128)(2,1)}), bf16[8,72,512]{2,1,0:T(8,128)(2,1)S(1)}, u32[]{:S(2)}, u32[]{:S(2)}) async-start(bf16[8,72,512]{2,1,0:T(8,128)(2,1)} %bitcast.21), calls=%async_computation.1 | async-start | bytes 1179648 | tf_op jit(solution)/shard_map/all_to_all | solution.py:343
  61.7 1.0 %copy-start.9 = (bf16[4,72,1024]{2,1,0:T(8,128)(2,1)}, bf16[4,72,1024]{2,1,0:T(8,128)(2,1)S(1)}, u32[]{:S(2)}) copy-start(bf16[4,72,1024]{2,1,0:T(8,128)(2,1)S(1)} %collective-permute-done.9.refs_7_) | copy-start | bytes 1769476
  61.8 0.9 %copy-start.10 = (bf16[4,72,1024]{2,1,0:T(8,128)(2,1)}, bf16[4,72,1024]{2,1,0:T(8,128)(2,1)S(1)}, u32[]{:S(2)}) copy-start(bf16[4,72,1024]{2,1,0:T(8,128)(2,1)S(1)} %collective-permute-done.10.refs_8_) | copy-start | bytes 1769476
  62.8 13.6 %copy-start.2 = (bf16[128,1024]{1,0:T(8,128)(2,1)S(1)}, bf16[128,1024]{1,0:T(8,128)(2,1)}, u32[]{:S(2)}) copy-start(bf16[128,1024]{1,0:T(8,128)(2,1)} %cot_ref.3) | copy-start | bytes 786436
  62.8 13.6 %copy-start.6 = (f32[4,128]{1,0:T(4,128)S(1)}, f32[4,128]{1,0:T(4,128)}, u32[]{:S(2)}) copy-start(f32[4,128]{1,0:T(4,128)} %get-tuple-element.42.target_ref) | copy-start | bytes 6148

commit v6 on v5

--- a/solution.py
+++ b/solution.py
@@ -175,17 +175,10 @@
     own, ups, downs = loads_of([(rows_hbm, rows_ref), (up_hbm, up_ref), (down_hbm, down_ref)], sems)
     stores = []
 
-    def product(k):
+    for k in range(held):
         own[k].wait()
         ups[k].wait()
-        return dot(rows_ref[k], up_ref[k], ((1,), (1,)))
-
-    hidden = product(0)
-    for k in range(held):
-        now = hidden
-        if k + 1 < held:
-            hidden = product(k + 1)
-        value, slope = gelu_both(now)
+        value, slope = gelu_both(dot(rows_ref[k], up_ref[k], ((1,), (1,))))
         act_ref[k] = value.astype(BF16)
         slope_ref[k] = slope.astype(BF16)
         for i, (near, there) in enumerate([(act_ref, act_hbm), (slope_ref, slope_hbm)]):

time: 78.5 us -> 78.3 us (level)
  no operation moved by 1% of the time
where the time goes in v6:
time: 78.3 us; the launch traced here: 77.9 us
  Pallas kernels  37.9 us (48%)
  starting transfers between devices  34.7 us (44%)
  local copies, waits for them, and re-layouts  3.57 us (5%)
  waiting for transfers between devices  0.96 us (1%)
  between operations  0.79 us (1%)
    ppermute x13, starting transfers between devices, across(): lax.ppermute(rows, axis, [(i, i ^ bit) for i in range(lax.axis_size(axis))])  18.1 us
    all_to_all x3, starting transfers between devices, exchange(): lax.all_to_all(cut, 'seq', split_axis=0, concat_axis=0, tiled=True, axis_...  16.6 us
    pallas_call x1, Pallas kernels, local_rows(): pl.pallas_call(functools.partial(gradient_kernel, peers, factor), out_sha...  13.6 us
    pallas_call x1, Pallas kernels, local_rows(): pl.pallas_call(functools.partial(forward_kernel, slots, held, sources, ma...  9.16 us
    pallas_call x1, Pallas kernels, local_rows(): pl.pallas_call(functools.partial(backward_kernel, slots, held, sources, m...  8.75 us
    unnamed x22, local copies, waits for them, and re-layouts  3.57 us
    pallas_call x1, Pallas kernels, local_rows(): pl.pallas_call(functools.partial(token_kernel, slots, sources), out_shape...  2.13 us
    pallas_call x1, Pallas kernels, local_rows(): pl.pallas_call(functools.partial(combine_kernel, slots, mask), out_shape=...  1.64 us
  transfers between devices with their start and end apart: 16, of which 3 were waited for; matrix products, arithmetic and copies ran while one was open for 0% of the time, Pallas kernels for 44%

profile of v6, /device:TPU:0, one launch (start us, length us, event | category | flops | bytes accessed | tf_op | source)
XLA Modules:
  0.0 77.9 jit_solution(506684715182505547)
XLA Ops:
  0.6 2.1 %dispatch_tokens.1 = (bf16[72,512]{1,0:T(8,128)(2,1)}, bf16[72,512]{1,0:T(8,128)(2,1)}, bf16[72,512]{1,0:T(8,128)(2,1)}, bf16[72,512]{1,0:T(8,128)(2,1)}, bf16[7...) custom-call(s32[2,128]{1,0:T(2,128)} %bitcast.23, ...), custom_call_target="tpu_custom_call" | custom-call | tf_op jit(solution)/shard_map/dispatch_tokens/pallas_call | solution.py:316
  2.8 6.0 %collective-permute-start = (bf16[72,512]{1,0:T(8,128)(2,1)}, bf16[72,512]{1,0:T(8,128)(2,1)S(1)}, u32[]{:S(2)}, u32[]{:S(2)}) collective-permute-start(bf16[72,512]{1,0:T(8,128)(2,1)} %get-tuple-element.44), channel_id=1, source_target_pairs={{0,7},{1,6},{2,5},{3,4},{4,3},{5,2},{6,1},{7,0},{8,15},{9,14},{10,... | collective-permute-start | bytes 221192 | tf_op jit(solution)/shard_map/ppermute | solution.py:351
  8.8 0.2 collective-permute-start.1
  9.0 0.8 collective-permute-start.2
  9.8 2.0 %collective-permute-start.3 = (bf16[72,512]{1,0:T(8,128)(2,1)}, bf16[72,512]{1,0:T(8,128)(2,1)S(1)}, u32[]{:S(2)}, u32[]{:S(2)}) collective-permute-start(bf16[72,512]{1,0:T(8,128)(2,1)} %get-tuple-element.47), channel_id=1, source_target_pairs={{0,4},{1,5},{2,6},{3,7},{4,0},{5,1},{6,2},{7,3},{8,12},{9,13},{10,... | collective-permute-start | bytes 221192 | tf_op jit(solution)/shard_map/ppermute | solution.py:351
  11.8 2.3 %collective-permute-start.4 = (bf16[72,512]{1,0:T(8,128)(2,1)}, bf16[72,512]{1,0:T(8,128)(2,1)S(1)}, u32[]{:S(2)}, u32[]{:S(2)}) collective-permute-start(bf16[72,512]{1,0:T(8,128)(2,1)} %get-tuple-element.48), channel_id=1, source_target_pairs={{0,3},{1,2},{2,1},{3,0},{4,7},{5,6},{6,5},{7,4},{8,11},{9,10},{10,... | collective-permute-start | bytes 221192 | tf_op jit(solution)/shard_map/ppermute | solution.py:351
  14.1 0.0 collective-permute-done.refs_7_
  14.1 2.6 %collective-permute-start.5 = (bf16[72,512]{1,0:T(8,128)(2,1)}, bf16[72,512]{1,0:T(8,128)(2,1)S(1)}, u32[]{:S(2)}, u32[]{:S(2)}) collective-permute-start(bf16[72,512]{1,0:T(8,128)(2,1)} %get-tuple-element.49), channel_id=1, source_target_pairs={{0,2},{1,3},{2,0},{3,1},{4,6},{5,7},{6,4},{7,5},{8,10},{9,11},{10,... | collective-permute-start | bytes 221192 | tf_op jit(solution)/shard_map/ppermute | solution.py:351
  16.7 0.0 collective-permute-done.1.refs_6_
  16.7 0.7 collective-permute-start.6
  17.4 0.9 %copy-done = bf16[128,1024]{1,0:T(8,128)(2,1)S(1)} copy-done((bf16[128,1024]{1,0:T(8,128)(2,1)S(1)}, bf16[128,1024]{1,0:T(8,128)(2,1)}, u32[]{:S(2)}) %copy-start) | copy-done | bytes 262168
  18.3 0.9 %copy-done.1 = bf16[128,1024]{1,0:T(8,128)(2,1)S(1)} copy-done((bf16[128,1024]{1,0:T(8,128)(2,1)S(1)}, bf16[128,1024]{1,0:T(8,128)(2,1)}, u32[]{:S(2)}) %copy-start.1) | copy-done | bytes 262168
  19.3 0.7 copy-done.5
  20.0 1.3 %dispatch_cotangents.1 = (bf16[576,512]{1,0:T(8,128)(2,1)}, bf16[72,512]{1,0:T(8,128)(2,1)S(1)}) custom-call(f32[4,128]{1,0:T(4,128)S(1)} %copy-done.5, bf16[128,1024]{1,0:T(8,128)(2,1)S(1)} %copy-done.1, bf16[128,1024]{1,0:T(8,128)(2,1)S(1)} %copy-done), custom_call_target="tpu_custom_call" | custom-call | tf_op jit(solution)/shard_map/dispatch_cotangents/pallas_call | solution.py:361
  21.3 0.0 collective-permute-done.2.refs_5_
  21.3 0.3 collective-permute-done.3.refs_4_
  21.6 0.0 collective-permute-done.4.refs_3_
  21.6 0.2 collective-permute-done.5.refs_2_
  21.8 0.0 collective-permute-done.6.refs_1_
  21.8 6.4 %all-to-all-start = ((bf16[8,72,512]{2,1,0:T(8,128)(2,1)}), bf16[8,72,512]{2,1,0:T(8,128)(2,1)S(1)}, u32[]{:S(2)}, u32[]{:S(2)}) async-start(bf16[8,72,512]{2,1,0:T(8,128)(2,1)} %bitcast.2), calls=%async_computation | async-start | bytes 1179648 | tf_op jit(solution)/shard_map/all_to_all | solution.py:336
  28.2 0.7 regroup.3.rows_hbm.refs_0_
  28.9 0.0 copy-start.3
  28.9 1.6 %collective-permute-start.7 = (bf16[4,72,1024]{2,1,0:T(8,128)(2,1)S(1)}, bf16[4,72,1024]{2,1,0:T(8,128)(2,1)S(1)}, u32[]{:S(2)}, u32[]{:S(2)}) collective-permute-start(bf16[4,72,1024]{2,1,0:T(8,128)(2,1)S(1)} %regroup.3.rows_hbm.refs_0_), channel_id=1, source_target_pairs={{0,16},{8,24},{16,0},{24,8},{1,17},{9,25},{17,1},{25,9},{2,18},{10... | collective-permute-start | bytes 1769480 | tf_op jit(solution)/shard_map/ppermute | solution.py:351
  30.5 0.0 copy-done.3
  30.5 9.2 %expert_forward.1 = (bf16[576,512]{1,0:T(8,128)(2,1)}, bf16[4,72,1024]{2,1,0:T(8,128)(2,1)}, bf16[4,72,1024]{2,1,0:T(8,128)(2,1)}) custom-call(bf16[4,72,1024]{2,1,0:T(8,128)(2,1)} %copy-done.3, bf16[4,1024,1024]{2,1,0:T(8,128)(2,1)} %bitcast.15, bf16[4,1024,1024]{2,1,0:T(8,128)(2,1)} %bitcast.18), custom_call_target="tpu_custom_call" | custom-call | flops 2415919104 | bytes 16777216 | tf_op jit(solution)/shard_map/expert_forward/pallas_call | solution.py:382
  39.7 0.0 all-to-all-done
  39.7 5.1 %all-to-all-start.2 = ((bf16[8,72,512]{2,1,0:T(8,128)(2,1)}), bf16[8,72,512]{2,1,0:T(8,128)(2,1)S(1)}, u32[]{:S(2)}, u32[]{:S(2)}) async-start(bf16[8,72,512]{2,1,0:T(8,128)(2,1)} %bitcast.22), calls=%async_computation.2 | async-start | bytes 1179648 | tf_op jit(solution)/shard_map/all_to_all | solution.py:336
  44.8 0.6 regroup.2.rows_hbm.refs_1_
  45.5 0.8 %collective-permute-start.8 = (bf16[4,72,1024]{2,1,0:T(8,128)(2,1)S(1)}, bf16[4,72,1024]{2,1,0:T(8,128)(2,1)S(1)}, u32[]{:S(2)}, u32[]{:S(2)}) collective-permute-start(bf16[4,72,1024]{2,1,0:T(8,128)(2,1)S(1)} %regroup.2.rows_hbm.refs_1_), channel_id=1, source_target_pairs={{0,16},{8,24},{16,0},{24,8},{1,17},{9,25},{17,1},{25,9},{2,18},{10... | collective-permute-start | bytes 1769480 | tf_op jit(solution)/shard_map/ppermute | solution.py:351
  46.3 0.0 collective-permute-done.7.refs_6_
  46.3 0.0 collective-permute-start.9
  46.3 0.5 collective-permute-start.10
  46.8 8.7 %expert_backward.1 = (bf16[576,512]{1,0:T(8,128)(2,1)}, bf16[4,72,1024]{2,1,0:T(8,128)(2,1)}) custom-call(bf16[4,72,1024]{2,1,0:T(8,128)(2,1)} %copy-done.4, bf16[4,72,1024]{2,1,0:T(8,128)(2,1)} %get-tuple-element.60.slope_hbm, bf16[4,1024,1024]{2,1,0:T(8,128)(2,1)} %bitcast.19, bf16[4,1024,1024]{2,1,0:T(8,128)(2,1)} %bitcast.16), custom_call_target="tpu_custom_call" | custom-call | flops 2415919104 | bytes 16777216 | tf_op jit(solution)/shard_map/expert_backward/pallas_call | solution.py:397
  55.6 0.4 collective-permute-done.8.refs_9_
  56.0 0.0 collective-permute-start.11
  56.0 0.5 collective-permute-start.12
  56.5 0.0 all-to-all-done.2
  56.5 5.1 %all-to-all-start.1 = ((bf16[8,72,512]{2,1,0:T(8,128)(2,1)}), bf16[8,72,512]{2,1,0:T(8,128)(2,1)S(1)}, u32[]{:S(2)}, u32[]{:S(2)}) async-start(bf16[8,72,512]{2,1,0:T(8,128)(2,1)} %bitcast.21), calls=%async_computation.1 | async-start | bytes 1179648 | tf_op jit(solution)/shard_map/all_to_all | solution.py:336
  61.6 0.0 collective-permute-done.9.refs_7_
  61.6 0.0 collective-permute-done.10.refs_8_
  61.6 0.0 copy-start.10
  61.6 0.0 collective-permute-done.11.refs_10_
  61.6 0.0 collective-permute-done.12.refs_11_
  61.6 0.9 %copy-done.10 = bf16[4,72,1024]{2,1,0:T(8,128)(2,1)} copy-done((bf16[4,72,1024]{2,1,0:T(8,128)(2,1)}, bf16[4,72,1024]{2,1,0:T(8,128)(2,1)S(1)}, u32[]{:S(2)}) %copy-start.10) | copy-done | bytes 589848
  62.5 0.1 copy-done.9
  62.6 13.6 %gradients.1 = (f32[256,4096]{1,0:T(8,128)}, f32[256,4096]{1,0:T(8,128)}) custom-call(s32[1]{0:T(128)} %bitcast.10.share_ref, bf16[4,72,1024]{2,1,0:T(8,128)(2,1)} %copy-done.3, bf16[4,72,1024]{2,1,0:T(8,128)(2,1)} %copy-done.4, bf16[4,72,1024]{2,1,0:T(8,128)(2,1)} %get-tuple-element.67.refs_2_, bf16[4,72,1024]{2,1,0:T(8,128)(2,1)} %get-tuple-element.68.refs_3_, ...), custom_call_target="tpu_custom_call" | custom-call | flops 7247757312 | bytes 33554432 | tf_op jit(solution)/shard_map/gradients/pallas_call | solution.py:421
  76.2 0.0 all-to-all-done.1
  76.2 1.6 %combine.1 = (bf16[128,1024]{1,0:T(8,128)(2,1)}, f32[2,128]{1,0:T(2,128)}, bf16[128,1024]{1,0:T(8,128)(2,1)}) custom-call(f32[4,128]{1,0:T(4,128)S(1)} %copy-done.6, bf16[128,1024]{1,0:T(8,128)(2,1)S(1)} %copy-done.2, bf16[576,512]{1,0:T(8,128)(2,1)S(1)} %bitcast.12, bf16[576,512]{1,0:T(8,128)(2,1)S(1)} %bitcast.13), custom_call_target="tpu_custom_call" | custom-call | tf_op jit(solution)/shard_map/combine/pallas_call | solution.py:437
  (14 shorter events, 0.0 us)
Async XLA Ops:
  2.8 11.3 %collective-permute-start = (bf16[72,512]{1,0:T(8,128)(2,1)}, bf16[72,512]{1,0:T(8,128)(2,1)S(1)}, u32[]{:S(2)}, u32[]{:S(2)}) collective-permute-start(bf16[72,512]{1,0:T(8,128)(2,1)} %get-tuple-element.44), channel_id=1, source_target_pairs={{0,7},{1,6},{2,5},{3,4},{4,3},{5,2},{6,1},{7,0},{8,15},{9,14},{10,... | collective-permute-start | bytes 221192 | tf_op jit(solution)/shard_map/ppermute | solution.py:351
  8.8 7.9 %collective-permute-start.1 = (bf16[72,512]{1,0:T(8,128)(2,1)}, bf16[72,512]{1,0:T(8,128)(2,1)S(1)}, u32[]{:S(2)}, u32[]{:S(2)}) collective-permute-start(bf16[72,512]{1,0:T(8,128)(2,1)} %get-tuple-element.45), channel_id=1, source_target_pairs={{0,6},{1,7},{2,4},{3,5},{4,2},{5,3},{6,0},{7,1},{8,14},{9,15},{10,... | collective-permute-start | bytes 221192 | tf_op jit(solution)/shard_map/ppermute | solution.py:351
  9.0 12.3 %collective-permute-start.2 = (bf16[72,512]{1,0:T(8,128)(2,1)}, bf16[72,512]{1,0:T(8,128)(2,1)S(1)}, u32[]{:S(2)}, u32[]{:S(2)}) collective-permute-start(bf16[72,512]{1,0:T(8,128)(2,1)} %get-tuple-element.46), channel_id=1, source_target_pairs={{0,5},{1,4},{2,7},{3,6},{4,1},{5,0},{6,3},{7,2},{8,13},{9,12},{10,... | collective-permute-start | bytes 221192 | tf_op jit(solution)/shard_map/ppermute | solution.py:351
  9.8 11.8 %collective-permute-start.3 = (bf16[72,512]{1,0:T(8,128)(2,1)}, bf16[72,512]{1,0:T(8,128)(2,1)S(1)}, u32[]{:S(2)}, u32[]{:S(2)}) collective-permute-start(bf16[72,512]{1,0:T(8,128)(2,1)} %get-tuple-element.47), channel_id=1, source_target_pairs={{0,4},{1,5},{2,6},{3,7},{4,0},{5,1},{6,2},{7,3},{8,12},{9,13},{10,... | collective-permute-start | bytes 221192 | tf_op jit(solution)/shard_map/ppermute | solution.py:351
  11.8 9.8 %collective-permute-start.4 = (bf16[72,512]{1,0:T(8,128)(2,1)}, bf16[72,512]{1,0:T(8,128)(2,1)S(1)}, u32[]{:S(2)}, u32[]{:S(2)}) collective-permute-start(bf16[72,512]{1,0:T(8,128)(2,1)} %get-tuple-element.48), channel_id=1, source_target_pairs={{0,3},{1,2},{2,1},{3,0},{4,7},{5,6},{6,5},{7,4},{8,11},{9,10},{10,... | collective-permute-start | bytes 221192 | tf_op jit(solution)/shard_map/ppermute | solution.py:351
  14.1 7.7 %collective-permute-start.5 = (bf16[72,512]{1,0:T(8,128)(2,1)}, bf16[72,512]{1,0:T(8,128)(2,1)S(1)}, u32[]{:S(2)}, u32[]{:S(2)}) collective-permute-start(bf16[72,512]{1,0:T(8,128)(2,1)} %get-tuple-element.49), channel_id=1, source_target_pairs={{0,2},{1,3},{2,0},{3,1},{4,6},{5,7},{6,4},{7,5},{8,10},{9,11},{10,... | collective-permute-start | bytes 221192 | tf_op jit(solution)/shard_map/ppermute | solution.py:351
  16.7 5.1 %collective-permute-start.6 = (bf16[72,512]{1,0:T(8,128)(2,1)}, bf16[72,512]{1,0:T(8,128)(2,1)S(1)}, u32[]{:S(2)}, u32[]{:S(2)}) collective-permute-start(bf16[72,512]{1,0:T(8,128)(2,1)} %get-tuple-element.50), channel_id=1, source_target_pairs={{0,1},{1,0},{2,3},{3,2},{4,5},{5,4},{6,7},{7,6},{8,9},{9,8},{10,11... | collective-permute-start | bytes 221192 | tf_op jit(solution)/shard_map/ppermute | solution.py:351
  17.4 0.9 %copy-start = (bf16[128,1024]{1,0:T(8,128)(2,1)S(1)}, bf16[128,1024]{1,0:T(8,128)(2,1)}, u32[]{:S(2)}) copy-start(bf16[128,1024]{1,0:T(8,128)(2,1)} %tok_ref.1) | copy-start | bytes 786436
  18.3 0.9 %copy-start.1 = (bf16[128,1024]{1,0:T(8,128)(2,1)S(1)}, bf16[128,1024]{1,0:T(8,128)(2,1)}, u32[]{:S(2)}) copy-start(bf16[128,1024]{1,0:T(8,128)(2,1)} %cot_ref.3) | copy-start | bytes 786436
  19.3 0.7 copy-start.5
  21.8 17.8 %all-to-all-start = ((bf16[8,72,512]{2,1,0:T(8,128)(2,1)}), bf16[8,72,512]{2,1,0:T(8,128)(2,1)S(1)}, u32[]{:S(2)}, u32[]{:S(2)}) async-start(bf16[8,72,512]{2,1,0:T(8,128)(2,1)} %bitcast.2), calls=%async_computation | async-start | bytes 1179648 | tf_op jit(solution)/shard_map/all_to_all | solution.py:336
  28.9 1.6 %copy-start.3 = (bf16[4,72,1024]{2,1,0:T(8,128)(2,1)}, bf16[4,72,1024]{2,1,0:T(8,128)(2,1)S(1)}, u32[]{:S(2)}) copy-start(bf16[4,72,1024]{2,1,0:T(8,128)(2,1)S(1)} %regroup.3.rows_hbm.refs_0_) | copy-start | bytes 1769476
  28.9 17.4 %collective-permute-start.7 = (bf16[4,72,1024]{2,1,0:T(8,128)(2,1)S(1)}, bf16[4,72,1024]{2,1,0:T(8,128)(2,1)S(1)}, u32[]{:S(2)}, u32[]{:S(2)}) collective-permute-start(bf16[4,72,1024]{2,1,0:T(8,128)(2,1)S(1)} %regroup.3.rows_hbm.refs_0_), channel_id=1, source_target_pairs={{0,16},{8,24},{16,0},{24,8},{1,17},{9,25},{17,1},{25,9},{2,18},{10... | collective-permute-start | bytes 1769480 | tf_op jit(solution)/shard_map/ppermute | solution.py:351
  39.7 16.8 %all-to-all-start.2 = ((bf16[8,72,512]{2,1,0:T(8,128)(2,1)}), bf16[8,72,512]{2,1,0:T(8,128)(2,1)S(1)}, u32[]{:S(2)}, u32[]{:S(2)}) async-start(bf16[8,72,512]{2,1,0:T(8,128)(2,1)} %bitcast.22), calls=%async_computation.2 | async-start | bytes 1179648 | tf_op jit(solution)/shard_map/all_to_all | solution.py:336
  45.4 1.4 %copy-start.4 = (bf16[4,72,1024]{2,1,0:T(8,128)(2,1)}, bf16[4,72,1024]{2,1,0:T(8,128)(2,1)S(1)}, u32[]{:S(2)}) copy-start(bf16[4,72,1024]{2,1,0:T(8,128)(2,1)S(1)} %regroup.2.rows_hbm.refs_1_) | copy-start | bytes 1769476
  45.5 10.5 %collective-permute-start.8 = (bf16[4,72,1024]{2,1,0:T(8,128)(2,1)S(1)}, bf16[4,72,1024]{2,1,0:T(8,128)(2,1)S(1)}, u32[]{:S(2)}, u32[]{:S(2)}) collective-permute-start(bf16[4,72,1024]{2,1,0:T(8,128)(2,1)S(1)} %regroup.2.rows_hbm.refs_1_), channel_id=1, source_target_pairs={{0,16},{8,24},{16,0},{24,8},{1,17},{9,25},{17,1},{25,9},{2,18},{10... | collective-permute-start | bytes 1769480 | tf_op jit(solution)/shard_map/ppermute | solution.py:351
  46.3 9.3 %copy-start.7 = (bf16[4,72,1024]{2,1,0:T(8,128)(2,1)}, bf16[4,72,1024]{2,1,0:T(8,128)(2,1)S(1)}, u32[]{:S(2)}) copy-start(bf16[4,72,1024]{2,1,0:T(8,128)(2,1)S(1)} %collective-permute-done.7.refs_6_) | copy-start | bytes 1769476
  46.3 15.3 %collective-permute-start.9 = (bf16[4,72,1024]{2,1,0:T(8,128)(2,1)}, bf16[4,72,1024]{2,1,0:T(8,128)(2,1)S(1)}, u32[]{:S(2)}, u32[]{:S(2)}) collective-permute-start(bf16[4,72,1024]{2,1,0:T(8,128)(2,1)} %copy-done.3), channel_id=1, source_target_pairs={{0,8},{8,0},{16,24},{24,16},{1,9},{9,1},{17,25},{25,17},{2,10},{10... | collective-permute-start | bytes 1769480 | tf_op jit(solution)/shard_map/ppermute | solution.py:351
  46.3 15.3 %collective-permute-start.10 = (bf16[4,72,1024]{2,1,0:T(8,128)(2,1)S(1)}, bf16[4,72,1024]{2,1,0:T(8,128)(2,1)S(1)}, u32[]{:S(2)}, u32[]{:S(2)}) collective-permute-start(bf16[4,72,1024]{2,1,0:T(8,128)(2,1)S(1)} %collective-permute-done.7.refs_6_), channel_id=1, source_target_pairs={{0,8},{8,0},{16,24},{24,16},{1,9},{9,1},{17,25},{25,17},{2,10},{10... | collective-permute-start | bytes 1769480 | tf_op jit(solution)/shard_map/ppermute | solution.py:351
  56.0 6.5 %copy-start.8 = (bf16[4,72,1024]{2,1,0:T(8,128)(2,1)}, bf16[4,72,1024]{2,1,0:T(8,128)(2,1)S(1)}, u32[]{:S(2)}) copy-start(bf16[4,72,1024]{2,1,0:T(8,128)(2,1)S(1)} %collective-permute-done.8.refs_9_) | copy-start | bytes 1769476
  56.0 5.6 %collective-permute-start.11 = (bf16[4,72,1024]{2,1,0:T(8,128)(2,1)}, bf16[4,72,1024]{2,1,0:T(8,128)(2,1)}, u32[]{:S(2)}, u32[]{:S(2)}) collective-permute-start(bf16[4,72,1024]{2,1,0:T(8,128)(2,1)} %copy-done.4), channel_id=1, source_target_pairs={{0,8},{8,0},{16,24},{24,16},{1,9},{9,1},{17,25},{25,17},{2,10},{10... | collective-permute-start | bytes 1769480 | tf_op jit(solution)/shard_map/ppermute | solution.py:351
  56.0 5.7 %collective-permute-start.12 = (bf16[4,72,1024]{2,1,0:T(8,128)(2,1)S(1)}, bf16[4,72,1024]{2,1,0:T(8,128)(2,1)}, u32[]{:S(2)}, u32[]{:S(2)}) collective-permute-start(bf16[4,72,1024]{2,1,0:T(8,128)(2,1)S(1)} %collective-permute-done.8.refs_9_), channel_id=1, source_target_pairs={{0,8},{8,0},{16,24},{24,16},{1,9},{9,1},{17,25},{25,17},{2,10},{10... | collective-permute-start | bytes 1769480 | tf_op jit(solution)/shard_map/ppermute | solution.py:351
  56.5 19.7 %all-to-all-start.1 = ((bf16[8,72,512]{2,1,0:T(8,128)(2,1)}), bf16[8,72,512]{2,1,0:T(8,128)(2,1)S(1)}, u32[]{:S(2)}, u32[]{:S(2)}) async-start(bf16[8,72,512]{2,1,0:T(8,128)(2,1)} %bitcast.21), calls=%async_computation.1 | async-start | bytes 1179648 | tf_op jit(solution)/shard_map/all_to_all | solution.py:336
  61.6 1.0 %copy-start.9 = (bf16[4,72,1024]{2,1,0:T(8,128)(2,1)}, bf16[4,72,1024]{2,1,0:T(8,128)(2,1)S(1)}, u32[]{:S(2)}) copy-start(bf16[4,72,1024]{2,1,0:T(8,128)(2,1)S(1)} %collective-permute-done.9.refs_7_) | copy-start | bytes 1769476
  61.6 0.9 %copy-start.10 = (bf16[4,72,1024]{2,1,0:T(8,128)(2,1)}, bf16[4,72,1024]{2,1,0:T(8,128)(2,1)S(1)}, u32[]{:S(2)}) copy-start(bf16[4,72,1024]{2,1,0:T(8,128)(2,1)S(1)} %collective-permute-done.10.refs_8_) | copy-start | bytes 1769476
  62.6 13.6 %copy-start.2 = (bf16[128,1024]{1,0:T(8,128)(2,1)S(1)}, bf16[128,1024]{1,0:T(8,128)(2,1)}, u32[]{:S(2)}) copy-start(bf16[128,1024]{1,0:T(8,128)(2,1)} %cot_ref.3) | copy-start | bytes 786436
  62.6 13.6 %copy-start.6 = (f32[4,128]{1,0:T(4,128)S(1)}, f32[4,128]{1,0:T(4,128)}, u32[]{:S(2)}) copy-start(f32[4,128]{1,0:T(4,128)} %get-tuple-element.42.target_ref) | copy-start | bytes 6148

commit v7 on v6

--- a/solution.py
+++ b/solution.py
@@ -260,16 +260,18 @@
     outs, ins = out_ref[...], in_ref[...]
     gates = target_ref[2:4, :]
     cot = cot_ref[...].astype(F32)
-    layer, dots = [0.0, 0.0], []
-    for k in (0, 1):
-        gate = as_column(gates[k : k + 1, :])
-        grad = 0.0
-        for side in (0, 1):
-            rows = dot(ones_where(picks[k][side]), outs, ((1,), (0,)))
-            layer[side] = layer[side] + gate * rows
-            part = cot[:, side * half : (side + 1) * half] * rows
-            grad = grad + jnp.sum(part, axis=1, keepdims=True)
-        dots.append(as_row(grad))
+    count = cot.shape[0]
+    columns = [as_column(gates[k : k + 1, :]) for k in (0, 1)]
+    layer, grads = [], [0.0, 0.0]
+    for side in (0, 1):
+        both = jnp.concatenate([ones_where(picks[k][side]) for k in (0, 1)], axis=0)
+        both = dot(both, outs, ((1,), (0,)))
+        rows = [both[:count], both[count:]]
+        layer.append(columns[0] * rows[0] + columns[1] * rows[1])
+        part = cot[:, side * half : (side + 1) * half]
+        for k in (0, 1):
+            grads[k] = grads[k] + jnp.sum(part * rows[k], axis=1, keepdims=True)
+    dots = [as_row(grad) for grad in grads]
     gate_grad_ref[...] = jnp.concatenate(dots, axis=0)
     for side in (0, 1):
         span = slice(side * half, (side + 1) * half)

time: 78.3 us -> 78.3 us (level)
  no operation moved by 1% of the time
where the time goes in v7:
time: 78.3 us; the launch traced here: 77.9 us
  Pallas kernels  37.9 us (48%)
  starting transfers between devices  34.7 us (44%)
  local copies, waits for them, and re-layouts  3.57 us (5%)
  waiting for transfers between devices  0.96 us (1%)
  between operations  0.79 us (1%)
    ppermute x13, starting transfers between devices, across(): lax.ppermute(rows, axis, [(i, i ^ bit) for i in range(lax.axis_size(axis))])  18.1 us
    all_to_all x3, starting transfers between devices, exchange(): lax.all_to_all(cut, 'seq', split_axis=0, concat_axis=0, tiled=True, axis_...  16.6 us
    pallas_call x1, Pallas kernels, local_rows(): pl.pallas_call(functools.partial(gradient_kernel, peers, factor), out_sha...  13.6 us
    pallas_call x1, Pallas kernels, local_rows(): pl.pallas_call(functools.partial(forward_kernel, slots, held, sources, ma...  9.16 us
    pallas_call x1, Pallas kernels, local_rows(): pl.pallas_call(functools.partial(backward_kernel, slots, held, sources, m...  8.75 us
    unnamed x22, local copies, waits for them, and re-layouts  3.57 us
    pallas_call x1, Pallas kernels, local_rows(): pl.pallas_call(functools.partial(token_kernel, slots, sources), out_shape...  2.13 us
    pallas_call x1, Pallas kernels, local_rows(): pl.pallas_call(functools.partial(combine_kernel, slots, mask), out_shape=...  1.62 us
  transfers between devices with their start and end apart: 16, of which 3 were waited for; matrix products, arithmetic and copies ran while one was open for 0% of the time, Pallas kernels for 44%

profile of v7, /device:TPU:0, one launch (start us, length us, event | category | flops | bytes accessed | tf_op | source)
XLA Modules:
  0.0 77.9 jit_solution(37697106572916114)
XLA Ops:
  0.6 2.1 %dispatch_tokens.1 = (bf16[72,512]{1,0:T(8,128)(2,1)}, bf16[72,512]{1,0:T(8,128)(2,1)}, bf16[72,512]{1,0:T(8,128)(2,1)}, bf16[72,512]{1,0:T(8,128)(2,1)}, bf16[7...) custom-call(s32[2,128]{1,0:T(2,128)} %bitcast.23, ...), custom_call_target="tpu_custom_call" | custom-call | tf_op jit(solution)/shard_map/dispatch_tokens/pallas_call | solution.py:318
  2.8 6.0 %collective-permute-start = (bf16[72,512]{1,0:T(8,128)(2,1)}, bf16[72,512]{1,0:T(8,128)(2,1)S(1)}, u32[]{:S(2)}, u32[]{:S(2)}) collective-permute-start(bf16[72,512]{1,0:T(8,128)(2,1)} %get-tuple-element.44), channel_id=1, source_target_pairs={{0,7},{1,6},{2,5},{3,4},{4,3},{5,2},{6,1},{7,0},{8,15},{9,14},{10,... | collective-permute-start | bytes 221192 | tf_op jit(solution)/shard_map/ppermute | solution.py:353
  8.8 0.2 collective-permute-start.1
  9.0 0.8 collective-permute-start.2
  9.8 2.0 %collective-permute-start.3 = (bf16[72,512]{1,0:T(8,128)(2,1)}, bf16[72,512]{1,0:T(8,128)(2,1)S(1)}, u32[]{:S(2)}, u32[]{:S(2)}) collective-permute-start(bf16[72,512]{1,0:T(8,128)(2,1)} %get-tuple-element.47), channel_id=1, source_target_pairs={{0,4},{1,5},{2,6},{3,7},{4,0},{5,1},{6,2},{7,3},{8,12},{9,13},{10,... | collective-permute-start | bytes 221192 | tf_op jit(solution)/shard_map/ppermute | solution.py:353
  11.8 2.3 %collective-permute-start.4 = (bf16[72,512]{1,0:T(8,128)(2,1)}, bf16[72,512]{1,0:T(8,128)(2,1)S(1)}, u32[]{:S(2)}, u32[]{:S(2)}) collective-permute-start(bf16[72,512]{1,0:T(8,128)(2,1)} %get-tuple-element.48), channel_id=1, source_target_pairs={{0,3},{1,2},{2,1},{3,0},{4,7},{5,6},{6,5},{7,4},{8,11},{9,10},{10,... | collective-permute-start | bytes 221192 | tf_op jit(solution)/shard_map/ppermute | solution.py:353
  14.1 0.0 collective-permute-done.refs_7_
  14.1 2.6 %collective-permute-start.5 = (bf16[72,512]{1,0:T(8,128)(2,1)}, bf16[72,512]{1,0:T(8,128)(2,1)S(1)}, u32[]{:S(2)}, u32[]{:S(2)}) collective-permute-start(bf16[72,512]{1,0:T(8,128)(2,1)} %get-tuple-element.49), channel_id=1, source_target_pairs={{0,2},{1,3},{2,0},{3,1},{4,6},{5,7},{6,4},{7,5},{8,10},{9,11},{10,... | collective-permute-start | bytes 221192 | tf_op jit(solution)/shard_map/ppermute | solution.py:353
  16.7 0.0 collective-permute-done.1.refs_6_
  16.7 0.7 collective-permute-start.6
  17.4 0.9 %copy-done = bf16[128,1024]{1,0:T(8,128)(2,1)S(1)} copy-done((bf16[128,1024]{1,0:T(8,128)(2,1)S(1)}, bf16[128,1024]{1,0:T(8,128)(2,1)}, u32[]{:S(2)}) %copy-start) | copy-done | bytes 262168
  18.3 0.9 %copy-done.1 = bf16[128,1024]{1,0:T(8,128)(2,1)S(1)} copy-done((bf16[128,1024]{1,0:T(8,128)(2,1)S(1)}, bf16[128,1024]{1,0:T(8,128)(2,1)}, u32[]{:S(2)}) %copy-start.1) | copy-done | bytes 262168
  19.3 0.7 copy-done.5
  20.0 1.3 %dispatch_cotangents.1 = (bf16[576,512]{1,0:T(8,128)(2,1)}, bf16[72,512]{1,0:T(8,128)(2,1)S(1)}) custom-call(f32[4,128]{1,0:T(4,128)S(1)} %copy-done.5, bf16[128,1024]{1,0:T(8,128)(2,1)S(1)} %copy-done.1, bf16[128,1024]{1,0:T(8,128)(2,1)S(1)} %copy-done), custom_call_target="tpu_custom_call" | custom-call | tf_op jit(solution)/shard_map/dispatch_cotangents/pallas_call | solution.py:363
  21.3 0.0 collective-permute-done.2.refs_5_
  21.3 0.3 collective-permute-done.3.refs_4_
  21.6 0.0 collective-permute-done.4.refs_3_
  21.6 0.2 collective-permute-done.5.refs_2_
  21.8 0.0 collective-permute-done.6.refs_1_
  21.8 6.4 %all-to-all-start = ((bf16[8,72,512]{2,1,0:T(8,128)(2,1)}), bf16[8,72,512]{2,1,0:T(8,128)(2,1)S(1)}, u32[]{:S(2)}, u32[]{:S(2)}) async-start(bf16[8,72,512]{2,1,0:T(8,128)(2,1)} %bitcast.2), calls=%async_computation | async-start | bytes 1179648 | tf_op jit(solution)/shard_map/all_to_all | solution.py:338
  28.2 0.7 regroup.3.rows_hbm.refs_0_
  28.9 0.0 copy-start.3
  28.9 1.6 %collective-permute-start.7 = (bf16[4,72,1024]{2,1,0:T(8,128)(2,1)S(1)}, bf16[4,72,1024]{2,1,0:T(8,128)(2,1)S(1)}, u32[]{:S(2)}, u32[]{:S(2)}) collective-permute-start(bf16[4,72,1024]{2,1,0:T(8,128)(2,1)S(1)} %regroup.3.rows_hbm.refs_0_), channel_id=1, source_target_pairs={{0,16},{8,24},{16,0},{24,8},{1,17},{9,25},{17,1},{25,9},{2,18},{10... | collective-permute-start | bytes 1769480 | tf_op jit(solution)/shard_map/ppermute | solution.py:353
  30.5 9.2 %expert_forward.1 = (bf16[576,512]{1,0:T(8,128)(2,1)}, bf16[4,72,1024]{2,1,0:T(8,128)(2,1)}, bf16[4,72,1024]{2,1,0:T(8,128)(2,1)}) custom-call(bf16[4,72,1024]{2,1,0:T(8,128)(2,1)} %copy-done.3, bf16[4,1024,1024]{2,1,0:T(8,128)(2,1)} %bitcast.15, bf16[4,1024,1024]{2,1,0:T(8,128)(2,1)} %bitcast.18), custom_call_target="tpu_custom_call" | custom-call | flops 2415919104 | bytes 16777216 | tf_op jit(solution)/shard_map/expert_forward/pallas_call | solution.py:384
  39.7 0.0 all-to-all-done
  39.7 5.1 %all-to-all-start.2 = ((bf16[8,72,512]{2,1,0:T(8,128)(2,1)}), bf16[8,72,512]{2,1,0:T(8,128)(2,1)S(1)}, u32[]{:S(2)}, u32[]{:S(2)}) async-start(bf16[8,72,512]{2,1,0:T(8,128)(2,1)} %bitcast.22), calls=%async_computation.2 | async-start | bytes 1179648 | tf_op jit(solution)/shard_map/all_to_all | solution.py:338
  44.8 0.6 regroup.2.rows_hbm.refs_1_
  45.4 0.0 copy-start.4
  45.5 0.8 %collective-permute-start.8 = (bf16[4,72,1024]{2,1,0:T(8,128)(2,1)S(1)}, bf16[4,72,1024]{2,1,0:T(8,128)(2,1)S(1)}, u32[]{:S(2)}, u32[]{:S(2)}) collective-permute-start(bf16[4,72,1024]{2,1,0:T(8,128)(2,1)S(1)} %regroup.2.rows_hbm.refs_1_), channel_id=1, source_target_pairs={{0,16},{8,24},{16,0},{24,8},{1,17},{9,25},{17,1},{25,9},{2,18},{10... | collective-permute-start | bytes 1769480 | tf_op jit(solution)/shard_map/ppermute | solution.py:353
  46.3 0.0 collective-permute-done.7.refs_6_
  46.3 0.0 collective-permute-start.9
  46.3 0.5 collective-permute-start.10
  46.8 0.0 copy-done.4
  46.8 8.7 %expert_backward.1 = (bf16[576,512]{1,0:T(8,128)(2,1)}, bf16[4,72,1024]{2,1,0:T(8,128)(2,1)}) custom-call(bf16[4,72,1024]{2,1,0:T(8,128)(2,1)} %copy-done.4, bf16[4,72,1024]{2,1,0:T(8,128)(2,1)} %get-tuple-element.60.slope_hbm, bf16[4,1024,1024]{2,1,0:T(8,128)(2,1)} %bitcast.19, bf16[4,1024,1024]{2,1,0:T(8,128)(2,1)} %bitcast.16), custom_call_target="tpu_custom_call" | custom-call | flops 2415919104 | bytes 16777216 | tf_op jit(solution)/shard_map/expert_backward/pallas_call | solution.py:399
  55.6 0.4 collective-permute-done.8.refs_9_
  56.0 0.0 collective-permute-start.11
  56.0 0.5 collective-permute-start.12
  56.5 0.0 all-to-all-done.2
  56.5 5.1 %all-to-all-start.1 = ((bf16[8,72,512]{2,1,0:T(8,128)(2,1)}), bf16[8,72,512]{2,1,0:T(8,128)(2,1)S(1)}, u32[]{:S(2)}, u32[]{:S(2)}) async-start(bf16[8,72,512]{2,1,0:T(8,128)(2,1)} %bitcast.21), calls=%async_computation.1 | async-start | bytes 1179648 | tf_op jit(solution)/shard_map/all_to_all | solution.py:338
  61.6 0.0 collective-permute-done.9.refs_7_
  61.6 0.0 collective-permute-done.10.refs_8_
  61.6 0.0 collective-permute-done.11.refs_10_
  61.6 0.0 collective-permute-done.12.refs_11_
  61.6 0.9 %copy-done.10 = bf16[4,72,1024]{2,1,0:T(8,128)(2,1)} copy-done((bf16[4,72,1024]{2,1,0:T(8,128)(2,1)}, bf16[4,72,1024]{2,1,0:T(8,128)(2,1)S(1)}, u32[]{:S(2)}) %copy-start.10) | copy-done | bytes 589848
  62.5 0.1 copy-done.9
  62.6 13.6 %gradients.1 = (f32[256,4096]{1,0:T(8,128)}, f32[256,4096]{1,0:T(8,128)}) custom-call(s32[1]{0:T(128)} %bitcast.10.share_ref, bf16[4,72,1024]{2,1,0:T(8,128)(2,1)} %copy-done.3, bf16[4,72,1024]{2,1,0:T(8,128)(2,1)} %copy-done.4, bf16[4,72,1024]{2,1,0:T(8,128)(2,1)} %get-tuple-element.67.refs_2_, bf16[4,72,1024]{2,1,0:T(8,128)(2,1)} %get-tuple-element.68.refs_3_, ...), custom_call_target="tpu_custom_call" | custom-call | flops 7247757312 | bytes 33554432 | tf_op jit(solution)/shard_map/gradients/pallas_call | solution.py:423
  76.2 0.0 all-to-all-done.1
  76.2 1.6 %combine.1 = (bf16[128,1024]{1,0:T(8,128)(2,1)}, f32[2,128]{1,0:T(2,128)}, bf16[128,1024]{1,0:T(8,128)(2,1)}) custom-call(f32[4,128]{1,0:T(4,128)S(1)} %copy-done.6, bf16[128,1024]{1,0:T(8,128)(2,1)S(1)} %copy-done.2, bf16[576,512]{1,0:T(8,128)(2,1)S(1)} %bitcast.12, bf16[576,512]{1,0:T(8,128)(2,1)S(1)} %bitcast.13), custom_call_target="tpu_custom_call" | custom-call | tf_op jit(solution)/shard_map/combine/pallas_call | solution.py:439
  (14 shorter events, 0.0 us)
Async XLA Ops:
  2.8 11.3 %collective-permute-start = (bf16[72,512]{1,0:T(8,128)(2,1)}, bf16[72,512]{1,0:T(8,128)(2,1)S(1)}, u32[]{:S(2)}, u32[]{:S(2)}) collective-permute-start(bf16[72,512]{1,0:T(8,128)(2,1)} %get-tuple-element.44), channel_id=1, source_target_pairs={{0,7},{1,6},{2,5},{3,4},{4,3},{5,2},{6,1},{7,0},{8,15},{9,14},{10,... | collective-permute-start | bytes 221192 | tf_op jit(solution)/shard_map/ppermute | solution.py:353
  8.8 7.9 %collective-permute-start.1 = (bf16[72,512]{1,0:T(8,128)(2,1)}, bf16[72,512]{1,0:T(8,128)(2,1)S(1)}, u32[]{:S(2)}, u32[]{:S(2)}) collective-permute-start(bf16[72,512]{1,0:T(8,128)(2,1)} %get-tuple-element.45), channel_id=1, source_target_pairs={{0,6},{1,7},{2,4},{3,5},{4,2},{5,3},{6,0},{7,1},{8,14},{9,15},{10,... | collective-permute-start | bytes 221192 | tf_op jit(solution)/shard_map/ppermute | solution.py:353
  9.0 12.3 %collective-permute-start.2 = (bf16[72,512]{1,0:T(8,128)(2,1)}, bf16[72,512]{1,0:T(8,128)(2,1)S(1)}, u32[]{:S(2)}, u32[]{:S(2)}) collective-permute-start(bf16[72,512]{1,0:T(8,128)(2,1)} %get-tuple-element.46), channel_id=1, source_target_pairs={{0,5},{1,4},{2,7},{3,6},{4,1},{5,0},{6,3},{7,2},{8,13},{9,12},{10,... | collective-permute-start | bytes 221192 | tf_op jit(solution)/shard_map/ppermute | solution.py:353
  9.8 11.8 %collective-permute-start.3 = (bf16[72,512]{1,0:T(8,128)(2,1)}, bf16[72,512]{1,0:T(8,128)(2,1)S(1)}, u32[]{:S(2)}, u32[]{:S(2)}) collective-permute-start(bf16[72,512]{1,0:T(8,128)(2,1)} %get-tuple-element.47), channel_id=1, source_target_pairs={{0,4},{1,5},{2,6},{3,7},{4,0},{5,1},{6,2},{7,3},{8,12},{9,13},{10,... | collective-permute-start | bytes 221192 | tf_op jit(solution)/shard_map/ppermute | solution.py:353
  11.8 9.8 %collective-permute-start.4 = (bf16[72,512]{1,0:T(8,128)(2,1)}, bf16[72,512]{1,0:T(8,128)(2,1)S(1)}, u32[]{:S(2)}, u32[]{:S(2)}) collective-permute-start(bf16[72,512]{1,0:T(8,128)(2,1)} %get-tuple-element.48), channel_id=1, source_target_pairs={{0,3},{1,2},{2,1},{3,0},{4,7},{5,6},{6,5},{7,4},{8,11},{9,10},{10,... | collective-permute-start | bytes 221192 | tf_op jit(solution)/shard_map/ppermute | solution.py:353
  14.1 7.7 %collective-permute-start.5 = (bf16[72,512]{1,0:T(8,128)(2,1)}, bf16[72,512]{1,0:T(8,128)(2,1)S(1)}, u32[]{:S(2)}, u32[]{:S(2)}) collective-permute-start(bf16[72,512]{1,0:T(8,128)(2,1)} %get-tuple-element.49), channel_id=1, source_target_pairs={{0,2},{1,3},{2,0},{3,1},{4,6},{5,7},{6,4},{7,5},{8,10},{9,11},{10,... | collective-permute-start | bytes 221192 | tf_op jit(solution)/shard_map/ppermute | solution.py:353
  16.7 5.1 %collective-permute-start.6 = (bf16[72,512]{1,0:T(8,128)(2,1)}, bf16[72,512]{1,0:T(8,128)(2,1)S(1)}, u32[]{:S(2)}, u32[]{:S(2)}) collective-permute-start(bf16[72,512]{1,0:T(8,128)(2,1)} %get-tuple-element.50), channel_id=1, source_target_pairs={{0,1},{1,0},{2,3},{3,2},{4,5},{5,4},{6,7},{7,6},{8,9},{9,8},{10,11... | collective-permute-start | bytes 221192 | tf_op jit(solution)/shard_map/ppermute | solution.py:353
  17.4 0.9 %copy-start = (bf16[128,1024]{1,0:T(8,128)(2,1)S(1)}, bf16[128,1024]{1,0:T(8,128)(2,1)}, u32[]{:S(2)}) copy-start(bf16[128,1024]{1,0:T(8,128)(2,1)} %tok_ref.1) | copy-start | bytes 786436
  18.3 0.9 %copy-start.1 = (bf16[128,1024]{1,0:T(8,128)(2,1)S(1)}, bf16[128,1024]{1,0:T(8,128)(2,1)}, u32[]{:S(2)}) copy-start(bf16[128,1024]{1,0:T(8,128)(2,1)} %cot_ref.3) | copy-start | bytes 786436
  19.3 0.7 copy-start.5
  21.8 17.8 %all-to-all-start = ((bf16[8,72,512]{2,1,0:T(8,128)(2,1)}), bf16[8,72,512]{2,1,0:T(8,128)(2,1)S(1)}, u32[]{:S(2)}, u32[]{:S(2)}) async-start(bf16[8,72,512]{2,1,0:T(8,128)(2,1)} %bitcast.2), calls=%async_computation | async-start | bytes 1179648 | tf_op jit(solution)/shard_map/all_to_all | solution.py:338
  28.9 1.6 %copy-start.3 = (bf16[4,72,1024]{2,1,0:T(8,128)(2,1)}, bf16[4,72,1024]{2,1,0:T(8,128)(2,1)S(1)}, u32[]{:S(2)}) copy-start(bf16[4,72,1024]{2,1,0:T(8,128)(2,1)S(1)} %regroup.3.rows_hbm.refs_0_) | copy-start | bytes 1769476
  28.9 17.4 %collective-permute-start.7 = (bf16[4,72,1024]{2,1,0:T(8,128)(2,1)S(1)}, bf16[4,72,1024]{2,1,0:T(8,128)(2,1)S(1)}, u32[]{:S(2)}, u32[]{:S(2)}) collective-permute-start(bf16[4,72,1024]{2,1,0:T(8,128)(2,1)S(1)} %regroup.3.rows_hbm.refs_0_), channel_id=1, source_target_pairs={{0,16},{8,24},{16,0},{24,8},{1,17},{9,25},{17,1},{25,9},{2,18},{10... | collective-permute-start | bytes 1769480 | tf_op jit(solution)/shard_map/ppermute | solution.py:353
  39.7 16.8 %all-to-all-start.2 = ((bf16[8,72,512]{2,1,0:T(8,128)(2,1)}), bf16[8,72,512]{2,1,0:T(8,128)(2,1)S(1)}, u32[]{:S(2)}, u32[]{:S(2)}) async-start(bf16[8,72,512]{2,1,0:T(8,128)(2,1)} %bitcast.22), calls=%async_computation.2 | async-start | bytes 1179648 | tf_op jit(solution)/shard_map/all_to_all | solution.py:338
  45.4 1.4 %copy-start.4 = (bf16[4,72,1024]{2,1,0:T(8,128)(2,1)}, bf16[4,72,1024]{2,1,0:T(8,128)(2,1)S(1)}, u32[]{:S(2)}) copy-start(bf16[4,72,1024]{2,1,0:T(8,128)(2,1)S(1)} %regroup.2.rows_hbm.refs_1_) | copy-start | bytes 1769476
  45.5 10.5 %collective-permute-start.8 = (bf16[4,72,1024]{2,1,0:T(8,128)(2,1)S(1)}, bf16[4,72,1024]{2,1,0:T(8,128)(2,1)S(1)}, u32[]{:S(2)}, u32[]{:S(2)}) collective-permute-start(bf16[4,72,1024]{2,1,0:T(8,128)(2,1)S(1)} %regroup.2.rows_hbm.refs_1_), channel_id=1, source_target_pairs={{0,16},{8,24},{16,0},{24,8},{1,17},{9,25},{17,1},{25,9},{2,18},{10... | collective-permute-start | bytes 1769480 | tf_op jit(solution)/shard_map/ppermute | solution.py:353
  46.3 9.3 %copy-start.7 = (bf16[4,72,1024]{2,1,0:T(8,128)(2,1)}, bf16[4,72,1024]{2,1,0:T(8,128)(2,1)S(1)}, u32[]{:S(2)}) copy-start(bf16[4,72,1024]{2,1,0:T(8,128)(2,1)S(1)} %collective-permute-done.7.refs_6_) | copy-start | bytes 1769476
  46.3 15.3 %collective-permute-start.9 = (bf16[4,72,1024]{2,1,0:T(8,128)(2,1)}, bf16[4,72,1024]{2,1,0:T(8,128)(2,1)S(1)}, u32[]{:S(2)}, u32[]{:S(2)}) collective-permute-start(bf16[4,72,1024]{2,1,0:T(8,128)(2,1)} %copy-done.3), channel_id=1, source_target_pairs={{0,8},{8,0},{16,24},{24,16},{1,9},{9,1},{17,25},{25,17},{2,10},{10... | collective-permute-start | bytes 1769480 | tf_op jit(solution)/shard_map/ppermute | solution.py:353
  46.3 15.3 %collective-permute-start.10 = (bf16[4,72,1024]{2,1,0:T(8,128)(2,1)S(1)}, bf16[4,72,1024]{2,1,0:T(8,128)(2,1)S(1)}, u32[]{:S(2)}, u32[]{:S(2)}) collective-permute-start(bf16[4,72,1024]{2,1,0:T(8,128)(2,1)S(1)} %collective-permute-done.7.refs_6_), channel_id=1, source_target_pairs={{0,8},{8,0},{16,24},{24,16},{1,9},{9,1},{17,25},{25,17},{2,10},{10... | collective-permute-start | bytes 1769480 | tf_op jit(solution)/shard_map/ppermute | solution.py:353
  56.0 6.5 %copy-start.8 = (bf16[4,72,1024]{2,1,0:T(8,128)(2,1)}, bf16[4,72,1024]{2,1,0:T(8,128)(2,1)S(1)}, u32[]{:S(2)}) copy-start(bf16[4,72,1024]{2,1,0:T(8,128)(2,1)S(1)} %collective-permute-done.8.refs_9_) | copy-start | bytes 1769476
  56.0 5.6 %collective-permute-start.11 = (bf16[4,72,1024]{2,1,0:T(8,128)(2,1)}, bf16[4,72,1024]{2,1,0:T(8,128)(2,1)}, u32[]{:S(2)}, u32[]{:S(2)}) collective-permute-start(bf16[4,72,1024]{2,1,0:T(8,128)(2,1)} %copy-done.4), channel_id=1, source_target_pairs={{0,8},{8,0},{16,24},{24,16},{1,9},{9,1},{17,25},{25,17},{2,10},{10... | collective-permute-start | bytes 1769480 | tf_op jit(solution)/shard_map/ppermute | solution.py:353
  56.0 5.7 %collective-permute-start.12 = (bf16[4,72,1024]{2,1,0:T(8,128)(2,1)S(1)}, bf16[4,72,1024]{2,1,0:T(8,128)(2,1)}, u32[]{:S(2)}, u32[]{:S(2)}) collective-permute-start(bf16[4,72,1024]{2,1,0:T(8,128)(2,1)S(1)} %collective-permute-done.8.refs_9_), channel_id=1, source_target_pairs={{0,8},{8,0},{16,24},{24,16},{1,9},{9,1},{17,25},{25,17},{2,10},{10... | collective-permute-start | bytes 1769480 | tf_op jit(solution)/shard_map/ppermute | solution.py:353
  56.5 19.7 %all-to-all-start.1 = ((bf16[8,72,512]{2,1,0:T(8,128)(2,1)}), bf16[8,72,512]{2,1,0:T(8,128)(2,1)S(1)}, u32[]{:S(2)}, u32[]{:S(2)}) async-start(bf16[8,72,512]{2,1,0:T(8,128)(2,1)} %bitcast.21), calls=%async_computation.1 | async-start | bytes 1179648 | tf_op jit(solution)/shard_map/all_to_all | solution.py:338
  61.6 1.0 %copy-start.9 = (bf16[4,72,1024]{2,1,0:T(8,128)(2,1)}, bf16[4,72,1024]{2,1,0:T(8,128)(2,1)S(1)}, u32[]{:S(2)}) copy-start(bf16[4,72,1024]{2,1,0:T(8,128)(2,1)S(1)} %collective-permute-done.9.refs_7_) | copy-start | bytes 1769476
  61.6 0.9 %copy-start.10 = (bf16[4,72,1024]{2,1,0:T(8,128)(2,1)}, bf16[4,72,1024]{2,1,0:T(8,128)(2,1)S(1)}, u32[]{:S(2)}) copy-start(bf16[4,72,1024]{2,1,0:T(8,128)(2,1)S(1)} %collective-permute-done.10.refs_8_) | copy-start | bytes 1769476
  62.6 13.6 %copy-start.2 = (bf16[128,1024]{1,0:T(8,128)(2,1)S(1)}, bf16[128,1024]{1,0:T(8,128)(2,1)}, u32[]{:S(2)}) copy-start(bf16[128,1024]{1,0:T(8,128)(2,1)} %cot_ref.3) | copy-start | bytes 786436
  62.6 13.6 %copy-start.6 = (f32[4,128]{1,0:T(4,128)S(1)}, f32[4,128]{1,0:T(4,128)}, u32[]{:S(2)}) copy-start(f32[4,128]{1,0:T(4,128)} %get-tuple-element.42.target_ref) | copy-start | bytes 6148
